TPU v7x, 32 devices: a whole 2x2x4 slice. The times are simulated.
32 devices in a mesh: dp: 8 (over z, y), mp: 4 (over x, core).
Axes of the slice: x: 2, y: 2, z: 4, core: 2. Of those that a mesh axis runs over, the one named last changes fastest.
Arguments:
- tokens: bfloat16 [64, 512, 768], P(('dp', 'mp')), may hold values from -6 to 6
- segment_ids: int32 [64, 512], P(('dp', 'mp')), may hold values from 0 to 31, as said below
- cotangent: bfloat16 [64, 512, 768], P(('dp', 'mp')), may hold values from -6 to 6
- norm1_gain: bfloat16 [768], replicated, may hold values from 0.25 to 1.75
- norm1_shift: bfloat16 [768], replicated, may hold values from -1.25 to 1.25
- w_qkv: bfloat16 [768, 3, 768], P(None, None, 'mp'), may hold values from -0.21875 to 0.21875
- qv_bias: bfloat16 [2, 768], P(None, 'mp'), may hold values from -1.25 to 1.25
- w_out: bfloat16 [768, 768], P('mp'), may hold values from -1.25 to 1.25
- out_bias: bfloat16 [768], replicated, may hold values from -1.25 to 1.25
- norm2_gain: bfloat16 [768], replicated, may hold values from 0.25 to 1.75
- norm2_shift: bfloat16 [768], replicated, may hold values from -1.25 to 1.25
- w_up: bfloat16 [768, 3072], P(None, 'mp'), may hold values from -0.21875 to 0.21875
- up_bias: bfloat16 [3072], P('mp'), may hold values from -1.25 to 1.25
- w_down: bfloat16 [3072, 768], P('mp'), may hold values from -0.109375 to 0.109375
- down_bias: bfloat16 [768], replicated, may hold values from -1.25 to 1.25
Outputs:
- mixed: bfloat16 [64, 512, 768], P(('dp', 'mp'))
- input_grad: bfloat16 [64, 512, 768], P(('dp', 'mp'))
- grad_norm1_gain: float32 [768], replicated
- grad_norm1_shift: float32 [768], replicated
- grad_w_qkv: float32 [768, 3, 768], P(None, None, 'mp')
- grad_qv_bias: float32 [2, 768], P(None, 'mp')
- grad_w_out: float32 [768, 768], P('mp')
- grad_out_bias: float32 [768], replicated
- grad_norm2_gain: float32 [768], replicated
- grad_norm2_shift: float32 [768], replicated
- grad_w_up: float32 [768, 3072], P(None, 'mp')
- grad_up_bias: float32 [3072], P('mp')
- grad_w_down: float32 [3072, 768], P('mp')
- grad_down_bias: float32 [768], replicated
Inputs may be any that keep to these rules, and one draw needn't show every extreme that they name: `segment_ids`: within each row the ids start at 0 and never fall, rising by one at each new caption; each row holds exactly 32 captions, positions with equal ids in one row forming one caption.
All inputs are finite; a program needn't handle non-finite values.
Results may differ from a plain program's by a relative error of at most 0.019.
Values may be sent and summed in bfloat16 or wider, within the bound.
A program may use at most 192 MiB of HBM per device.

v0:
```python
import jax
import jax.numpy as jnp
from jax import lax
from jax.sharding import PartitionSpec as P

HEAD = 64
MICRO = 2


EPS = 1e-06
MASKED = -1e30


def flat_dot(left_side, right_side):
    result = jnp.dot(
        left_side.reshape(-1, left_side.shape[-1]), right_side, preferred_element_type=jnp.float32
    )
    return result.reshape(left_side.shape[:-1] + (right_side.shape[-1],))


def back_dot(grad_in, weight):
    result = lax.dot_general(
        grad_in.reshape(-1, grad_in.shape[-1]),
        weight,
        (((1,), (1,)), ((), ())),
        preferred_element_type=jnp.float32,
    )
    return result.reshape(grad_in.shape[:-1] + (weight.shape[0],))


def cross_dot(left_side, right_side):
    return lax.dot_general(
        left_side.reshape(-1, left_side.shape[-1]),
        right_side.reshape(-1, right_side.shape[-1]),
        (((0,), (0,)), ((), ())),
        preferred_element_type=jnp.float32,
    )


def norm_forward(values, gain_f, shift_f):
    average = jnp.mean(values, axis=-1, keepdims=True)
    centred = values - average
    inv_std = lax.rsqrt(jnp.mean(centred * centred, axis=-1, keepdims=True) + EPS)
    normed = centred * inv_std
    return (normed * gain_f + shift_f, normed, inv_std)


def norm_backward(grad_in, normed, inv_std, gain_f):
    scaled = grad_in * gain_f
    inner = (
        scaled
        - jnp.mean(scaled, axis=-1, keepdims=True)
        - normed * jnp.mean(scaled * normed, axis=-1, keepdims=True)
    )
    return (inner * inv_std, jnp.sum(grad_in * normed, axis=(0, 1)), jnp.sum(grad_in, axis=(0, 1)))


def gelu_slope(pre_act):
    cumul = 0.5 * (1.0 + lax.erf(pre_act * 0.7071067811865476))
    return cumul + pre_act * jnp.exp(-0.5 * pre_act * pre_act) * 0.3989422804014327


def masked_scores(queries, key_rows, seg_ids, score_scale):
    scores = (
        jnp.einsum("bqhe,bkhe->bhqk", queries, key_rows, preferred_element_type=jnp.float32)
        * score_scale
    )
    same_doc = (seg_ids[:, :, None] == seg_ids[:, None, :])[:, None]
    return jnp.where(same_doc, scores, MASKED)


def attention_forward(queries, key_rows, values, seg_ids, score_scale):
    scores = masked_scores(queries, key_rows, seg_ids, score_scale)
    highest = jnp.max(scores, axis=-1, keepdims=True)
    log_total = highest + jnp.log(jnp.sum(jnp.exp(scores - highest), axis=-1, keepdims=True))
    attn_prob = jnp.exp(scores - log_total).astype(jnp.bfloat16)
    mixed_heads = jnp.einsum(
        "bhqk,bkhe->bqhe", attn_prob, values, preferred_element_type=jnp.float32
    )
    return (mixed_heads.astype(jnp.bfloat16), log_total)


def attention_backward(queries, key_rows, values, seg_ids, log_total, grad_mixed, score_scale):
    attn_prob = jnp.exp(masked_scores(queries, key_rows, seg_ids, score_scale) - log_total)
    grad_values = jnp.einsum(
        "bhqk,bqhe->bkhe",
        attn_prob.astype(jnp.bfloat16),
        grad_mixed,
        preferred_element_type=jnp.float32,
    )
    grad_prob = jnp.einsum(
        "bqhe,bkhe->bhqk", grad_mixed, values, preferred_element_type=jnp.float32
    )
    grad_scores = (
        attn_prob * (grad_prob - jnp.sum(attn_prob * grad_prob, axis=-1, keepdims=True))
    ).astype(jnp.bfloat16)
    grad_queries = (
        jnp.einsum("bhqk,bkhe->bqhe", grad_scores, key_rows, preferred_element_type=jnp.float32)
        * score_scale
    )
    grad_keys = (
        jnp.einsum("bhqk,bqhe->bkhe", grad_scores, queries, preferred_element_type=jnp.float32)
        * score_scale
    )
    return (grad_queries, grad_keys, grad_values)


def on_device(
    tokens,
    segment_ids,
    cotangent,
    norm1_gain,
    norm1_shift,
    w_qkv,
    qv_bias,
    w_out,
    out_bias,
    norm2_gain,
    norm2_shift,
    w_up,
    up_bias,
    w_down,
    down_bias,
):
    groups = lax.axis_size("mp")
    local_rows = tokens.shape[0] // MICRO
    score_scale = HEAD ** (-0.5)
    qkv_use, qv_use, out_use, up_use, upb_use, down_use = (
        w_qkv,
        qv_bias,
        w_out,
        w_up,
        up_bias,
        w_down,
    )
    seg_whole = lax.all_gather(segment_ids, "mp", axis=0, tiled=True)
    head_width = qkv_use.shape[2]
    heads_here = head_width // HEAD
    qkv_flat = qkv_use.reshape(qkv_use.shape[0], 3 * head_width)
    qv_float = qv_use.astype(jnp.float32)
    proj_bias = jnp.stack([qv_float[0], jnp.zeros_like(qv_float[0]), qv_float[1]])
    upb_float = upb_use.astype(jnp.float32)
    gain_one = norm1_gain.astype(jnp.float32)
    shift_one = norm1_shift.astype(jnp.float32)
    gain_two = norm2_gain.astype(jnp.float32)
    shift_two = norm2_shift.astype(jnp.float32)
    outb_float = out_bias.astype(jnp.float32)
    downb_float = down_bias.astype(jnp.float32)
    grad_qkv = jnp.zeros(qkv_use.shape, jnp.float32)
    grad_qv = jnp.zeros(qv_use.shape, jnp.float32)
    grad_wout = jnp.zeros(out_use.shape, jnp.float32)
    grad_wup = jnp.zeros(up_use.shape, jnp.float32)
    grad_upb = jnp.zeros(upb_use.shape, jnp.float32)
    grad_wdown = jnp.zeros(down_use.shape, jnp.float32)
    grad_gain_one = jnp.zeros(norm1_gain.shape, jnp.float32)
    grad_shift_one = jnp.zeros(norm1_gain.shape, jnp.float32)
    grad_outb = jnp.zeros(norm1_gain.shape, jnp.float32)
    grad_gain_two = jnp.zeros(norm1_gain.shape, jnp.float32)
    grad_shift_two = jnp.zeros(norm1_gain.shape, jnp.float32)
    grad_downb = jnp.zeros(norm1_gain.shape, jnp.float32)
    mixed_parts = []
    input_parts = []
    for micro_step in range(MICRO):
        first_row = micro_step * local_rows
        x_own = tokens[first_row : first_row + local_rows].astype(jnp.float32)
        seg_ids = seg_whole.reshape(groups, MICRO, local_rows, -1)[:, micro_step].reshape(
            groups * local_rows, -1
        )
        norm_one, hat_one, inv_one = norm_forward(x_own, gain_one, shift_one)
        low_one = norm_one.astype(jnp.bfloat16)
        low_one_all = lax.all_gather(low_one, "mp", axis=0, tiled=True)
        batch_rows = low_one_all.shape[0]
        seq_len = low_one_all.shape[1]
        projected = (
            flat_dot(low_one_all, qkv_flat).reshape(batch_rows, seq_len, 3, head_width) + proj_bias
        ).astype(jnp.bfloat16)
        heads_view = projected.reshape(batch_rows, seq_len, 3, heads_here, HEAD)
        queries = heads_view[:, :, 0]
        key_rows = heads_view[:, :, 1]
        values = heads_view[:, :, 2]
        mixed_heads, log_total = attention_forward(queries, key_rows, values, seg_ids, score_scale)
        mixed_rows = mixed_heads.reshape(batch_rows, seq_len, head_width)
        attn_part = flat_dot(mixed_rows, out_use)
        attn_own = lax.psum_scatter(
            attn_part.astype(jnp.bfloat16), "mp", scatter_dimension=0, tiled=True
        ).astype(jnp.float32)
        middle = x_own + attn_own + outb_float
        norm_two, hat_two, inv_two = norm_forward(middle, gain_two, shift_two)
        low_two = norm_two.astype(jnp.bfloat16)
        low_two_all = lax.all_gather(low_two, "mp", axis=0, tiled=True)
        pre_act = flat_dot(low_two_all, up_use) + upb_float
        hidden = jax.nn.gelu(pre_act, approximate=False).astype(jnp.bfloat16)
        down_part = flat_dot(hidden, down_use)
        down_own = lax.psum_scatter(
            down_part.astype(jnp.bfloat16), "mp", scatter_dimension=0, tiled=True
        ).astype(jnp.float32)
        mixed_parts.append((middle + down_own + downb_float).astype(jnp.bfloat16))
        grad_low = cotangent[first_row : first_row + local_rows]
        grad_top = grad_low.astype(jnp.float32)
        grad_downb = grad_downb + jnp.sum(grad_top, axis=(0, 1))
        grad_top_all = lax.all_gather(grad_low, "mp", axis=0, tiled=True)
        grad_wdown = grad_wdown + cross_dot(hidden, grad_top_all)
        grad_pre = (back_dot(grad_top_all, down_use) * gelu_slope(pre_act)).astype(jnp.bfloat16)
        grad_upb = grad_upb + jnp.sum(grad_pre, axis=(0, 1), dtype=jnp.float32)
        grad_wup = grad_wup + cross_dot(low_two_all, grad_pre)
        grad_two_part = back_dot(grad_pre, up_use)
        grad_two = lax.psum_scatter(
            grad_two_part.astype(jnp.bfloat16), "mp", scatter_dimension=0, tiled=True
        ).astype(jnp.float32)
        grad_norm_two, step_gain_two, step_shift_two = norm_backward(
            grad_two, hat_two, inv_two, gain_two
        )
        grad_gain_two = grad_gain_two + step_gain_two
        grad_shift_two = grad_shift_two + step_shift_two
        grad_middle = grad_top + grad_norm_two
        grad_mid_low = grad_middle.astype(jnp.bfloat16)
        grad_outb = grad_outb + jnp.sum(grad_mid_low, axis=(0, 1), dtype=jnp.float32)
        grad_mid_all = lax.all_gather(grad_mid_low, "mp", axis=0, tiled=True)
        grad_wout = grad_wout + cross_dot(mixed_rows, grad_mid_all)
        grad_mixed = (
            back_dot(grad_mid_all, out_use)
            .astype(jnp.bfloat16)
            .reshape(batch_rows, seq_len, heads_here, HEAD)
        )
        grad_queries, grad_keys, grad_values = attention_backward(
            queries, key_rows, values, seg_ids, log_total, grad_mixed, score_scale
        )
        grad_proj = jnp.stack(
            [
                grad_queries.reshape(batch_rows, seq_len, head_width),
                grad_keys.reshape(batch_rows, seq_len, head_width),
                grad_values.reshape(batch_rows, seq_len, head_width),
            ],
            axis=2,
        ).astype(jnp.bfloat16)
        proj_sums = jnp.sum(grad_proj, axis=(0, 1), dtype=jnp.float32)
        grad_qv = grad_qv + jnp.stack([proj_sums[0], proj_sums[2]])
        grad_proj_flat = grad_proj.reshape(batch_rows, seq_len, 3 * head_width)
        grad_qkv = grad_qkv + cross_dot(low_one_all, grad_proj_flat).reshape(qkv_use.shape)
        grad_one_part = back_dot(grad_proj_flat, qkv_flat)
        grad_one = lax.psum_scatter(
            grad_one_part.astype(jnp.bfloat16), "mp", scatter_dimension=0, tiled=True
        ).astype(jnp.float32)
        grad_norm_one, step_gain_one, step_shift_one = norm_backward(
            grad_one, hat_one, inv_one, gain_one
        )
        grad_gain_one = grad_gain_one + step_gain_one
        grad_shift_one = grad_shift_one + step_shift_one
        input_parts.append((grad_middle + grad_norm_one).astype(jnp.bfloat16))
    grad_qkv, grad_qv, grad_wout, grad_wup, grad_upb, grad_wdown = lax.psum(
        (grad_qkv, grad_qv, grad_wout, grad_wup, grad_upb, grad_wdown), "dp"
    )
    grad_gain_one, grad_shift_one, grad_outb, grad_gain_two, grad_shift_two, grad_downb = lax.psum(
        (grad_gain_one, grad_shift_one, grad_outb, grad_gain_two, grad_shift_two, grad_downb),
        ("dp", "mp"),
    )
    mixed = jnp.concatenate(mixed_parts, axis=0)
    input_grad = jnp.concatenate(input_parts, axis=0)
    return (
        mixed,
        input_grad,
        grad_gain_one,
        grad_shift_one,
        grad_qkv,
        grad_qv,
        grad_wout,
        grad_outb,
        grad_gain_two,
        grad_shift_two,
        grad_wup,
        grad_upb,
        grad_wdown,
        grad_downb,
    )


def solution(mesh):
    placed = (
        P(("dp", "mp"), None, None),
        P(("dp", "mp"), None),
        P(("dp", "mp"), None, None),
        P(),
        P(),
        P(None, None, "mp"),
        P(None, "mp"),
        P("mp", None),
        P(),
        P(),
        P(),
        P(None, "mp"),
        P("mp"),
        P("mp", None),
        P(),
    )
    return jax.shard_map(
        on_device,
        mesh=mesh,
        in_specs=placed,
        out_specs=(
            P(("dp", "mp"), None, None),
            P(("dp", "mp"), None, None),
            P(),
            P(),
            P(None, None, "mp"),
            P(None, "mp"),
            P("mp", None),
            P(),
            P(),
            P(),
            P(None, "mp"),
            P("mp"),
            P("mp", None),
            P(),
        ),
        check_vma=False,
    )
```

profile of v0, /device:TPU:0, one launch (start us, length us, event | category | flops | bytes accessed | tf_op | source)
XLA Modules:
  0.0 851.1 jit_solution(16188669441258042531)
XLA Ops:
  15.1 6.2 all-gather
  23.1 22.7 %all-gather.14.cloned.1.call-done = bf16[4,512,768]{2,1,0:T(8,128)(2,1)} async-done(((bf16[1,512,768]{2,1,0:T(8,128)(2,1)}), bf16[4,512,768]{2,1,0:T(8,128)(2,1)}) %all-gather.14.cloned.1.call-update) | async-done | bytes 3145744 | tf_op jit(solution)/shard_map/all_gather | solution.py:171
  45.7 4.2 add_convert_fusion
  50.0 6.3 fusion.1
  56.2 7.6 exponential_reduce_fusion
  63.9 6.6 convolution_convert_fusion.8
  76.5 4.2 add_convert_fusion.1
  80.7 6.6 fusion
  87.3 7.8 exponential_reduce_fusion.1
  95.2 7.1 convolution_convert_fusion.9
  106.6 10.4 %reduce-scatter.13.cloned.1.call-done = bf16[1,512,768]{2,1,0:T(8,128)(2,1)} async-done(((bf16[4,512,768]{2,1,0:T(8,128)(2,1)}), bf16[1,512,768]{2,1,0:T(8,128)(2,1)}) %reduce-scatter.13.cloned.1.call-update) | async-done | bytes 786448 | tf_op jit(solution)/shard_map/reduce_scatter | solution.py:184
  117.0 40.6 %reduce-scatter.9.cloned.1.call-done = bf16[1,512,768]{2,1,0:T(8,128)(2,1)} async-done(((bf16[4,512,768]{2,1,0:T(8,128)(2,1)}), bf16[1,512,768]{2,1,0:T(8,128)(2,1)}) %reduce-scatter.9.cloned.1.call-update) | async-done | bytes 786448 | tf_op jit(solution)/shard_map/reduce_scatter | solution.py:184
  166.8 10.5 %reduce-scatter.21.cloned.1.call-start = ((), (), s32[]{:S(2)}) async-start(), calls=%async_computation.21 | async-start | bytes 3932160 | tf_op jit(solution)/shard_map/reduce_scatter | solution.py:207
  178.6 12.7 %all-gather.16.cloned.1.call-done = bf16[4,512,768]{2,1,0:T(8,128)(2,1)} async-done(((bf16[1,512,768]{2,1,0:T(8,128)(2,1)}), bf16[4,512,768]{2,1,0:T(8,128)(2,1)}) %all-gather.16.cloned.1.call-update) | async-done | bytes 3145744 | tf_op jit(solution)/shard_map/all_gather | solution.py:190
  191.3 7.2 fusion.100
  198.5 22.8 %all-gather.22.cloned.1.call-done = bf16[4,512,768]{2,1,0:T(8,128)(2,1)} async-done(((bf16[1,512,768]{2,1,0:T(8,128)(2,1)}), bf16[4,512,768]{2,1,0:T(8,128)(2,1)}) %all-gather.22.cloned.1.call-update) | async-done | bytes 3145744 | tf_op jit(solution)/shard_map/all_gather | solution.py:201
  221.3 7.5 convert_reduce_fusion
  230.5 4.0 convolution_convert_fusion.2
  234.6 17.4 %all-gather.12.cloned.1.call-done = bf16[4,512,768]{2,1,0:T(8,128)(2,1)} async-done(((bf16[1,512,768]{2,1,0:T(8,128)(2,1)}), bf16[4,512,768]{2,1,0:T(8,128)(2,1)}) %all-gather.12.cloned.1.call-update) | async-done | bytes 3145744 | tf_op jit(solution)/shard_map/all_gather | solution.py:190
  252.0 12.4 %fusion.92 = (u8[512,768]{1,0:T(8,128)(4,1)S(1)}, u8[512,768]{1,0:T(8,128)(4,1)S(1)}, u8[512,768]{1,0:T(8,128)(4,1)S(1)}, u8[512,768]{1,0:T(8,128)(4,1)S(1)}, f32[4,512,768]{2,1,0:T(8,128)S(1)}) fusion(f32[768]{0:T(1024)} %convert_element_type.215, f32[4,512,768]{2,1,0:T(8,128)} %fusion.100, bf16[4,512,768]{2,1,0:T(8,128)(2,1)} %all-gather.12.cloned.1.call-done, ...), kind=kOutput, calls=%fused_computation.177 | convolution fusion | flops 2458386432 | bytes 18484224 | tf_op jit(solution)/shard_map/dot_general | solution.py:15
  264.4 32.0 %fusion.6 = (bf16[4,512,768]{2,1,0:T(8,128)(2,1)S(1)}, bf16[4,512,768]{2,1,0:T(8,128)(2,1)}) fusion(f32[4,512,768]{2,1,0:T(8,128)S(1)} %get-tuple-element.99, f32[768]{0:T(1024)} %convert_element_type.215, u8[512,768]{1,0:T(8,128)(4,1)S(1)} %get-tuple-element.15, u8[512,768]{1,0:T(8,128)(4,1)S(1)} %get-tuple-element.14, ...), kind=kLoop, calls=%fused_computation.20 | loop fusion | flops 221773824 | bytes 20450304 | tf_op jit(solution)/shard_map/convert_element_type | solution.py:192
  298.0 3.9 convolution_convert_fusion.5
  302.0 6.9 convolution_convert_fusion.4
  309.2 7.6 convert_reduce_fusion.1
  318.5 4.0 convolution_convert_fusion.3
  323.2 40.0 %reduce-scatter.11.cloned.1.call-done = bf16[1,512,768]{2,1,0:T(8,128)(2,1)} async-done(((bf16[4,512,768]{2,1,0:T(8,128)(2,1)}), bf16[1,512,768]{2,1,0:T(8,128)(2,1)}) %reduce-scatter.11.cloned.1.call-update) | async-done | bytes 786448 | tf_op jit(solution)/shard_map/reduce_scatter | solution.py:194
  363.2 40.6 %reduce-scatter.15.cloned.1.call-done = bf16[1,512,768]{2,1,0:T(8,128)(2,1)} async-done(((bf16[4,512,768]{2,1,0:T(8,128)(2,1)}), bf16[1,512,768]{2,1,0:T(8,128)(2,1)}) %reduce-scatter.15.cloned.1.call-update) | async-done | bytes 786448 | tf_op jit(solution)/shard_map/reduce_scatter | solution.py:194
  403.8 40.5 %reduce-scatter.17.cloned.1.call-done = bf16[1,512,768]{2,1,0:T(8,128)(2,1)} async-done(((bf16[4,512,768]{2,1,0:T(8,128)(2,1)}), bf16[1,512,768]{2,1,0:T(8,128)(2,1)}) %reduce-scatter.17.cloned.1.call-update) | async-done | bytes 786448 | tf_op jit(solution)/shard_map/reduce_scatter | solution.py:207
  444.3 4.7 fusion.86
  449.1 3.3 convert_reduce_fusion.13
  453.5 27.7 %all-gather.20.cloned.1.call-done = bf16[4,512,768]{2,1,0:T(8,128)(2,1)} async-done(((bf16[1,512,768]{2,1,0:T(8,128)(2,1)}), bf16[4,512,768]{2,1,0:T(8,128)(2,1)}) %all-gather.20.cloned.1.call-update) | async-done | bytes 3145744 | tf_op jit(solution)/shard_map/all_gather | solution.py:218
  481.2 3.2 convolution_convert_fusion.7
  484.4 12.4 %multiply_reduce_fusion.1 = (f32[4,3,512]{2,1,0:T(4,128)S(1)}, f32[4,3,512,512]{2,3,1,0:T(8,128)}) fusion(f32[4,3,512,512]{2,3,1,0:T(8,128)} %get-tuple-element.96, f32[4,3,512]{2,1,0:T(4,128)S(1)} %copy-done.47, pred[4,512,512]{1,2,0:T(8,128)(4,1)S(1)} %copy-done.6, bf16[4,512,3,64]{1,3,2,0:T(8,128)(2,1)S(1)} %bitcast.280, ...), kind=kOutput, calls=%fused_computation.3 | convolution fusion | flops 418375680 | bytes 27844608 | tf_op jit(solution)/shard_map/bqhe,bkhe->bhqk/dot_general | solution.py:91
  497.6 7.2 multiply_convert_fusion.1
  508.0 3.7 fusion.121
  513.6 4.1 bitcast_convert_fusion.1
  518.6 3.2 convolution_convert_fusion.6
  521.8 12.4 %multiply_reduce_fusion = (f32[4,3,512]{2,1,0:T(4,128)S(1)}, f32[4,3,512,512]{2,3,1,0:T(8,128)}) fusion(f32[4,3,512,512]{2,3,1,0:T(8,128)} %get-tuple-element.98, f32[4,3,512]{2,1,0:T(4,128)S(1)} %copy-done.45, pred[4,512,512]{1,2,0:T(8,128)(4,1)S(1)} %copy-done.4, bf16[4,512,3,64]{1,3,2,0:T(8,128)(2,1)S(1)} %bitcast.282, ...), kind=kOutput, calls=%fused_computation.1 | convolution fusion | flops 418375680 | bytes 27844608 | tf_op jit(solution)/shard_map/bqhe,bkhe->bhqk/dot_general | solution.py:91
  536.3 7.2 multiply_convert_fusion
  546.7 3.7 fusion.118
  552.3 4.0 bitcast_convert_fusion
  566.6 4.2 bitcast_add_fusion.1
  570.7 4.1 bitcast_add_fusion
  586.4 3.3 convolution_add_fusion
  592.9 21.7 %all-reduce.1 = (f32[2,192]{1,0:T(2,128)}, f32[768]{0:T(1024)}) all-reduce(f32[2,192]{1,0:T(2,128)S(1)} %maximum_add_fusion, f32[768]{0:T(1024)S(1)} %add.289), channel_id=1, replica_groups=mesh['dp'=8,'mp'=4] {'dp'}, use_global_device_ids=true, to_apply=%region_39.40 | all-reduce | flops 1152 | bytes 9216 | tf_op jit(solution)/shard_map/psum | solution.py:250
  617.5 41.6 %all-reduce = (f32[768]{0:T(1024)}, f32[768]{0:T(1024)}, f32[768]{0:T(1024)}, f32[768]{0:T(1024)}, f32[768]{0:T(1024)}, /*index=5*/f32[768]{0:T(1024)}) all-reduce(f32[768]{0:T(1024)S(1)} %add.280, f32[768]{0:T(1024)S(1)} %add.281, f32[768]{0:T(1024)S(1)} %add.285, f32[768]{0:T(1024)S(1)} %add.286, ...), channel_id=1, replica_groups=mesh['dp'=8,'mp'=4] {'dp','mp'}, use_global_device_ids=true, to_apply=%region_32.33 | all-reduce | flops 4608 | bytes 36864 | tf_op jit(solution)/shard_map/psum | solution.py:253
  663.1 174.4 %all-reduce.5.cloned.1.call-done = (f32[768,3,192]{0,2,1:T(8,128)}, f32[192,768]{1,0:T(8,128)}, f32[768,768]{1,0:T(8,128)}, f32[768,768]{1,0:T(8,128)}) async-done(((f32[768,3,192]{0,2,1:T(8,128)}, f32[192,768]{1,0:T(8,128)}, f32[768,768]{1,0:T(8,128)}, f32[768,768]{1,0:T(8,128)}), (f32[768,3,192]{0,2,1:T(8,128)}, f32[192,768]{1,0:T(8,128)}, f32[768,768]{1,0:T(8,128)}, ...) | async-done | bytes 7077904 | tf_op jit(solution)/shard_map/psum | solution.py:250
  837.5 2.9 copy.145
  (291 shorter events, 86.3 us)
Async XLA Ops:
  7.2 184.1 %copy-start = (bf16[768,768]{1,0:T(8,128)(2,1)S(1)}, bf16[768,768]{1,0:T(8,128)(2,1)}, u32[]{:S(2)}) copy-start(bf16[768,768]{1,0:T(8,128)(2,1)} %param.26) | copy-start | bytes 3538948
  7.2 5.3 copy-start.2
  7.2 38.5 %all-gather.14.cloned.1.call-start = ((), (), s32[]{:S(2)}) async-start(), calls=%async_computation.12 | async-start | bytes 3932160 | tf_op jit(solution)/shard_map/all_gather | solution.py:171
  8.1 6.2 copy-start.48
  10.5 11.0 %copy-start.66 = (bf16[2,192]{1,0:T(2,128)(2,1)S(1)}, bf16[2,192]{1,0:T(2,128)(2,1)}, u32[]{:S(2)}) copy-start(bf16[2,192]{1,0:T(2,128)(2,1)} %param.21) | copy-start | bytes 2308
  14.3 62.1 %all-gather.10.cloned.1.call-start = ((), (), s32[]{:S(2)}) async-start(), calls=%async_computation.8 | async-start | bytes 3932160 | tf_op jit(solution)/shard_map/all_gather | solution.py:171
  15.1 101.9 %reduce-scatter.13.cloned.1.call-start = ((), (), s32[]{:S(2)}) async-start(), calls=%async_computation.13 | async-start | bytes 3932160 | tf_op jit(solution)/shard_map/reduce_scatter | solution.py:184
  50.0 13.9 %copy-start.17 = (bf16[4,512,3,192]{1,3,2,0:T(8,128)(2,1)}, bf16[4,512,3,192]{1,3,2,0:T(8,128)(2,1)S(1)}, u32[]{:S(2)}) copy-start(bf16[4,512,3,192]{1,3,2,0:T(8,128)(2,1)S(1)} %add_convert_fusion) | copy-start | bytes 7077892
  63.9 6.7 copy-start.44
  63.9 7.5 copy-start.41
  74.2 83.4 %reduce-scatter.9.cloned.1.call-start = ((), (), s32[]{:S(2)}) async-start(), calls=%async_computation.9 | async-start | bytes 3932160 | tf_op jit(solution)/shard_map/reduce_scatter | solution.py:184
  80.7 14.4 %copy-start.19 = (bf16[4,512,3,192]{1,3,2,0:T(8,128)(2,1)}, bf16[4,512,3,192]{1,3,2,0:T(8,128)(2,1)S(1)}, u32[]{:S(2)}) copy-start(bf16[4,512,3,192]{1,3,2,0:T(8,128)(2,1)S(1)} %add_convert_fusion.1) | copy-start | bytes 7077892
  95.2 7.1 copy-start.46
  105.9 85.4 %all-gather.16.cloned.1.call-start = ((), (), s32[]{:S(2)}) async-start(), calls=%async_computation.14 | async-start | bytes 3932160 | tf_op jit(solution)/shard_map/all_gather | solution.py:190
  117.0 42.6 %copy-start.7 = (bf16[1,512,768]{2,1,0:T(8,128)(2,1)S(1)}, bf16[1,512,768]{2,1,0:T(8,128)(2,1)}, u32[]{:S(2)}) copy-start(bf16[1,512,768]{2,1,0:T(8,128)(2,1)} %reduce-scatter.13.cloned.1.call-done) | copy-start | bytes 2359300
  162.6 58.7 %all-gather.22.cloned.1.call-start = ((), (), s32[]{:S(2)}) async-start(), calls=%async_computation.20 | async-start | bytes 3932160 | tf_op jit(solution)/shard_map/all_gather | solution.py:201
  165.3 86.7 %all-gather.12.cloned.1.call-start = ((), (), s32[]{:S(2)}) async-start(), calls=%async_computation.10 | async-start | bytes 3932160 | tf_op jit(solution)/shard_map/all_gather | solution.py:190
  166.1 143.2 %all-gather.18.cloned.1.call-start = ((), (), s32[]{:S(2)}) async-start(), calls=%async_computation.16 | async-start | bytes 3932160 | tf_op jit(solution)/shard_map/all_gather | solution.py:201
  166.8 156.4 %reduce-scatter.21.cloned.1.call-start = ((), (), s32[]{:S(2)}) async-start(), calls=%async_computation.21 | async-start | bytes 3932160 | tf_op jit(solution)/shard_map/reduce_scatter | solution.py:207
  234.5 128.7 %reduce-scatter.11.cloned.1.call-start = ((), (), s32[]{:S(2)}) async-start(), calls=%async_computation.11 | async-start | bytes 3932160 | tf_op jit(solution)/shard_map/reduce_scatter | solution.py:194
  264.4 32.0 %copy-start.16 = (f32[4,512,768]{2,1,0:T(8,128)}, f32[4,512,768]{2,1,0:T(8,128)S(1)}, u32[]{:S(2)}) copy-start(f32[4,512,768]{2,1,0:T(8,128)S(1)} %get-tuple-element.99) | copy-start | bytes 18874372
  264.4 33.6 %copy-start.75 = (bf16[768,768]{1,0:T(8,128)(2,1)S(1)}, bf16[768,768]{1,0:T(8,128)(2,1)}, u32[]{:S(2)}) copy-start(bf16[768,768]{1,0:T(8,128)(2,1)} %param.28) | copy-start | bytes 3538948
  302.0 101.8 %reduce-scatter.15.cloned.1.call-start = ((), (), s32[]{:S(2)}) async-start(), calls=%async_computation.15 | async-start | bytes 3932160 | tf_op jit(solution)/shard_map/reduce_scatter | solution.py:194
  308.9 135.3 %reduce-scatter.17.cloned.1.call-start = ((), (), s32[]{:S(2)}) async-start(), calls=%async_computation.17 | async-start | bytes 3932160 | tf_op jit(solution)/shard_map/reduce_scatter | solution.py:207
  322.5 121.7 %copy-start.9 = (bf16[1,512,768]{2,1,0:T(8,128)(2,1)S(1)}, bf16[1,512,768]{2,1,0:T(8,128)(2,1)}, u32[]{:S(2)}) copy-start(bf16[1,512,768]{2,1,0:T(8,128)(2,1)} %reduce-scatter.9.cloned.1.call-done) | copy-start | bytes 2359300
  322.6 121.7 %copy-start.59 = (f32[512]{0:T(512)S(1)}, f32[512]{0:T(512)}, u32[]{:S(2)}) copy-start(f32[512]{0:T(512)} %copy-done.58) | copy-start | bytes 6148
  322.6 121.7 %copy-start.61 = (f32[512]{0:T(512)S(1)}, f32[512]{0:T(512)}, u32[]{:S(2)}) copy-start(f32[512]{0:T(512)} %copy-done.60) | copy-start | bytes 6148
  322.6 158.6 %all-gather.20.cloned.1.call-start = ((), (), s32[]{:S(2)}) async-start(), calls=%async_computation.18 | async-start | bytes 3932160 | tf_op jit(solution)/shard_map/all_gather | solution.py:218
  444.3 4.8 copy-start.37
  452.4 32.0 %copy-start.6 = (pred[4,512,512]{1,2,0:T(8,128)(4,1)S(1)}, pred[4,512,512]{1,2,0:T(8,128)(4,1)}, u32[]{:S(2)}) copy-start(pred[4,512,512]{1,2,0:T(8,128)(4,1)} %broadcast_compare_fusion.1) | copy-start | bytes 3145732
  452.4 32.0 %copy-start.47 = (f32[4,3,512]{2,1,0:T(4,128)S(1)}, f32[4,3,512]{2,1,0:T(4,128)}, u32[]{:S(2)}) copy-start(f32[4,3,512]{2,1,0:T(4,128)} %copy-done.46) | copy-start | bytes 73732
  452.4 65.4 %all-gather.24.cloned.1.call-start = ((), (), s32[]{:S(2)}) async-start(), calls=%async_computation.22 | async-start | bytes 3932160 | tf_op jit(solution)/shard_map/all_gather | solution.py:218
  453.0 161.5 %reduce-scatter.19.cloned.1.call-start = ((), (), s32[]{:S(2)}) async-start(), calls=%async_computation.19 | async-start | bytes 3932160 | tf_op jit(solution)/shard_map/reduce_scatter | solution.py:241
  484.4 12.5 %slice-start.3 = ((s8[12582912]{0:T(1024)(128)(4,1)}), s8[4194304]{0:T(1024)(128)(4,1)S(1)}, s32[]{:S(2)}) async-start(s8[12582912]{0:T(1024)(128)(4,1)} %bitcast.250), calls=%async_computation.28 | async-start | bytes 8388608
  484.4 12.4 %slice-start.4 = ((s8[12582912]{0:T(1024)(128)(4,1)}), s8[4194304]{0:T(1024)(128)(4,1)S(1)}, s32[]{:S(2)}) async-start(s8[12582912]{0:T(1024)(128)(4,1)} %bitcast.250), calls=%async_computation.29 | async-start | bytes 8388608
  484.4 13.1 %slice-start.5 = ((s8[12582912]{0:T(1024)(128)(4,1)}), s8[4194304]{0:T(1024)(128)(4,1)S(1)}, s32[]{:S(2)}) async-start(s8[12582912]{0:T(1024)(128)(4,1)} %bitcast.250), calls=%async_computation.30 | async-start | bytes 8388608
  517.6 96.9 %reduce-scatter.23.cloned.1.call-start = ((), (), s32[]{:S(2)}) async-start(), calls=%async_computation.23 | async-start | bytes 3932160 | tf_op jit(solution)/shard_map/reduce_scatter | solution.py:241
  521.8 12.5 %slice-start = ((s8[12582912]{0:T(1024)(128)(4,1)}), s8[4194304]{0:T(1024)(128)(4,1)S(1)}, s32[]{:S(2)}) async-start(s8[12582912]{0:T(1024)(128)(4,1)} %bitcast.248), calls=%async_computation.25 | async-start | bytes 8388608
  521.8 12.4 %slice-start.1 = ((s8[12582912]{0:T(1024)(128)(4,1)}), s8[4194304]{0:T(1024)(128)(4,1)S(1)}, s32[]{:S(2)}) async-start(s8[12582912]{0:T(1024)(128)(4,1)} %bitcast.248), calls=%async_computation.26 | async-start | bytes 8388608
  521.8 14.5 %slice-start.2 = ((s8[12582912]{0:T(1024)(128)(4,1)}), s8[4194304]{0:T(1024)(128)(4,1)S(1)}, s32[]{:S(2)}) async-start(s8[12582912]{0:T(1024)(128)(4,1)} %bitcast.248), calls=%async_computation.27 | async-start | bytes 8388608
  556.3 281.2 %all-reduce.5.cloned.1.call-start = ((), (), s32[]{:S(2)}) async-start(), calls=%async_computation.24 | async-start | bytes 14155776 | tf_op jit(solution)/shard_map/psum | solution.py:250
  589.7 24.9 %copy-start.49 = (f32[768]{0:T(1024)S(1)}, f32[768]{0:T(1024)}, u32[]{:S(2)}) copy-start(f32[768]{0:T(1024)} %copy-done.48) | copy-start | bytes 9220
  589.7 24.8 %copy-start.51 = (f32[512]{0:T(512)S(1)}, f32[512]{0:T(512)}, u32[]{:S(2)}) copy-start(f32[512]{0:T(512)} %copy-done.50) | copy-start | bytes 6148
  589.7 24.8 %copy-start.53 = (f32[512]{0:T(512)S(1)}, f32[512]{0:T(512)}, u32[]{:S(2)}) copy-start(f32[512]{0:T(512)} %copy-done.52) | copy-start | bytes 6148
  589.7 24.8 %copy-start.55 = (f32[512]{0:T(512)S(1)}, f32[512]{0:T(512)}, u32[]{:S(2)}) copy-start(f32[512]{0:T(512)} %copy-done.54) | copy-start | bytes 6148
  589.7 24.8 %copy-start.57 = (f32[512]{0:T(512)S(1)}, f32[512]{0:T(512)}, u32[]{:S(2)}) copy-start(f32[512]{0:T(512)} %copy-done.56) | copy-start | bytes 6148
  614.5 44.6 %copy-start.29 = (bf16[1,512,768]{2,1,0:T(8,128)(2,1)S(1)}, bf16[1,512,768]{2,1,0:T(8,128)(2,1)}, u32[]{:S(2)}) copy-start(bf16[1,512,768]{2,1,0:T(8,128)(2,1)} %reduce-scatter.19.cloned.1.call-done) | copy-start | bytes 2359300
  614.6 44.5 %copy-start.30 = (bf16[1,512,768]{2,1,0:T(8,128)(2,1)S(1)}, bf16[1,512,768]{2,1,0:T(8,128)(2,1)}, u32[]{:S(2)}) copy-start(bf16[1,512,768]{2,1,0:T(8,128)(2,1)} %reduce-scatter.23.cloned.1.call-done) | copy-start | bytes 2359300
  (55 other events, 141.6 us)
Sparse Core Ops, SparseCore 0:
  14.5 31.2 all-gather.13
  47.8 28.5 all-gather.9
  79.0 37.9 reduce-scatter.12
  119.6 37.9 reduce-scatter.8
  162.7 28.5 all-gather.15
  192.7 28.5 all-gather.21
  223.4 28.5 all-gather.11
  253.5 28.5 all-gather.17
  284.7 37.9 reduce-scatter.20
  325.2 37.9 reduce-scatter.10
  365.7 37.9 reduce-scatter.14
  406.3 37.9 reduce-scatter.16
  452.6 28.5 all-gather.19
  482.6 28.5 all-gather.23
  517.8 37.3 reduce-scatter.18
  557.7 37.9 reduce-scatter.22
  600.5 236.9 all-reduce.4
where the time goes:
time: 860 us; the launch traced here: 851 us
  waiting for transfers between devices  453 us (53%)
  matrix products  169 us (20%)
  other arithmetic  97.6 us (11%)
  blocking collectives  69.4 us (8%)
  local copies, waits for them, and re-layouts  34.5 us (4%)
  between operations  15.5 us (2%)
  starting transfers between devices  12.5 us (1%)
    psum x1, waiting for transfers between devices, on_device(): lax.psum((grad_qkv, grad_qv, grad_wout, grad_wup, grad_upb, grad_wdown),...  174 us
    reduce_scatter x2, waiting for transfers between devices, on_device(): lax.psum_scatter(down_part.astype(jnp.bfloat16), 'mp', scatter_dimension=...  80.5 us
    reduce_scatter x2, waiting for transfers between devices, on_device(): lax.psum_scatter(attn_part.astype(jnp.bfloat16), 'mp', scatter_dimension=...  50.9 us
    dot_general x8, matrix products, flat_dot(): jnp.dot(left_side.reshape(-1, left_side.shape[-1]), right_side, preferred...  44.4 us
    psum x1, blocking collectives, on_device(): lax.psum((grad_gain_one, grad_shift_one, grad_outb, grad_gain_two, grad_s...  41.6 us
    reduce_scatter x2, waiting for transfers between devices, on_device(): lax.psum_scatter(grad_two_part.astype(jnp.bfloat16), 'mp', scatter_dimens...  40.5 us
    dot_general x8, matrix products, back_dot(): lax.dot_general(grad_in.reshape(-1, grad_in.shape[-1]), weight, (((1,), (...  37.7 us
    convert_element_type x1, other arithmetic, on_device(): hidden = jax.nn.gelu(pre_act, approximate=False).astype(jnp.bfloat16)  32 us
  transfers between devices with their start and end apart: 17, of which 12 were waited for; matrix products, arithmetic and copies ran while one was open for 30% of the time, Pallas kernels for 0%

commit v1 on v0

v1 whole, which is shorter than its diff:
```python
import jax
import jax.numpy as jnp
from jax import lax
from jax.sharding import PartitionSpec as P

HEAD = 64


EPS = 1e-06
MASKED = -1e30


def flat_dot(left_side, right_side):
    result = jnp.dot(
        left_side.reshape(-1, left_side.shape[-1]), right_side, preferred_element_type=jnp.float32
    )
    return result.reshape(left_side.shape[:-1] + (right_side.shape[-1],))


def back_dot(grad_in, weight):
    result = lax.dot_general(
        grad_in.reshape(-1, grad_in.shape[-1]),
        weight,
        (((1,), (1,)), ((), ())),
        preferred_element_type=jnp.float32,
    )
    return result.reshape(grad_in.shape[:-1] + (weight.shape[0],))


def cross_dot(left_side, right_side):
    return lax.dot_general(
        left_side.reshape(-1, left_side.shape[-1]),
        right_side.reshape(-1, right_side.shape[-1]),
        (((0,), (0,)), ((), ())),
        preferred_element_type=jnp.float32,
    )


def norm_forward(values, gain_f, shift_f):
    average = jnp.mean(values, axis=-1, keepdims=True)
    centred = values - average
    inv_std = lax.rsqrt(jnp.mean(centred * centred, axis=-1, keepdims=True) + EPS)
    normed = centred * inv_std
    return (normed * gain_f + shift_f, normed, inv_std)


def norm_backward(grad_in, normed, inv_std, gain_f):
    scaled = grad_in * gain_f
    inner = (
        scaled
        - jnp.mean(scaled, axis=-1, keepdims=True)
        - normed * jnp.mean(scaled * normed, axis=-1, keepdims=True)
    )
    return (inner * inv_std, jnp.sum(grad_in * normed, axis=(0, 1)), jnp.sum(grad_in, axis=(0, 1)))


def gelu_slope(pre_act):
    cumul = 0.5 * (1.0 + lax.erf(pre_act * 0.7071067811865476))
    return cumul + pre_act * jnp.exp(-0.5 * pre_act * pre_act) * 0.3989422804014327


def masked_scores(queries, key_rows, seg_ids, score_scale):
    scores = (
        jnp.einsum("bqhe,bkhe->bhqk", queries, key_rows, preferred_element_type=jnp.float32)
        * score_scale
    )
    same_doc = (seg_ids[:, :, None] == seg_ids[:, None, :])[:, None]
    return jnp.where(same_doc, scores, MASKED)


def attention_forward(queries, key_rows, values, seg_ids, score_scale):
    scores = masked_scores(queries, key_rows, seg_ids, score_scale)
    highest = jnp.max(scores, axis=-1, keepdims=True)
    log_total = highest + jnp.log(jnp.sum(jnp.exp(scores - highest), axis=-1, keepdims=True))
    attn_prob = jnp.exp(scores - log_total).astype(jnp.bfloat16)
    mixed_heads = jnp.einsum(
        "bhqk,bkhe->bqhe", attn_prob, values, preferred_element_type=jnp.float32
    )
    return (mixed_heads.astype(jnp.bfloat16), log_total)


def attention_backward(queries, key_rows, values, seg_ids, log_total, grad_mixed, score_scale):
    attn_prob = jnp.exp(masked_scores(queries, key_rows, seg_ids, score_scale) - log_total)
    grad_values = jnp.einsum(
        "bhqk,bqhe->bkhe",
        attn_prob.astype(jnp.bfloat16),
        grad_mixed,
        preferred_element_type=jnp.float32,
    )
    grad_prob = jnp.einsum(
        "bqhe,bkhe->bhqk", grad_mixed, values, preferred_element_type=jnp.float32
    )
    grad_scores = (
        attn_prob * (grad_prob - jnp.sum(attn_prob * grad_prob, axis=-1, keepdims=True))
    ).astype(jnp.bfloat16)
    grad_queries = (
        jnp.einsum("bhqk,bkhe->bqhe", grad_scores, key_rows, preferred_element_type=jnp.float32)
        * score_scale
    )
    grad_keys = (
        jnp.einsum("bhqk,bqhe->bkhe", grad_scores, queries, preferred_element_type=jnp.float32)
        * score_scale
    )
    return (grad_queries, grad_keys, grad_values)


def on_device(
    tokens,
    segment_ids,
    cotangent,
    norm1_gain,
    norm1_shift,
    w_qkv,
    qv_bias,
    w_out,
    out_bias,
    norm2_gain,
    norm2_shift,
    w_up,
    up_bias,
    w_down,
    down_bias,
):
    score_scale = HEAD ** (-0.5)
    f32, bf16 = jnp.float32, jnp.bfloat16
    width = tokens.shape[-1]
    qkv_all = lax.all_gather(w_qkv, "mp", axis=2, tiled=True).reshape(width, 3 * width)
    qv_all = lax.all_gather(qv_bias, "mp", axis=1, tiled=True).astype(f32)
    out_all = lax.all_gather(w_out, "mp", axis=0, tiled=True)
    up_all = lax.all_gather(w_up, "mp", axis=1, tiled=True)
    upb_all = lax.all_gather(up_bias, "mp", axis=0, tiled=True).astype(f32)
    down_all = lax.all_gather(w_down, "mp", axis=0, tiled=True)
    proj_bias = jnp.stack([qv_all[0], jnp.zeros_like(qv_all[0]), qv_all[1]])
    gain_one = norm1_gain.astype(f32)
    shift_one = norm1_shift.astype(f32)
    gain_two = norm2_gain.astype(f32)
    shift_two = norm2_shift.astype(f32)
    rows, seq = tokens.shape[:2]
    heads = width // HEAD

    x_own = tokens.astype(f32)
    norm_one, hat_one, inv_one = norm_forward(x_own, gain_one, shift_one)
    low_one = norm_one.astype(bf16)
    projected = (
        flat_dot(low_one, qkv_all).reshape(rows, seq, 3, width) + proj_bias
    ).astype(bf16)
    heads_view = projected.reshape(rows, seq, 3, heads, HEAD)
    queries = heads_view[:, :, 0]
    key_rows = heads_view[:, :, 1]
    values = heads_view[:, :, 2]
    mixed_heads, log_total = attention_forward(queries, key_rows, values, segment_ids, score_scale)
    mixed_rows = mixed_heads.reshape(rows, seq, width)
    middle = x_own + flat_dot(mixed_rows, out_all) + out_bias.astype(f32)
    norm_two, hat_two, inv_two = norm_forward(middle, gain_two, shift_two)
    low_two = norm_two.astype(bf16)
    pre_act = flat_dot(low_two, up_all) + upb_all
    hidden = jax.nn.gelu(pre_act, approximate=False).astype(bf16)
    mixed = (middle + flat_dot(hidden, down_all) + down_bias.astype(f32)).astype(bf16)
    grad_top = cotangent.astype(f32)
    grad_downb = jnp.sum(grad_top, axis=(0, 1))
    grad_wdown = cross_dot(hidden, cotangent)
    grad_pre = (back_dot(cotangent, down_all) * gelu_slope(pre_act)).astype(bf16)
    grad_upb = jnp.sum(grad_pre, axis=(0, 1), dtype=f32)
    grad_wup = cross_dot(low_two, grad_pre)
    grad_two = back_dot(grad_pre, up_all)
    grad_norm_two, grad_gain_two, grad_shift_two = norm_backward(
        grad_two, hat_two, inv_two, gain_two
    )
    grad_middle = grad_top + grad_norm_two
    grad_mid_low = grad_middle.astype(bf16)
    grad_outb = jnp.sum(grad_mid_low, axis=(0, 1), dtype=f32)
    grad_wout = cross_dot(mixed_rows, grad_mid_low)
    grad_mixed = back_dot(grad_mid_low, out_all).astype(bf16).reshape(rows, seq, heads, HEAD)
    grad_queries, grad_keys, grad_values = attention_backward(
        queries, key_rows, values, segment_ids, log_total, grad_mixed, score_scale
    )
    grad_proj = jnp.stack(
        [
            grad_queries.reshape(rows, seq, width),
            grad_keys.reshape(rows, seq, width),
            grad_values.reshape(rows, seq, width),
        ],
        axis=2,
    ).astype(bf16)
    proj_sums = jnp.sum(grad_proj, axis=(0, 1), dtype=f32)
    grad_qv = jnp.stack([proj_sums[0], proj_sums[2]])
    grad_proj_flat = grad_proj.reshape(rows, seq, 3 * width)
    grad_qkv = cross_dot(low_one, grad_proj_flat).reshape(width, 3, width)
    grad_one = back_dot(grad_proj_flat, qkv_all)
    grad_norm_one, grad_gain_one, grad_shift_one = norm_backward(
        grad_one, hat_one, inv_one, gain_one
    )
    input_grad = (grad_middle + grad_norm_one).astype(bf16)

    def spread(value, axis):
        return lax.psum_scatter(
            value.astype(bf16), "mp", scatter_dimension=axis, tiled=True
        )

    grad_qkv, grad_wout, grad_wup, grad_wdown = lax.psum(
        (spread(grad_qkv, 2), spread(grad_wout, 0), spread(grad_wup, 1), spread(grad_wdown, 0)),
        "dp",
    )
    parts = [
        grad_gain_one, grad_shift_one, grad_outb, grad_gain_two, grad_shift_two, grad_downb,
        grad_qv.reshape(-1), grad_upb,
    ]
    sizes = [part.shape[0] for part in parts]
    total = lax.psum(jnp.concatenate(parts), ("dp", "mp"))
    pieces, start = [], 0
    for size in sizes:
        pieces.append(total[start : start + size])
        start += size
    me = lax.axis_index("mp")
    qv_here = qv_bias.shape[1]
    grad_qv = lax.dynamic_slice_in_dim(pieces[6].reshape(2, width), me * qv_here, qv_here, 1)
    up_here = up_bias.shape[0]
    grad_upb = lax.dynamic_slice_in_dim(pieces[7], me * up_here, up_here, 0)
    return (
        mixed,
        input_grad,
        pieces[0],
        pieces[1],
        grad_qkv.astype(f32),
        grad_qv,
        grad_wout.astype(f32),
        pieces[2],
        pieces[3],
        pieces[4],
        grad_wup.astype(f32),
        grad_upb,
        grad_wdown.astype(f32),
        pieces[5],
    )


def solution(mesh):
    placed = (
        P(("dp", "mp"), None, None),
        P(("dp", "mp"), None),
        P(("dp", "mp"), None, None),
        P(),
        P(),
        P(None, None, "mp"),
        P(None, "mp"),
        P("mp", None),
        P(),
        P(),
        P(),
        P(None, "mp"),
        P("mp"),
        P("mp", None),
        P(),
    )
    return jax.shard_map(
        on_device,
        mesh=mesh,
        in_specs=placed,
        out_specs=(
            P(("dp", "mp"), None, None),
            P(("dp", "mp"), None, None),
            P(),
            P(),
            P(None, None, "mp"),
            P(None, "mp"),
            P("mp", None),
            P(),
            P(),
            P(),
            P(None, "mp"),
            P("mp"),
            P("mp", None),
            P(),
        ),
        check_vma=False,
    )
```

time: 860 us -> 573 us (0.67)
  waiting for transfers between devices: 453 us -> 198 us
  blocking collectives: 69.4 us -> 55.8 us
  local copies, waits for them, and re-layouts: 34.5 us -> 46.8 us
  starting transfers between devices: 12.5 us -> 0.36 us
    reduce_scatter x8 -> x4, waiting for transfers between devices: 172 us -> 78.1 us  [spread(): lax.psum_scatter(value.astype(bf16), 'mp', scatter_dimension=axis, tiled=...]
    psum x1, waiting for transfers between devices: 174 us -> 83.6 us  [on_device(): lax.psum((spread(grad_qkv, 2), spread(grad_wout, 0), spread(grad_wup, 1),...]
    all_gather x8 -> x4, waiting for transfers between devices: 104 us -> 33.5 us  [the longest x1 21.1 us: on_device(): down_all = lax.all_gather(w_down, 'mp', axis=0, tiled=True)]
    psum x2 -> x1, blocking collectives: 63.3 us -> 44.2 us  [on_device(): total = lax.psum(jnp.concatenate(parts), ('dp', 'mp'))]
    reduce_scatter x8 -> x4, starting transfers between devices: 11.9 us -> 0.16 us  [spread(): lax.psum_scatter(value.astype(bf16), 'mp', scatter_dimension=axis, tiled=...]
    unnamed x182 -> x72, local copies, waits for them, and re-layouts: 26.7 us -> 15.1 us
    convert_element_type x2 -> x3, local copies, waits for them, and re-layouts: 3.89 us -> 14.3 us  [the longest x1 12.5 us: on_device(): grad_proj = jnp.stack([grad_queries.reshape(rows, seq, width), grad_keys....]
    dot_general x2 -> x1, matrix products: 24.8 us -> 17.1 us  [attention_backward(): jnp.einsum('bqhe,bkhe->bhqk', grad_mixed, values, preferred_element_type=...]
  transfers between devices with their start and end apart: 17 -> 9, of which waited for: 12 -> 5; matrix products, arithmetic and copies ran while one was open for 30% -> 39% of each run, Pallas kernels for 0% -> 0%
where the time goes in v1:
time: 573 us; the launch traced here: 568 us
  waiting for transfers between devices  198 us (35%)
  matrix products  162 us (28%)
  other arithmetic  90.3 us (16%)
  blocking collectives  55.8 us (10%)
  local copies, waits for them, and re-layouts  46.8 us (8%)
  between operations  14.9 us (3%)
    psum x1, waiting for transfers between devices, on_device(): lax.psum((spread(grad_qkv, 2), spread(grad_wout, 0), spread(grad_wup, 1),...  83.6 us
    reduce_scatter x4, waiting for transfers between devices, spread(): lax.psum_scatter(value.astype(bf16), 'mp', scatter_dimension=axis, tiled=...  78.1 us
    psum x1, blocking collectives, on_device(): total = lax.psum(jnp.concatenate(parts), ('dp', 'mp'))  44.2 us
    dot_general x4, matrix products, flat_dot(): jnp.dot(left_side.reshape(-1, left_side.shape[-1]), right_side, preferred...  38.5 us
    convert_element_type x1, other arithmetic, on_device(): hidden = jax.nn.gelu(pre_act, approximate=False).astype(bf16)  31.3 us
    dot_general x4, matrix products, back_dot(): lax.dot_general(grad_in.reshape(-1, grad_in.shape[-1]), weight, (((1,), (...  30.7 us
    dot_general x4, matrix products, cross_dot(): lax.dot_general(left_side.reshape(-1, left_side.shape[-1]), right_side.re...  26.4 us
    all_gather x1, waiting for transfers between devices, on_device(): down_all = lax.all_gather(w_down, 'mp', axis=0, tiled=True)  21.1 us
  transfers between devices with their start and end apart: 9, of which 5 were waited for; matrix products, arithmetic and copies ran while one was open for 39% of the time, Pallas kernels for 0%

profile of v1, /device:TPU:0, one launch (start us, length us, event | category | flops | bytes accessed | tf_op | source)
XLA Modules:
  0.0 567.8 jit_solution(4004627430209753270)
XLA Ops:
  13.5 6.2 %all-gather = bf16[4,192,2]{1,2,0:T(2,128)(2,1)S(1)} all-gather(bf16[1,192,2]{1,2,0:T(2,128)(2,1)} %bitcast.163), channel_id=1, replica_groups=mesh['dp'=8,'mp'=4] {'mp'}, dimensions={0}, use_global_device_ids=true | all-gather | bytes 3840 | tf_op jit(solution)/shard_map/all_gather | solution.py:128
  20.5 1.9 convert_reduce_fusion.2
  23.0 5.4 all-gather.1
  29.0 1.8 fusion.35
  30.7 12.4 %all-gather.7.cloned.1.call-done = bf16[768,3,768]{0,2,1:T(8,128)(2,1)} async-done(((bf16[768,3,192]{0,2,1:T(8,128)(2,1)}), bf16[768,3,768]{0,2,1:T(8,128)(2,1)}) %all-gather.7.cloned.1.call-update) | async-done | bytes 3538960 | tf_op jit(solution)/shard_map/all_gather | solution.py:127
  43.2 8.5 %add_convert_fusion = bf16[2,512,3,768]{3,1,2,0:T(8,128)(2,1)} fusion(f32[3,768]{1,0:T(4,128)S(1)} %pad_maximum_fusion, bf16[768,3,768]{0,2,1:T(8,128)(2,1)} %all-gather.7.cloned.1.call-done, bf16[2,512,768]{2,1,0:T(8,128)(2,1)} %fusion.35), kind=kOutput, calls=%fused_computation.41 | convolution fusion | flops 3628597248 | bytes 9839616 | tf_op jit(solution)/shard_map/dot_general | solution.py:14
  51.6 7.0 %copy.107 = bf16[2,512,3,768]{1,3,0,2:T(8,128)(2,1)} copy(bf16[2,512,3,768]{3,1,2,0:T(8,128)(2,1)} %add_convert_fusion) | data formatting | bytes 9437184 | tf_op jit(solution)/shard_map/reshape | solution.py:147
  58.6 12.5 %fusion = (f32[2,12,512]{2,1,0:T(8,128)S(1)}, f32[2,12,512,512]{2,3,1,0:T(8,128)}) fusion(pred[2,512,512]{1,2,0:T(8,128)(4,1)S(1)} %broadcast_compare_fusion, bf16[2,512,3,12,64]{1,4,3,0,2:T(8,128)(2,1)} %bitcast.139), kind=kOutput, calls=%fused_computation.5 | convolution fusion | flops 824168448 | bytes 28884992 | tf_op jit(solution)/shard_map/bqhe,bkhe->bhqk/dot_general | solution.py:64
  71.1 11.9 %exponential_reduce_fusion = f32[2,12,512]{2,1,0:T(8,128)S(1)} fusion(f32[2,12,512,512]{2,3,1,0:T(8,128)} %get-tuple-element.45, f32[2,12,512]{2,1,0:T(8,128)S(1)} %get-tuple-element.44, pred[2,512,512]{1,2,0:T(8,128)(4,1)S(1)} %broadcast_compare_fusion), kind=kLoop, calls=%fused_computation.3 | loop fusion | flops 25153536 | bytes 25788416 | tf_op jit(solution)/shard_map/reduce_sum | solution.py:74
  83.0 11.7 %convolution_convert_fusion.1 = bf16[2,12,64,512]{3,2,1,0:T(8,128)(2,1)S(1)} fusion(bf16[2,512,3,12,64]{1,4,3,0,2:T(8,128)(2,1)} %bitcast.140, f32[2,12,512,512]{2,3,1,0:T(8,128)} %get-tuple-element.45, f32[2,12,512]{2,1,0:T(8,128)S(1)} %log_add_fusion, pred[2,512,512]{1,2,0:T(8,128)(4,1)S(1)} %broadcast_compare_fusion), kind=kOutput, calls=%fused_computation.90 | convolution fusion | flops 831258624 | bytes 28884992 | tf_op jit(solution)/shard_map/bhqk,bkhe->bqhe/dot_general | solution.py:76
  94.8 1.6 copy.95
  98.0 3.8 fusion.68
  102.4 16.7 %fusion.45 = (u8[512,3072]{1,0:T(8,128)(4,1)}, u8[512,3072]{1,0:T(8,128)(4,1)}, f32[2,512,3072]{2,1,0:T(8,128)}) fusion(f32[3072]{0:T(1024)S(1)} %bitcast.159, bf16[768,3072]{1,0:T(8,128)(2,1)} %all-gather.11.cloned.1.call-done, f32[2,512,768]{2,1,0:T(8,128)S(1)} %get-tuple-element.47, f32[768]{0:T(1024)S(1)} %convert_element_type.123, ...), kind=kOutput, calls=%fused_computation.83 | convolution fusion | flops 4876664832 | bytes 23619584 | tf_op jit(solution)/shard_map/dot_general | solution.py:14
  119.1 21.1 %all-gather.13.cloned.1.call-done = bf16[3072,768]{1,0:T(8,128)(2,1)} async-done(((bf16[768,768]{1,0:T(8,128)(2,1)}), bf16[3072,768]{1,0:T(8,128)(2,1)}) %all-gather.13.cloned.1.call-update) | async-done | bytes 4718608 | tf_op jit(solution)/shard_map/all_gather | solution.py:132
  140.2 12.3 %convert_reduce_fusion = (f32[3072]{0:T(1024)S(1)}, bf16[2,512,3072]{2,1,0:T(8,128)(2,1)S(1)}) fusion(f32[2,512,3072]{2,1,0:T(8,128)} %get-tuple-element.48, f32[3072]{0:T(1024)S(1)} %bitcast.160, bf16[2,512,768]{2,1,0:T(8,128)(2,1)} %param.17, bf16[3072,768]{1,0:T(8,128)(2,1)} %all-gather.13.cloned.1.call-done), kind=kOutput, calls=%fused_computation.23 | convolution fusion | flops 4872729600 | bytes 25190400 | tf_op jit(solution)/shard_map/dot_general | solution.py:21
  152.6 5.7 %multiply_reduce_fusion.1 = (f32[768]{0:T(1024)S(1)}, f32[2,512]{1,0:T(2,128)S(1)}, f32[2,512]{1,0:T(2,128)S(1)}, f32[768]{0:T(1024)S(1)}, f32[2,512,768]{2,1,0:T(8,128)S(1)}) fusion(f32[2,512,768]{2,1,0:T(8,128)S(1)} %get-tuple-element.47, f32[2,512]{1,0:T(2,128)S(1)} %add_rsqrt_fusion, f32[2,512]{1,0:T(2,128)S(1)} %broadcast_multiply_fusion.4, ...), kind=kOutput, calls=%fused_computation.76 | convolution fusion | flops 4838912000 | bytes 17327104 | tf_op jit(solution)/shard_map/dot_general | solution.py:21
  161.1 2.6 convolution_convert_fusion.2
  163.7 1.7 copy.87
  165.4 12.6 %fusion.56 = bf16[2,12,64,512]{3,2,1,0:T(8,128)(2,1)} fusion(bf16[2,512,12,64]{1,3,2,0:T(8,128)(2,1)S(1)} %bitcast.148, f32[2,12,512,512]{2,3,1,0:T(8,128)} %get-tuple-element.45, f32[2,12,512]{2,1,0:T(8,128)S(1)} %log_add_fusion, pred[2,512,512]{1,2,0:T(8,128)(4,1)S(1)} %copy-done.5), kind=kOutput, calls=%fused_computation.103 | convolution fusion | flops 830472192 | bytes 28884992 | tf_op jit(solution)/shard_map/bhqk,bqhe->bkhe/dot_general | solution.py:84
  178.0 17.1 %multiply_reduce_fusion = (f32[2,12,512]{2,1,0:T(8,128)S(1)}, f32[2,12,512,512]{2,3,1,0:T(8,128)}) fusion(f32[2,12,512,512]{2,3,1,0:T(8,128)} %get-tuple-element.45, f32[2,12,512]{2,1,0:T(8,128)S(1)} %log_add_fusion, pred[2,512,512]{1,2,0:T(8,128)(4,1)S(1)} %copy-done.5, bf16[2,512,12,64]{1,3,2,0:T(8,128)(2,1)S(1)} %bitcast.149, ...), kind=kOutput, calls=%fused_computation.1 | convolution fusion | flops 836751360 | bytes 54099968 | tf_op jit(solution)/shard_map/bqhe,bkhe->bhqk/dot_general | solution.py:90
  195.0 4.3 convolution_convert_fusion.3
  199.5 18.0 %multiply_convert_fusion = bf16[2,12,512,512]{2,3,1,0:T(8,128)(2,1)S(1)} fusion(f32[2,12,512,512]{2,3,1,0:T(8,128)} %get-tuple-element.51, f32[2,12,512,512]{2,3,1,0:T(8,128)} %get-tuple-element.45, f32[2,12,512]{2,1,0:T(8,128)S(1)} %get-tuple-element.50, f32[2,12,512]{2,1,0:T(8,128)S(1)} %log_add_fusion, pred[2,512,512]{1,2,0:T(8,128)(4,1)S(1)} %copy-done.5), kind=kLoop, calls=%fused_computation | loop fusion | flops 37748736 | bytes 63537152 | tf_op jit(solution)/shard_map/convert_element_type | solution.py:95
  217.6 2.1 convolution_multiply_fusion.1
  219.7 2.4 copy-done
  222.1 2.6 copy.93
  224.7 1.6 copy.91
  226.3 10.2 %convolution_multiply_fusion = bf16[2,12,64,512]{3,2,1,0:T(8,128)(2,1)} fusion(bf16[2,12,512,512]{2,3,1,0:T(8,128)(2,1)} %copy-done, bf16[2,512,3,12,64]{1,4,3,0,2:T(8,128)(2,1)} %bitcast.142), kind=kOutput, calls=%fused_computation.88 | convolution fusion | flops 806879232 | bytes 15728640 | tf_op jit(solution)/shard_map/bhqk,bqhe->bkhe/dot_general | solution.py:101
  236.5 2.6 copy.92
  239.1 3.9 convert_reduce_fusion.1
  243.0 12.5 %copy.94 = bf16[2,512,3,768]{1,0,3,2:T(2,128)(2,1)} copy(bf16[2,512,3,768]{3,1,2,0:T(8,128)(2,1)} %get-tuple-element.29) | data formatting | bytes 9437184 | tf_op jit(solution)/shard_map/convert_element_type | solution.py:184
  255.5 4.0 copy.110
  259.5 5.4 convolution_convert_fusion
  265.0 31.3 %fusion.4 = bf16[2,512,3072]{2,1,0:T(8,128)(2,1)S(1)} fusion(f32[2,512,3072]{2,1,0:T(8,128)} %get-tuple-element.48, f32[3072]{0:T(1024)S(1)} %bitcast.161, u8[512,3072]{1,0:T(8,128)(4,1)S(1)} %copy-done.13, u8[512,3072]{1,0:T(8,128)(4,1)S(1)} %copy-done.12), kind=kLoop, calls=%fused_computation.11 | loop fusion | flops 223346688 | bytes 22032384 | tf_op jit(solution)/shard_map/convert_element_type | solution.py:157
  296.2 2.7 copy-done.9
  298.9 6.9 %bitcast_convert_fusion = bf16[3072,768]{1,0:T(8,128)(2,1)} fusion(bf16[2,512,3072]{2,1,0:T(8,128)(2,1)S(1)} %fusion.4, bf16[2,512,768]{2,1,0:T(8,128)(2,1)S(1)} %copy-done.11), kind=kOutput, calls=%fused_computation.38 | convolution fusion | flops 4834197504 | bytes 12582912 | tf_op jit(solution)/shard_map/dot_general | solution.py:31
  305.8 1.8 copy-done.2
  307.7 9.8 %bitcast_convert_fusion.1 = bf16[768,3072]{1,0:T(8,128)(2,1)} fusion(bf16[2,512,3072]{2,1,0:T(8,128)(2,1)} %copy-done.28, f32[2,512,768]{2,1,0:T(8,128)S(1)} %copy-done.2, f32[768]{0:T(1024)S(1)} %convert_element_type.123, f32[768]{0:T(1024)S(1)} %convert_element_type.122, f32[2,512]{1,0:T(2,128)S(1)} %add_rsqrt_fusion, ...), kind=kOutput, calls=%fused_computation.39 | convolution fusion | flops 4838129664 | bytes 14170112 | tf_op jit(solution)/shard_map/dot_general | solution.py:31
  318.3 10.1 %fusion.41 = (f32[768]{0:T(1024)S(1)}, f32[2,512]{1,0:T(2,128)S(1)}, f32[2,512]{1,0:T(2,128)S(1)}, f32[768]{0:T(1024)S(1)}, f32[2,512,768,1]{2,1,3,0:T(8,128)}) fusion(bf16[2,512,768]{2,1,0:T(8,128)(2,1)} %param.15, f32[2,512]{1,0:T(2,128)S(1)} %copy-done.23, f32[2,512]{1,0:T(2,128)S(1)} %copy-done.19, f32[768]{0:T(1024)S(1)} %copy-done.21, ...), kind=kOutput, calls=%fused_computation.71 | convolution fusion | flops 3631739392 | bytes 13001728 | tf_op jit(solution)/shard_map/dot_general | solution.py:21
  328.4 27.5 %reduce-scatter.11.cloned.1.call-done = bf16[768,768]{1,0:T(8,128)(2,1)} async-done(((bf16[3072,768]{1,0:T(8,128)(2,1)}), bf16[768,768]{1,0:T(8,128)(2,1)}) %reduce-scatter.11.cloned.1.call-update) | async-done | bytes 1179664 | tf_op jit(solution)/shard_map/reduce_scatter | solution.py:196
  355.9 50.6 %reduce-scatter.9.cloned.1.call-done = bf16[768,768]{1,0:T(8,128)(2,1)} async-done(((bf16[768,3072]{1,0:T(8,128)(2,1)}), bf16[768,768]{1,0:T(8,128)(2,1)}) %reduce-scatter.9.cloned.1.call-update) | async-done | bytes 1179664 | tf_op jit(solution)/shard_map/reduce_scatter | solution.py:196
  406.5 6.2 %convert_reduce_fusion.3 = (f32[768]{0:T(1024)S(1)}, bf16[2,512,768]{2,1,0:T(8,128)(2,1)}) fusion(bf16[2,512,768]{2,1,0:T(8,128)(2,1)} %param.17, f32[2,512]{1,0:T(2,128)S(1)} %broadcast_multiply_fusion, f32[2,512]{1,0:T(2,128)S(1)} %copy-done.23, f32[2,512]{1,0:T(2,128)S(1)} %copy-done.19, bf16[2,512,768]{2,1,0:T(8,128)(2,1)} %param.15, ...), kind=kLoop, calls=%fused_computation.52 | loop fusion | flops 15727872 | bytes 14197760 | tf_op jit(solution)/shard_map/reduce_sum | solution.py:160
  412.7 44.2 %psum.35 = f32[9216]{0:T(1024)S(1)} all-reduce(f32[9216]{0:T(1024)S(1)} %constant_dynamic-update-slice_fusion), channel_id=1, replica_groups=mesh['dp'=8,'mp'=4] {'dp','mp'}, use_global_device_ids=true, to_apply=%region_19.20 | all-reduce | flops 9216 | bytes 73728 | tf_op jit(solution)/shard_map/psum | solution.py:209
  458.9 9.4 %add_convert_fusion.1 = bf16[2,512,768]{2,1,0:T(8,128)(2,1)} fusion(f32[2,512,768]{2,1,0:T(8,128)S(1)} %copy-done.2, bf16[2,512,3072]{2,1,0:T(8,128)(2,1)} %copy-done.9, bf16[3072,768]{1,0:T(8,128)(2,1)} %all-gather.13.cloned.1.call-done, f32[768]{0:T(1024)S(1)} %convert_element_type.127), kind=kOutput, calls=%fused_computation.79 | convolution fusion | flops 4834197504 | bytes 15731712 | tf_op jit(solution)/shard_map/dot_general | solution.py:14
  468.3 83.6 %all-reduce.3.cloned.1.call-done = (bf16[768,3,192]{0,2,1:T(8,128)(2,1)}, bf16[192,768]{1,0:T(8,128)(2,1)}, bf16[768,768]{1,0:T(8,128)(2,1)}, bf16[768,768]{1,0:T(8,128)(2,1)}) async-done(((bf16[768,3,192]{0,2,1:T(8,128)(2,1)}, bf16[192,768]{1,0:T(8,128)(2,1)}, bf16[768,768]{1,0:T(8,128)(2,1)}, bf16[768,768]{1,0:T(8,128)(2,1)}), (bf16[768,3,192]{0,2,1:T(8,128)(2,1)}, bf16[192,768]{1,0:T(8,128)(2,1)}, ...) | async-done | bytes 3538960 | tf_op jit(solution)/shard_map/psum | solution.py:200
  552.0 1.9 convert_element_type.143
  553.9 2.5 convert_element_type.141
  556.4 2.8 convert_element_type.145
  559.2 1.6 convert_element_type.147
  (126 shorter events, 16.0 us)
Async XLA Ops:
  7.2 15.2 %copy-start.3 = (bf16[2,512,768]{2,1,0:T(8,128)(2,1)S(1)}, bf16[2,512,768]{2,1,0:T(8,128)(2,1)}, u32[]{:S(2)}) copy-start(bf16[2,512,768]{2,1,0:T(8,128)(2,1)} %param.15) | copy-start | bytes 4718596
  7.2 21.2 %copy-start.24 = (s32[2,512]{1,0:T(2,128)S(1)}, s32[2,512]{1,0:T(2,128)}, u32[]{:S(2)}) copy-start(s32[2,512]{1,0:T(2,128)} %param.16) | copy-start | bytes 12292
  7.2 36.0 %all-gather.7.cloned.1.call-start = ((), (), s32[]{:S(2)}) async-start(), calls=%async_computation.4 | async-start | bytes 4423680 | tf_op jit(solution)/shard_map/all_gather | solution.py:127
  7.9 90.1 %all-gather.9.cloned.1.call-start = ((), (), s32[]{:S(2)}) async-start(), calls=%async_computation.5 | async-start | bytes 1474560 | tf_op jit(solution)/shard_map/all_gather | solution.py:129
  8.7 93.7 %all-gather.11.cloned.1.call-start = ((), (), s32[]{:S(2)}) async-start(), calls=%async_computation.6 | async-start | bytes 5898240 | tf_op jit(solution)/shard_map/all_gather | solution.py:130
  9.4 130.8 %all-gather.13.cloned.1.call-start = ((), (), s32[]{:S(2)}) async-start(), calls=%async_computation.7 | async-start | bytes 5898240 | tf_op jit(solution)/shard_map/all_gather | solution.py:132
  10.0 318.4 %reduce-scatter.7.cloned.1.call-start = ((), (), s32[]{:S(2)}) async-start(), calls=%async_computation.9 | async-start | bytes 1474560 | tf_op jit(solution)/shard_map/reduce_scatter | solution.py:196
  12.1 39.5 %copy-start.20 = (f32[768]{0:T(1024)}, f32[768]{0:T(1024)S(1)}, u32[]{:S(2)}) copy-start(f32[768]{0:T(1024)S(1)} %convert_element_type.113) | copy-start | bytes 9220
  22.4 6.6 %copy-start.18 = (f32[2,512]{1,0:T(2,128)}, f32[2,512]{1,0:T(2,128)S(1)}, u32[]{:S(2)}) copy-start(f32[2,512]{1,0:T(2,128)S(1)} %broadcast_multiply_fusion.5) | copy-start | bytes 12292
  23.0 28.6 %copy-start.22 = (f32[2,512]{1,0:T(2,128)}, f32[2,512]{1,0:T(2,128)S(1)}, u32[]{:S(2)}) copy-start(f32[2,512]{1,0:T(2,128)S(1)} %add_rsqrt_fusion.1) | copy-start | bytes 12292
  28.8 54.2 %copy-start.4 = (pred[2,512,512]{1,2,0:T(8,128)(4,1)}, pred[2,512,512]{1,2,0:T(8,128)(4,1)S(1)}, u32[]{:S(2)}) copy-start(pred[2,512,512]{1,2,0:T(8,128)(4,1)S(1)} %broadcast_compare_fusion) | copy-start | bytes 1572868
  94.8 3.2 copy-start.15
  101.8 56.4 %copy-start.1 = (f32[2,512,768]{2,1,0:T(8,128)}, f32[2,512,768]{2,1,0:T(8,128)S(1)}, u32[]{:S(2)}) copy-start(f32[2,512,768]{2,1,0:T(8,128)S(1)} %get-tuple-element.47) | copy-start | bytes 9437188
  140.2 12.4 %copy-start.26 = (bf16[768,3072]{1,0:T(8,128)(2,1)S(1)}, bf16[768,3072]{1,0:T(8,128)(2,1)}, u32[]{:S(2)}) copy-start(bf16[768,3072]{1,0:T(8,128)(2,1)} %all-gather.11.cloned.1.call-done) | copy-start | bytes 14155780
  152.5 5.7 %copy-start.28 = (bf16[2,512,3072]{2,1,0:T(8,128)(2,1)}, bf16[2,512,3072]{2,1,0:T(8,128)(2,1)S(1)}, u32[]{:S(2)}) copy-start(bf16[2,512,3072]{2,1,0:T(8,128)(2,1)S(1)} %get-tuple-element.54) | copy-start | bytes 18874372
  152.6 5.7 %copy-start.10 = (bf16[2,512,768]{2,1,0:T(8,128)(2,1)S(1)}, bf16[2,512,768]{2,1,0:T(8,128)(2,1)}, u32[]{:S(2)}) copy-start(bf16[2,512,768]{2,1,0:T(8,128)(2,1)} %param.17) | copy-start | bytes 4718596
  158.3 1.7 copy-start.6
  158.3 2.8 copy-start.27
  159.9 1.2 copy-start.16
  161.1 4.3 copy-start.5
  195.0 22.5 %slice-start = ((s8[4718592]{0:T(1024)(128)(4,1)}), s8[524288]{0:T(1024)(128)(4,1)S(1)}, s32[]{:S(2)}) async-start(s8[4718592]{0:T(1024)(128)(4,1)} %bitcast.143), calls=%async_computation.13 | async-start | bytes 1048576
  199.4 129.0 %reduce-scatter.5.cloned.1.call-start = ((), (), s32[]{:S(2)}) async-start(), calls=%async_computation.8 | async-start | bytes 4423680 | tf_op jit(solution)/shard_map/reduce_scatter | solution.py:196
  199.4 18.1 %slice-start.1 = ((s8[4718592]{0:T(1024)(128)(4,1)}), s8[4194304]{0:T(1024)(128)(4,1)S(1)}, s32[]{:S(2)}) async-start(s8[4718592]{0:T(1024)(128)(4,1)} %bitcast.143), calls=%async_computation.14 | async-start | bytes 8388608
  217.5 4.6 copy-start
  226.3 12.8 %copy-start.7 = (bf16[2,512,1,768]{3,1,2,0:T(8,128)(2,1)S(1)}, bf16[2,512,1,768]{3,1,2,0:T(8,128)(2,1)}, u32[]{:S(2)}) copy-start(bf16[2,512,1,768]{3,1,2,0:T(8,128)(2,1)} %copy.93) | copy-start | bytes 4718596
  226.3 12.8 %copy-start.8 = (bf16[2,512,1,768]{3,1,2,0:T(8,128)(2,1)S(1)}, bf16[2,512,1,768]{3,1,2,0:T(8,128)(2,1)}, u32[]{:S(2)}) copy-start(bf16[2,512,1,768]{3,1,2,0:T(8,128)(2,1)} %copy.91) | copy-start | bytes 4718596
  255.5 4.0 copy-start.14
  259.5 5.5 copy-start.12
  259.5 5.5 copy-start.13
  264.9 91.0 %reduce-scatter.11.cloned.1.call-start = ((), (), s32[]{:S(2)}) async-start(), calls=%async_computation.11 | async-start | bytes 5898240 | tf_op jit(solution)/shard_map/reduce_scatter | solution.py:196
  265.0 33.9 %copy-start.11 = (bf16[2,512,768]{2,1,0:T(8,128)(2,1)S(1)}, bf16[2,512,768]{2,1,0:T(8,128)(2,1)}, u32[]{:S(2)}) copy-start(bf16[2,512,768]{2,1,0:T(8,128)(2,1)} %param.17) | copy-start | bytes 4718596
  296.2 2.7 copy-start.9
  305.8 1.9 copy-start.2
  305.8 100.6 %reduce-scatter.9.cloned.1.call-start = ((), (), s32[]{:S(2)}) async-start(), calls=%async_computation.10 | async-start | bytes 5898240 | tf_op jit(solution)/shard_map/reduce_scatter | solution.py:196
  317.5 0.7 copy-start.25
  317.5 0.7 copy-start.19
  317.5 0.7 copy-start.21
  317.5 0.8 copy-start.23
  317.5 234.4 %all-reduce.3.cloned.1.call-start = ((), (), s32[]{:S(2)}) async-start(), calls=%async_computation.12 | async-start | bytes 7077888 | tf_op jit(solution)/shard_map/psum | solution.py:200
  551.9 7.3 %copy-start.17 = (bf16[768,768]{1,0:T(8,128)(2,1)S(1)}, bf16[768,768]{1,0:T(8,128)(2,1)}, u32[]{:S(2)}) copy-start(bf16[768,768]{1,0:T(8,128)(2,1)} %get-tuple-element.27) | copy-start | bytes 3538948
Sparse Core Ops, SparseCore 0:
  9.6 33.5 all-gather.6
  44.7 17.4 all-gather.8
  63.8 37.4 all-gather.10
  102.7 37.4 all-gather.12
  199.5 25.7 reduce-scatter.6
  265.0 40.4 reduce-scatter.4
  308.0 47.8 reduce-scatter.10
  358.6 47.8 reduce-scatter.8
  410.4 141.5 all-reduce.2

commit v2 on v1

v2 whole, which is shorter than its diff:
```python
import functools

import jax
import jax.numpy as jnp
from jax import lax
from jax.experimental import pallas as pl
from jax.experimental.pallas import tpu as pltpu
from jax.sharding import PartitionSpec as P

HEAD = 64
EPS = 1e-06
MASKED = -1e30
UNIT = 256
SPLIT = 2
INV_LANE = 32
F32, BF16 = jnp.float32, jnp.bfloat16

GAIN1, SHIFT1, OUTB, GAIN2, SHIFT2, DOWNB, QUERYB, VALUEB, UPB = range(9)

BETWEEN, FIRST_HEADS, LAST_NORM, STEPS = 12, 13, 19, 27
FAR_PAIRS = (0, 1, 0, 1, 1, 0)

WHEN = {
    "pass_x": {0: 4, 1: 5, 3: 6},
    "pass_z": {1: 4, 3: 5, 5: 6},
    "pass_y": {2: 4, 5: 5, 7: 6},
    "pass_done": {2: 4, 6: 5, 8: 6},
    "mate_done": {0: 4, 4: 5, 10: 6},
    "pair_send": {1: 0, 3: 1, 5: 2, 7: 3, 9: 4, 11: 5},
    "pair_add": {2: 0, 4: 1, 6: 2, 8: 3, 10: 4, 12: 5},
    "far_send": {14: 0, 15: 1, 16: 2},
    "far_add": {15: 0, 16: 1, 17: 2},
    "near_send": {17: 0, 18: 1, 19: 2},
    "near_add": {18: 0, 19: 1, 20: 2},
    "add_x": {8: 0, 11: 1, 13: 2, 15: 3, 17: 4, 18: 5, 20: 6, 21: 7, 22: 8},
    "add_y": {10: 0, 13: 1, 15: 2, 16: 3, 18: 4, 20: 5, 21: 6, 22: 7, 23: 8},
    "add_z": {12: 0, 14: 1, 16: 2, 17: 3, 19: 4, 21: 5, 22: 6, 23: 7, 24: 8},
    "give_y": {13: 0, 15: 1, 17: 2, 18: 3, 20: 4, 22: 5, 23: 6, 24: 7, 25: 8},
    "finish": {15: 0, 17: 1, 18: 2, 19: 3, 21: 4, 23: 5, 24: 6, 25: 7, 26: 8},
    "sums": {20: 0, 21: 1, 22: 2, 23: 3, 24: 4},
}


def dot(left, right, left_dim, right_dim):
    return lax.dot_general(
        left, right, (((left_dim,), (right_dim,)), ((), ())), preferred_element_type=F32
    )


def column_sum(values):
    return jnp.sum(values, axis=0, keepdims=True)


def gelu_parts(pre):
    size = jnp.abs(pre) * 0.7071067811865476
    part = 1.0 / (1.0 + 0.3275911 * size)
    tail = jnp.exp(-0.5 * pre * pre)
    poly = part * (
        0.254829592
        + part * (-0.284496736 + part * (1.421413741 + part * (-1.453152027 + part * 1.061405429)))
    )
    half = 0.5 * poly * tail
    return jnp.where(pre >= 0, 1.0 - half, half), tail * 0.3989422804014327


def kernel(
    x_in, g_in, seg_ref, small_ref, bias_in, qkv_in, out_in, up_in, down_in,
    mixed_out, input_out, grads_out, sums_out,
    wq, wo, wm, wb, grad, mate_buf, x_buf, y_buf, z_buf,
    x_ref, g_ref, a1_ref, proj_ref, o_ref, x1_ref, hat2_ref, a2_ref, da2_ref,
    hid_ref, low_ref, lse_ref, aug_q, aug_k, sums, sums_recv,
    local_sem, wm_s, wm_r, wx_s, wx_r, wy_s, wy_r, wz_s, wz_r, wf_s, wf_r, wb_s, wb_r,
    pair_s, pair_r, ex_s, ex_r, ey_s, ey_r, ez_s, ez_r, fz_s, fz_r, fy_s, fy_r, sums_s, sums_r,
    *, rows, seq,
):
    tokens, width = x_ref.shape
    dp, mp = lax.axis_index("dp"), lax.axis_index("mp")
    c, x = mp % 2, mp // 2
    y, z = dp % 2, (dp // 2) % 4
    block = dp - dp % 8
    zb = z % 2
    nx, nc, ny = 1 - x, 1 - c, 1 - y

    def device(zz, yy, xx, cc):
        return (block + zz * 2 + yy, xx * 2 + cc)

    mate = device(z, y, x, nc)
    x_peer = device(z, y, nx, c)
    y_peer = device(z, ny, x, c)
    z_peers = [device((z + step) % 4, y, x, c) for step in (1, 2, 3)]
    z_pair = device(z + 1 - 2 * zb, y, x, c)
    cross = device(z, y, nx, nc)

    def remote(src, dst, send, recv, where):
        return pltpu.make_async_remote_copy(
            src_ref=src, dst_ref=dst, send_sem=send, recv_sem=recv,
            device_id=where, device_id_type=pl.DeviceIdType.MESH,
        )

    up_stage = grad.at[0, 0, pl.ds(0, width)]
    locals_ = [
        pltpu.make_async_copy(qkv_in, wq.at[x, :, :, c], local_sem.at[0]),
        pltpu.make_async_copy(x_in, x_ref, local_sem.at[1]),
        pltpu.make_async_copy(bias_in, wb.at[x, c], local_sem.at[2]),
        pltpu.make_async_copy(out_in, wo.at[x, :, c], local_sem.at[3]),
        pltpu.make_async_copy(up_in, up_stage, local_sem.at[4]),
        pltpu.make_async_copy(down_in, wm.at[x, c, :, pl.ds(UNIT, UNIT)], local_sem.at[5]),
        pltpu.make_async_copy(g_in, g_ref, local_sem.at[6]),
    ]
    for copy in locals_:
        copy.start()

    barrier = pltpu.get_barrier_semaphore()
    everyone = [mate, x_peer, cross, y_peer] + z_peers
    for peer in everyone:
        pl.semaphore_signal(barrier, inc=1, device_id=peer, device_id_type=pl.DeviceIdType.MESH)
    pl.semaphore_wait(barrier, len(everyone))

    third = width // 3

    def piece(kind, index, xx, cc, lanes=slice(None)):
        if kind == "q":
            return wq.at[xx, index, :, cc, :, lanes]
        if kind == "o":
            return wo.at[xx, :, cc, :, lanes]
        return wm.at[xx, cc, index, :, lanes]

    def lanes_of(part):
        return pl.ds(pl.multiple_of(part * third, third), third)

    part_x = jnp.where(zb == 1, 2, y)
    part_z = jnp.where(zb == 1, y, 2)

    def kinds(number, run):
        if isinstance(number, int):
            run("q" if number < 3 else "o" if number == 3 else "m", number - 4 if number > 3 else number)
            return
        pl.when(number < 3)(lambda: run("q", number))
        pl.when(number == 3)(lambda: run("o", number))
        pl.when(number > 3)(lambda: run("m", number - 4))

    def to_mate(number, kind, index):
        own = piece(kind, index, x, c)
        return remote(own, own, wm_s.at[number], wm_r.at[number], mate)

    def to_x(number, kind, index):
        own = piece(kind, index, x, c, lanes_of(part_x))
        return remote(own, own, wx_s.at[number], wx_r.at[number], x_peer)

    def on_z(number, kind, index, part):
        held = piece(kind, index, nx, c, lanes_of(part))
        return remote(held, held, wz_s.at[number], wz_r.at[number], z_pair)

    def on_y(number, kind, index, part):
        held = piece(kind, index, nx, c, lanes_of(part))
        return remote(held, held, wy_s.at[number], wy_r.at[number], y_peer)

    def forward(number, kind, index):
        held = piece(kind, index, nx, c)
        return remote(held, held, wf_s.at[number], wf_r.at[number], mate)

    def mate_done(number):
        kinds(number, lambda kind, index: to_mate(number, kind, index).wait_recv())

    def start_x(number):
        kinds(number, lambda kind, index: to_x(number, kind, index).start())

    def pass_x(number):
        def run(kind, index):
            to_x(number, kind, index).wait_recv()
            on_z(number, kind, index, part_x).start()
            pl.when(zb == 0)(lambda: on_y(number, kind, index, part_x).start())

        kinds(number, run)
        pl.when(number < 5)(lambda: start_x(number + 2))

    def pass_z(number):
        def run(kind, index):
            on_z(number, kind, index, part_x).wait_recv()
            pl.when(zb == 1)(lambda: on_y(number, kind, index, part_z).start())

        kinds(number, run)

    def pass_y(number):
        def run(kind, index):
            on_y(number, kind, index, part_x).wait_recv()
            forward(number, kind, index).start()

        kinds(number, run)

    def pass_done(number):
        kinds(number, lambda kind, index: forward(number, kind, index).wait_recv())

    biases = [
        remote(wb.at[x, c], wb.at[x, c], wb_s.at[i], wb_r.at[i], peer)
        for i, peer in enumerate((mate, x_peer, cross))
    ]
    locals_[0].wait()
    start_x(0)
    for number in range(3):
        to_mate(number, "q", number).start()
    locals_[2].wait()
    for copy in biases:
        copy.start()
    start_x(1)
    locals_[3].wait()
    to_mate(3, "o", 3).start()

    chunk = 128
    locals_[1].wait()

    def small(row):
        return small_ref[row : row + 1, :]

    def norm(values):
        centred = values - jnp.mean(values, axis=-1, keepdims=True)
        inv = lax.rsqrt(jnp.mean(centred * centred, axis=-1, keepdims=True) + EPS)
        return centred * inv, inv

    def at_chunk(step):
        return pl.ds(pl.multiple_of(step * chunk, chunk), chunk)

    def first_norm(step, carry):
        where = at_chunk(step)
        hat, _ = norm(x_ref[where, :].astype(F32))
        a1_ref[where, :] = (small(0) * hat + small(1)).astype(BF16)
        return carry

    lax.fori_loop(0, tokens // chunk, first_norm, 0)

    lane = lax.broadcasted_iota(jnp.int32, (seq, 128), 1)
    for row in range(rows):
        ids = jnp.broadcast_to(seg_ref[row : row + 1, :].astype(F32), (128, seq)).T
        spot = lane % 64
        same = spot == ids.astype(jnp.int32)
        inside = spot < 32
        where = pl.ds(row * seq, seq)
        aug_q[where, :] = jnp.where(same, 1.0, 0.0).astype(BF16)
        aug_k[where, :] = jnp.where(jnp.logical_and(inside, jnp.logical_not(same)), MASKED, 0.0).astype(BF16)

    even = lane < 64

    def pick(values, others):
        return jnp.where(even, values, others), jnp.where(even, others, values)

    def attend_forward(step):
        xx, t = jnp.where(step < 3, x, nx), step % 3
        weights = wq[xx, t].reshape(3 * 128, width)
        biasq = wb[xx, 0, 1:2, :].astype(F32) + wb[xx, 1, 1:2, :].astype(F32)
        biasv = wb[xx, 0, 2:3, :].astype(F32) + wb[xx, 1, 2:3, :].astype(F32)
        pq = jnp.where(t == 0, biasq[:, :128], jnp.where(t == 1, biasq[:, 128:256], biasq[:, 256:384]))
        pv = jnp.where(t == 0, biasv[:, :128], jnp.where(t == 1, biasv[:, 128:256], biasv[:, 256:384]))
        for row in range(rows):
            where = pl.ds(row * seq, seq)
            value = dot(a1_ref[where, :], weights, 1, 1)
            proj_ref[xx, t, where, 0:128] = ((value[:, :128] + pq).astype(BF16) * 0.125).astype(BF16)
            proj_ref[xx, t, where, 128:256] = value[:, 128:256].astype(BF16)
            proj_ref[xx, t, where, 256:384] = (value[:, 256:] + pv).astype(BF16)
        group = xx * 3 + t
        for row in range(rows):
            where = pl.ds(row * seq, seq)
            qs = pick(proj_ref[xx, t, where, 0:128], aug_q[where, :])
            ks = pick(proj_ref[xx, t, where, 128:256], aug_k[where, :])
            vs = pick(proj_ref[xx, t, where, 256:384], jnp.ones((seq, 128), BF16))
            highest, result = [], []
            for q, k, v in zip(qs, ks, vs):
                scores = dot(q, k, 1, 1)
                top = jnp.max(scores, axis=-1, keepdims=True)
                highest.append(top)
                result.append(dot(jnp.exp(scores - top).astype(BF16), v, 1, 0))
            total = pltpu.roll(jnp.where(even, result[1], result[0]), 64, 1)
            mixed = jnp.where(even, result[0], result[1]) / total
            o_ref[where, pl.ds(pl.multiple_of(group * 128, 128), 128)] = mixed.astype(BF16)
            log_total = jnp.where(even, highest[0], highest[1]) + jnp.log(total)
            lse_ref[where, :] = jnp.where(lane % 64 == group, log_total, lse_ref[where, :])

    lse_ref[...] = jnp.zeros_like(lse_ref)

    def forward_step(step, carry):
        @pl.when(step == 0)
        def _():
            biases[0].wait_recv()

        @pl.when(step == 3)
        def _():
            biases[1].wait_recv()
            biases[2].wait_recv()

        pl.when(jnp.logical_and(step >= 1, step < 5))(lambda: pass_x(step - 1))
        pl.when(step >= 2)(lambda: pass_z(step - 2))
        pl.when(step >= 3)(lambda: pass_y(step - 3))
        pl.when(step >= 3)(lambda: pass_done(step - 3))
        pl.when(step < 3)(lambda: mate_done(step))
        attend_forward(step)

        @pl.when(step == 0)
        def _():
            locals_[4].wait()
            locals_[5].wait()
            for index in range(3):
                wm[x, c, index, pl.ds(0, UNIT), :] = up_stage[:, index * UNIT : (index + 1) * UNIT].T
                to_mate(4 + index, "m", index).start()

        return carry

    lax.fori_loop(0, 6, forward_step, 0)
    pass_y(3)
    mate_done(3)
    pass_done(3)

    def second_norm(step, carry):
        where = pl.ds(pl.multiple_of(step * 256, 256), 256)
        value = x_ref[where, :].astype(F32) + dot(o_ref[where, :], wo[...].reshape(width, width), 1, 0) + small(2)
        hat, inv = norm(value)
        hat2_ref[where, :] = hat.astype(BF16)
        spot = lax.broadcasted_iota(jnp.int32, (256, 128), 1)
        lse_ref[where, :] = jnp.where(spot == INV_LANE, inv, lse_ref[where, :])
        a2_ref[where, :] = (small(3) * hat + small(4)).astype(BF16)
        x1_ref[where, :] = value + small(5)
        da2_ref[where, :] = jnp.zeros_like(value)
        return carry

    lax.fori_loop(0, tokens // 256, second_norm, 0)
    sums[...] = jnp.zeros_like(sums)
    locals_[6].wait()

    def pair_place(pair):
        far = sum(jnp.where(pair == p, 1, 0) for p, flag in enumerate(FAR_PAIRS) if flag)
        return jnp.where(far == 1, nx, x), pair // 2

    def expert_tile(step):
        xx, index = pair_place(step // 2)
        cc = jnp.where(step % 2 == 0, nc, c)
        w_up = wm[xx, cc, index, pl.ds(0, UNIT), :]
        w_down = wm[xx, cc, index, pl.ds(UNIT, UNIT), :]
        lanes = pl.ds(pl.multiple_of(index * UNIT, UNIT), UNIT)
        bias = wb[xx, cc, 0:1, lanes].astype(F32)
        upb_sum = None
        part_rows = tokens // SPLIT
        for part in range(SPLIT):
            where = pl.ds(part * part_rows, part_rows)
            pre = dot(a2_ref[where, :], w_up, 1, 1) + bias
            back = dot(g_ref[where, :], w_down, 1, 1)
            cumul, density = gelu_parts(pre)
            hidden = (pre * cumul).astype(BF16)
            low = (back * (cumul + pre * density)).astype(BF16)
            hid_ref[where, :] = hidden
            low_ref[where, :] = low
            one = column_sum(low.astype(F32))
            upb_sum = one if upb_sum is None else upb_sum + one
            x1_ref[where, :] += dot(hidden, w_down, 1, 0)
            da2_ref[where, :] += dot(low, w_up, 1, 0)
        sums[pl.ds(UPB + xx * 2 + cc, 1), lanes] = upb_sum
        base = pl.multiple_of(index * 2 * UNIT, UNIT)
        grad[xx, cc, pl.ds(base, UNIT), :] = dot(low_ref[...], a2_ref[...], 0, 0).astype(BF16)
        grad[xx, cc, pl.ds(base + UNIT, UNIT), :] = dot(hid_ref[...], g_ref[...], 0, 0).astype(BF16)

    def norm_back(grad_in, hat, inv, gain):
        scaled = grad_in * gain
        return inv * (
            scaled
            - jnp.mean(scaled, axis=-1, keepdims=True)
            - hat * jnp.mean(scaled * hat, axis=-1, keepdims=True)
        )

    def add_sum(row, values):
        sums[row : row + 1, :] += column_sum(values)

    heads_rows = 6 * UNIT

    def between():
        def one(step, carry):
            where = at_chunk(step)
            da2, hat = da2_ref[where, :], hat2_ref[where, :].astype(F32)
            top = g_ref[where, :].astype(F32)
            add_sum(GAIN2, da2 * hat)
            add_sum(SHIFT2, da2)
            add_sum(DOWNB, top)
            middle = top + norm_back(da2, hat, lse_ref[where, INV_LANE : INV_LANE + 1], small(3))
            da2_ref[where, :] = middle
            low = middle.astype(BF16)
            add_sum(OUTB, low.astype(F32))
            a2_ref[where, :] = low
            hat2_ref[where, :] = x1_ref[where, :].astype(BF16)
            return carry

        lax.fori_loop(0, tokens // chunk, one, 0)
        mixed_copy.start()
        for xx in range(2):
            half = dot(o_ref[:, xx * 384 : (xx + 1) * 384], a2_ref[...], 0, 0).astype(BF16)
            for t in range(3):
                for cc in range(2):
                    start = (t * 2 + cc) * 64
                    grad[xx, cc, pl.ds(heads_rows + t * 64, 64), :] = half[start : start + 64]

        def back(step, carry):
            where = pl.ds(pl.multiple_of(step * 256, 256), 256)
            a2_ref[where, :] = dot(a2_ref[where, :], wo[...].reshape(width, width), 1, 1).astype(BF16)
            return carry

        lax.fori_loop(0, tokens // 256, back, 0)

    def attend_backward(step):
        xx, t = jnp.where(step < 3, nx, x), step % 3
        group = xx * 3 + t
        lanes = pl.ds(pl.multiple_of(group * 128, 128), 128)

        def one_row(row, carry):
            where = pl.ds(pl.multiple_of(row * seq, seq), seq)
            query, key, value = (proj_ref[xx, t, where, i * 128 : (i + 1) * 128] for i in range(3))
            out, back = o_ref[where, lanes], a2_ref[where, lanes]
            none = jnp.zeros((seq, 128), BF16)
            product = out.astype(F32) * back.astype(F32)
            log_total = lse_ref[where, :]
            spot = lane % 64
            tops = [
                jnp.sum(jnp.where(lane == group + shift, log_total, 0.0), axis=-1, keepdims=True)
                for shift in (0, 64)
            ]
            deltas = [jnp.sum(item, axis=-1, keepdims=True) for item in pick(product, jnp.zeros_like(product))]
            q_aug, k_aug = pick(query, aug_q[where, :]), pick(key, aug_k[where, :])
            q_own, k_own, b_own = pick(query, none), pick(key, none), pick(back, none)
            v_aug = pick(value, jnp.where(spot < 3, 1.0, 0.0).astype(BF16))
            splits = []
            for delta in deltas:
                first = (-delta).astype(BF16).astype(F32)
                second = (-delta - first).astype(BF16).astype(F32)
                last = -delta - first - second
                splits.append(
                    jnp.where(spot == 0, first, jnp.where(spot == 1, second, jnp.where(spot == 2, last, 0.0)))
                )
            b_aug = (
                jnp.where(even, back, splits[0].astype(BF16)),
                jnp.where(even, splits[1].astype(BF16), back),
            )
            d_query = d_key = d_value = None
            for i in range(2):
                prob = jnp.exp(dot(q_aug[i], k_aug[i], 1, 1) - tops[i])
                low = prob.astype(BF16)
                inner = dot(b_aug[i], v_aug[i], 1, 1)
                d_score = (prob * inner).astype(BF16)
                parts = (dot(d_score, k_own[i], 1, 0), dot(d_score, q_own[i], 0, 0), dot(low, b_own[i], 0, 0))
                if i == 0:
                    d_query, d_key, d_value = parts
                else:
                    d_query, d_key, d_value = d_query + parts[0], d_key + parts[1], d_value + parts[2]
            low_query = (d_query * 0.125).astype(BF16)
            low_value = d_value.astype(BF16)
            proj_ref[xx, t, where, 0:128] = low_query
            proj_ref[xx, t, where, 128:256] = d_key.astype(BF16)
            proj_ref[xx, t, where, 256:384] = low_value
            sums[QUERYB : QUERYB + 1, lanes] += column_sum(low_query.astype(F32))
            sums[VALUEB : VALUEB + 1, lanes] += column_sum(low_value.astype(F32))
            return carry

        lax.fori_loop(0, rows, one_row, 0)
        whole = proj_ref[xx, t]
        weight_grad = dot(whole, a1_ref[...], 0, 0).astype(BF16)
        for part in range(3):
            for cc in range(2):
                start = part * 128 + cc * 64
                place = pl.multiple_of(heads_rows + 192 + t * 192 + part * 64, 64)
                grad[xx, cc, pl.ds(place, 64), :] = weight_grad[start : start + 64]
        part = dot(whole, wq[xx, t].reshape(3 * 128, width), 1, 0)

        @pl.when(step == 0)
        def _():
            x1_ref[...] = part

        @pl.when(step > 0)
        def _():
            x1_ref[...] += part

    def last_norm():
        def one(step, carry):
            where = at_chunk(step)
            hat, inv = norm(x_ref[where, :].astype(F32))
            da1 = x1_ref[where, :]
            add_sum(GAIN1, da1 * hat)
            add_sum(SHIFT1, da1)
            g_ref[where, :] = (da2_ref[where, :] + norm_back(da1, hat, inv, small(0))).astype(BF16)
            return carry

        lax.fori_loop(0, tokens // chunk, one, 0)
        input_copy.start()

    mixed_copy = pltpu.make_async_copy(hat2_ref, mixed_out, local_sem.at[7])
    input_copy = pltpu.make_async_copy(g_ref, input_out, local_sem.at[8])

    def add_into(xx, start, count, other, other_start):
        def one(step, carry):
            mine = pl.ds(pl.multiple_of(start + step * 32, 32), 32)
            theirs = pl.ds(pl.multiple_of(other_start + step * 32, 32), 32)
            grad[xx, c, mine, :] = (grad[xx, c, mine, :].astype(F32) + other[theirs, :].astype(F32)).astype(BF16)
            return carry

        lax.fori_loop(0, count // 32, one, 0)

    def pair_copy(xx, granule, start, count):
        return remote(
            grad.at[xx, nc, pl.ds(start, count)],
            mate_buf.at[granule % 2, pl.ds(0, count)],
            pair_s.at[granule], pair_r.at[granule], mate,
        )

    def x_copy(unit):
        where = pl.ds(pl.multiple_of(unit * UNIT, UNIT), UNIT)
        return remote(grad.at[nx, c, where], x_buf.at[where], ex_s.at[unit], ex_r.at[unit], x_peer)

    def granule_add(xx, granule, start, count):
        pair_copy(xx, granule, start, count).wait_recv()
        add_into(xx, start, count, mate_buf.at[granule % 2], 0)

    def tile_start(index):
        return pl.multiple_of(index * 2 * UNIT, 2 * UNIT)

    def pair_send(pair):
        xx, index = pair_place(pair)
        pair_copy(xx, pair, tile_start(index), 2 * UNIT).start()

    def pair_add(pair):
        xx, index = pair_place(pair)
        granule_add(xx, pair, tile_start(index), 2 * UNIT)

        @pl.when(xx == nx)
        def _():
            x_copy(2 * index).start()
            x_copy(2 * index + 1).start()

    def heads_start(number):
        return pl.multiple_of(heads_rows + number * UNIT, UNIT)

    def far_send(number):
        pair_copy(nx, 6 + number, heads_start(number), UNIT).start()

    def far_add(number):
        granule_add(nx, 6 + number, heads_start(number), UNIT)
        x_copy(6 + number).start()

    def near_send(number):
        pair_copy(x, 9 + number, heads_start(number), UNIT).start()

    def near_add(number):
        granule_add(x, 9 + number, heads_start(number), UNIT)

    half = UNIT // 2
    share = half // 4

    def y_copy(unit):
        return remote(
            grad.at[x, c, pl.ds(pl.multiple_of(unit * UNIT + ny * half, half), half)],
            y_buf.at[pl.ds(pl.multiple_of(unit * half, half), half)],
            ey_s.at[unit], ey_r.at[unit], y_peer,
        )

    def share_rows(unit, yy, zz):
        return pl.ds(pl.multiple_of(unit * UNIT + yy * half + zz * share, share), share)

    def z_copy(unit, step):
        return remote(
            grad.at[x, c, share_rows(unit, y, (z + step) % 4)],
            z_buf.at[unit, step - 1], ez_s.at[unit, step - 1], ez_r.at[unit, step - 1], z_peers[step - 1],
        )

    def back_z_copy(unit, step):
        where = share_rows(unit, y, z)
        return remote(
            x_buf.at[where], x_buf.at[where], fz_s.at[unit, step - 1], fz_r.at[unit, step - 1], z_peers[step - 1]
        )

    def back_y_copy(unit):
        where = pl.ds(pl.multiple_of(unit * UNIT + y * half, half), half)
        return remote(x_buf.at[where], x_buf.at[where], fy_s.at[unit], fy_r.at[unit], y_peer)

    def add_x(unit):
        x_copy(unit).wait_recv()
        start = pl.multiple_of(unit * UNIT, UNIT)
        add_into(x, start, UNIT, x_buf, start)
        y_copy(unit).start()

    def add_y(unit):
        y_copy(unit).wait_recv()
        add_into(x, pl.multiple_of(unit * UNIT + y * half, half), half, y_buf, pl.multiple_of(unit * half, half))
        for step in (1, 2, 3):
            z_copy(unit, step).start()

    def add_z(unit):
        for step in (1, 2, 3):
            z_copy(unit, step).wait_recv()
        where = share_rows(unit, y, z)
        total = grad[x, c, where, :].astype(F32)
        for step in range(3):
            total += z_buf[unit, step].astype(F32)
        x_buf[where, :] = total.astype(BF16)
        for step in (1, 2, 3):
            back_z_copy(unit, step).start()

    def give_y(unit):
        for step in (1, 2, 3):
            back_z_copy(unit, step).wait_recv()
        back_y_copy(unit).start()

    def out_copy(unit):
        where = pl.ds(pl.multiple_of(unit * UNIT, UNIT), UNIT)
        return pltpu.make_async_copy(x_buf.at[where], grads_out.at[where], local_sem.at[9 + unit])

    def finish(unit):
        back_y_copy(unit).wait_recv()
        out_copy(unit).start()

    def sums_copy(slot, source, peer):
        return remote(sums_recv.at[6 + source], sums_recv.at[slot], sums_s.at[slot], sums_r.at[slot], peer)

    small_peers = [(0, 0, mate), (1, 1, x_peer), (2, 2, y_peer)]

    def sums_step(number):
        @pl.when(number == 0)
        def _():
            sums_recv[6] = sums[...]
            sums_copy(*small_peers[0]).start()

        for index in (1, 2):
            @pl.when(number == index)
            def _(index=index):
                sums_copy(*small_peers[index - 1]).wait_recv()
                sums_recv[6 + index] = sums_recv[5 + index] + sums_recv[index - 1]
                sums_copy(*small_peers[index]).start()

        @pl.when(number == 3)
        def _():
            sums_copy(*small_peers[2]).wait_recv()
            sums_recv[9] = sums_recv[8] + sums_recv[2]
            for step in (1, 2, 3):
                sums_copy(2 + step, 3, z_peers[step - 1]).start()

        @pl.when(number == 4)
        def _():
            for step in (1, 2, 3):
                sums_copy(2 + step, 3, z_peers[step - 1]).wait_recv()
            total = None
            for zz in range(4):
                behind = (z - zz + 4) % 4
                value = jnp.where(
                    behind == 0,
                    sums_recv[9],
                    jnp.where(behind == 1, sums_recv[3], jnp.where(behind == 2, sums_recv[4], sums_recv[5])),
                )
                total = value if total is None else total + value
            sums_out[...] = total

    events = {
        "pair_add": pair_add, "far_add": far_add, "near_add": near_add,
        "pair_send": pair_send, "far_send": far_send, "near_send": near_send,
        "pass_x": pass_x, "pass_z": pass_z, "pass_y": pass_y, "pass_done": pass_done, "mate_done": mate_done,
        "add_x": add_x, "add_y": add_y, "add_z": add_z, "give_y": give_y, "finish": finish,
        "sums": sums_step,
    }

    def main_step(step, carry):
        for name, run in events.items():
            number = jnp.int32(-1)
            for at, which in WHEN[name].items():
                number = jnp.where(step == at, which, number)
            pl.when(number >= 0)(functools.partial(run, number))
        pl.when(step < BETWEEN)(lambda: expert_tile(step))
        pl.when(step == BETWEEN)(between)
        pl.when(jnp.logical_and(step >= FIRST_HEADS, step < LAST_NORM))(
            lambda: attend_backward(step - FIRST_HEADS)
        )
        pl.when(step == LAST_NORM)(last_norm)
        return carry

    lax.fori_loop(0, STEPS, main_step, 0)

    mixed_copy.wait()
    input_copy.wait()
    for copy in biases:
        copy.wait_send()

    def piece_sends(number):
        def run(kind, index):
            to_mate(number, kind, index).wait_send()
            to_x(number, kind, index).wait_send()
            on_z(number, kind, index, part_x).wait_send()
            on_y(number, kind, index, part_x).wait_send()
            forward(number, kind, index).wait_send()

        kinds(number, run)

    def last_waits(unit, carry):
        x_copy(unit).wait_send()
        y_copy(unit).wait_send()
        for step in (1, 2, 3):
            z_copy(unit, step).wait_send()
            back_z_copy(unit, step).wait_send()
        back_y_copy(unit).wait_send()
        out_copy(unit).wait()
        pl.when(unit < 7)(lambda: piece_sends(unit))
        @pl.when(unit < 6)
        def _():
            xx, index = pair_place(unit)
            pair_copy(xx, unit, tile_start(index), 2 * UNIT).wait_send()

        @pl.when(unit < 3)
        def _():
            pair_copy(nx, 6 + unit, heads_start(unit), UNIT).wait_send()
            pair_copy(x, 9 + unit, heads_start(unit), UNIT).wait_send()

        return carry

    lax.fori_loop(0, 9, last_waits, 0)
    for slot, source, peer in small_peers:
        sums_copy(slot, source, peer).wait_send()
    for step in (1, 2, 3):
        sums_copy(2 + step, 3, z_peers[step - 1]).wait_send()


def on_device(
    tokens, segment_ids, cotangent, norm1_gain, norm1_shift, w_qkv, qv_bias, w_out, out_bias,
    norm2_gain, norm2_shift, w_up, up_bias, w_down, down_bias,
):
    rows, seq, width = tokens.shape
    count = rows * seq
    me = lax.axis_index("mp")
    core = me % 2
    shard = w_up.shape[1]
    heads = w_out.shape[0] // HEAD
    tiles = shard // UNIT
    units = 2 * tiles + 3

    small = jnp.stack([norm1_gain, norm1_shift, out_bias, norm2_gain, norm2_shift, down_bias]).astype(F32)
    spread = jnp.zeros((2, heads, 2, HEAD), BF16)
    spread = lax.dynamic_update_slice(spread, qv_bias.reshape(2, heads, 1, HEAD), (0, 0, core, 0))
    spread = spread.reshape(2, heads * 2 * HEAD)
    bias = jnp.concatenate(
        [up_bias[None], jnp.pad(spread, ((0, 0), (0, width - spread.shape[1]))), jnp.zeros((13, width), BF16)]
    )
    qkv_rows = jnp.transpose(w_qkv, (1, 2, 0)).reshape(3, heads, HEAD, width).transpose(1, 0, 2, 3)

    any_space = pl.BlockSpec(memory_space=pl.ANY)
    vmem = pl.BlockSpec(memory_space=pltpu.VMEM)
    dma = pltpu.SemaphoreType.DMA
    vm = pltpu.VMEM
    mixed, input_grad, grads, sums = pl.pallas_call(
        functools.partial(kernel, rows=rows, seq=seq),
        out_shape=(
            jax.ShapeDtypeStruct((count, width), BF16),
            jax.ShapeDtypeStruct((count, width), BF16),
            jax.ShapeDtypeStruct((units * UNIT, width), BF16),
            jax.ShapeDtypeStruct((16, width), F32),
        ),
        in_specs=[any_space, any_space, vmem, vmem, any_space, any_space, any_space, any_space, any_space],
        out_specs=(any_space, any_space, any_space, vmem),
        scratch_shapes=[
            vm((2, heads, 3, 2, HEAD, width), BF16),
            vm((2, heads, 2, HEAD, width), BF16),
            vm((2, 2, tiles, 2 * UNIT, width), BF16),
            vm((2, 2, 16, width), BF16),
            vm((2, 2, units * UNIT, width), BF16),
            vm((2, 2 * UNIT, width), BF16),
            vm((units * UNIT, width), BF16),
            vm((units * UNIT // 2, width), BF16),
            vm((units, 3, UNIT // 8, width), BF16),
            vm((count, width), BF16),
            vm((count, width), BF16),
            vm((count, width), BF16),
            vm((2, heads, count, 3 * 128), BF16),
            vm((count, width), BF16),
            vm((count, width), F32),
            vm((count, width), BF16),
            vm((count, width), BF16),
            vm((count, width), F32),
            vm((count, UNIT), BF16),
            vm((count, UNIT), BF16),
            vm((count, 128), F32),
            vm((count, 128), BF16),
            vm((count, 128), BF16),
            vm((16, width), F32),
            vm((10, 16, width), F32),
            dma((9 + units,)),
            dma((7,)), dma((7,)), dma((7,)), dma((7,)), dma((7,)), dma((7,)),
            dma((7,)), dma((7,)), dma((7,)), dma((7,)), dma((3,)), dma((3,)),
            dma((12,)), dma((12,)),
            dma((units,)), dma((units,)), dma((units,)), dma((units,)),
            dma((units, 3)), dma((units, 3)), dma((units, 3)), dma((units, 3)),
            dma((units,)), dma((units,)), dma((6,)), dma((6,)),
        ],
        compiler_params=pltpu.CompilerParams(
            collective_id=0, has_side_effects=True, vmem_limit_bytes=64 * 2**20 - 2**16
        ),
    )(
        tokens.reshape(count, width), cotangent.reshape(count, width), segment_ids, small, bias,
        qkv_rows, w_out.reshape(heads, HEAD, width), w_up, w_down.reshape(tiles, UNIT, width),
    )

    groups = lax.axis_size("dp") // 8
    if groups > 1:
        grads, sums = lax.psum((grads.astype(F32) * 0.125, sums * 0.125), "dp")
    grads = grads.astype(F32)
    split = 2 * tiles * UNIT
    expert = grads[:split].reshape(tiles, 2, UNIT, width)
    grad_up = expert[:, 0].reshape(shard, width).T
    grad_down = expert[:, 1].reshape(shard, width)
    grad_out = grads[split : split + heads * HEAD]
    grad_qkv = grads[split + heads * HEAD :].reshape(heads, 3, HEAD, width)
    grad_qkv = grad_qkv.transpose(3, 1, 0, 2).reshape(width, 3, heads * HEAD)
    grad_qv = sums[QUERYB : VALUEB + 1].reshape(2, 2, heads, 2, HEAD)
    grad_qv = lax.dynamic_slice(grad_qv, (0, me // 2, 0, core, 0), (2, 1, heads, 1, HEAD)).reshape(2, heads * HEAD)
    grad_upb = lax.dynamic_slice(sums, (UPB + me, 0), (1, width))[0]
    return (
        mixed.reshape(rows, seq, width),
        input_grad.reshape(rows, seq, width),
        sums[GAIN1],
        sums[SHIFT1],
        grad_qkv,
        grad_qv,
        grad_out,
        sums[OUTB],
        sums[GAIN2],
        sums[SHIFT2],
        grad_up,
        grad_upb,
        grad_down,
        sums[DOWNB],
    )


def solution(mesh):
    tall = P(("dp", "mp"), None, None)
    return jax.shard_map(
        on_device,
        mesh=mesh,
        in_specs=(
            tall, P(("dp", "mp"), None), tall, P(), P(), P(None, None, "mp"), P(None, "mp"), P("mp", None),
            P(), P(), P(), P(None, "mp"), P("mp"), P("mp", None), P(),
        ),
        out_specs=(
            tall, tall, P(), P(), P(None, None, "mp"), P(None, "mp"), P("mp", None), P(), P(), P(),
            P(None, "mp"), P("mp"), P("mp", None), P(),
        ),
        check_vma=False,
    )
```

time: 573 us -> 225 us (0.39)
  waiting for transfers between devices: 198 us -> 0 us
  Pallas kernels: 0 us -> 196 us
  matrix products: 162 us -> 0 us
  other arithmetic: 90.3 us -> 1.29 us
  blocking collectives: 55.8 us -> 0 us
  local copies, waits for them, and re-layouts: 46.8 us -> 24.9 us
  between operations: 14.9 us -> 0.73 us
    pallas_call x0 -> x1, Pallas kernels: none -> 196 us  [on_device(): pl.pallas_call(functools.partial(kernel, rows=rows, seq=seq), out_shape=(...]
    dot_general x18 -> x0, matrix products: 162 us -> none  [the longest x4 38.5 us: flat_dot(): jnp.dot(left_side.reshape(-1, left_side.shape[-1]), right_side, preferred...]
    psum x1 -> x0, waiting for transfers between devices: 83.6 us -> none  [on_device(): lax.psum((spread(grad_qkv, 2), spread(grad_wout, 0), spread(grad_wup, 1),...]
    reduce_scatter x4 -> x0, waiting for transfers between devices: 78.1 us -> none  [spread(): lax.psum_scatter(value.astype(bf16), 'mp', scatter_dimension=axis, tiled=...]
    convert_element_type x15 -> x1, other arithmetic: 63.4 us -> 0.61 us  [on_device(): jnp.stack([norm1_gain, norm1_shift, out_bias, norm2_gain, norm2_shift, do...]
    psum x1 -> x0, blocking collectives: 44.2 us -> none  [on_device(): total = lax.psum(jnp.concatenate(parts), ('dp', 'mp'))]
    all_gather x4 -> x0, waiting for transfers between devices: 33.5 us -> none  [the longest x1 21.1 us: on_device(): down_all = lax.all_gather(w_down, 'mp', axis=0, tiled=True)]
    reduce_sum x7 -> x0, other arithmetic: 26.4 us -> none  [the longest x1 11.9 us: attention_forward(): jnp.sum(jnp.exp(scores - highest), axis=-1, keepdims=True)]
  transfers between devices with their start and end apart: 9 -> 0, of which waited for: 5 -> 0; matrix products, arithmetic and copies ran while one was open for 39% -> 0% of each run, Pallas kernels for 0% -> 0%
where the time goes in v2:
time: 225 us; the launch traced here: 223 us
  Pallas kernels  196 us (87%)
  local copies, waits for them, and re-layouts  24.9 us (11%)
    pallas_call x1, Pallas kernels, on_device(): pl.pallas_call(functools.partial(kernel, rows=rows, seq=seq), out_shape=(...  196 us
    unnamed x7, local copies, waits for them, and re-layouts  7.17 us

profile of v2, /device:TPU:0, one launch (start us, length us, event | category | flops | bytes accessed | tf_op | source)
XLA Modules:
  0.0 222.9 jit_solution(3006979825173074868)
XLA Ops:
  0.7 0.1 pad.7.clone
  0.8 0.7 stack.21
  1.4 0.7 stack.22
  2.1 0.8 reshape.84
  2.9 0.7 stack.23
  3.6 0.7 stack.24
  4.3 0.7 stack.25
  4.9 0.7 broadcast_in_dim.9
  5.6 0.7 stack.26
  6.4 0.1 reshape.73
  6.5 0.6 convert_element_type.8.small_ref
  7.1 0.7 fusion.3.bias_in
  7.8 2.1 copy.39
  9.9 196.0 %shard_map.254 = (bf16[1024,768]{1,0:T(8,128)(2,1)}, bf16[1024,768]{1,0:T(8,128)(2,1)}, bf16[2304,768]{1,0:T(8,128)(2,1)}, f32[16,768]{1,0:T(8,128)}) custom-call(bf16[1024,768]{1,0:T(8,128)(2,1)} %bitcast.31, bf16[1024,768]{1,0:T(8,128)(2,1)} %bitcast.32, s32[2,512]{1,0:T(2,128)} %seg_ref.1, f32[6,768]{1,0:T(8,128)} %convert_element_type.8.small_ref, ...), custom_call_target="tpu_custom_call" | custom-call | tf_op jit(solution)/shard_map/pallas_call | solution.py:744
  206.0 0.7 slice.39
  206.7 1.6 slice_reduce_fusion
  208.3 0.1 reshape.81
  208.5 0.7 reshape.82
  209.1 1.8 slice.49
  210.9 1.3 slice.48
  212.2 0.0 copy-start
  212.2 1.3 copy.34
  213.6 1.3 copy-done
  214.9 0.4 slice.50
  215.2 1.8 fusion.4
  217.1 1.9 copy.36
  219.0 0.0 copy-start.1
  219.0 2.8 %copy.43 = bf16[2,512,768]{2,1,0:T(8,128)(2,1)} copy(bf16[2,512,768]{2,1,0:T(8,128)(2,1)} %bitcast.30) | data formatting | bytes 3145728
  221.8 0.0 copy-done.1
  221.8 1.1 copy.44
  (5 shorter events, 0.1 us)
Async XLA Ops:
  212.2 2.6 %copy-start = (bf16[2304,768]{1,0:T(8,128)(2,1)S(1)}, bf16[2304,768]{1,0:T(8,128)(2,1)}, u32[]{:S(2)}) copy-start(bf16[2304,768]{1,0:T(8,128)(2,1)} %get-tuple-element.21) | copy-start | bytes 10616836
  219.0 2.8 %copy-start.1 = (bf16[1024,768]{1,0:T(8,128)(2,1)S(1)}, bf16[1024,768]{1,0:T(8,128)(2,1)}, u32[]{:S(2)}) copy-start(bf16[1024,768]{1,0:T(8,128)(2,1)} %get-tuple-element.19) | copy-start | bytes 4718596

commit v3 on v2

v3 whole, which is shorter than its diff:
```python
import functools

import jax
import jax.numpy as jnp
from jax import lax
from jax.experimental import pallas as pl
from jax.experimental.pallas import tpu as pltpu
from jax.sharding import PartitionSpec as P

HEAD = 64
EPS = 1e-06
MASKED = -1e30
UNIT = 256
SPLIT = 2
INV_LANE = 32
OWN_UP, OWN_QV = 12, 13
F32, BF16 = jnp.float32, jnp.bfloat16

GAIN1, SHIFT1, OUTB, GAIN2, SHIFT2, DOWNB, QUERYB, VALUEB, UPB = range(9)

FAR_PAIRS = (0, 1, 0, 1, 0, 1)
PAIR_TILES = (0, 0, 1, 1, 2, 2)
BETWEEN, FIRST_HEADS, LAST_NORM = 12, 15, 33
PLAN_FORWARD = (
    (("mate_done", 0), ("bias_done", 0),),
    (("pass_x", 0), ("pass_x", 1), ("mate_done", 1),),
    (("mate_done", 2),),
    (("pass_x", 2), ("pass_x", 3), ("pass_z", 0), ("pass_z", 1), ("pass_y", 0), ("pass_done", 0), ("bias_done", 1), ("bias_done", 2),),
    (("pass_x", 4), ("pass_z", 2), ("pass_z", 3), ("pass_y", 1), ("pass_done", 1),),
    (("pass_x", 5), ("pass_y", 2), ("pass_done", 2),),
)
PLAN_SECOND = (("pass_x", 6), ("pass_z", 4), ("pass_y", 3), ("mate_done", 3), ("pass_done", 3), )
PLAN_MAIN = (
    (("pass_z", 5), ("mate_done", 4),),
    (("pass_z", 6), ("pass_y", 4), ("pair_send", 0),),
    (("pass_y", 5), ("pass_done", 4),),
    (("pair_add", 0), ("pair_send", 1),),
    (("pass_y", 6), ("pair_add", 1), ("mate_done", 5),),
    (("pair_send", 2),),
    (("pair_add", 2), ("pass_done", 5),),
    (("pair_send", 3), ("add_x", 0),),
    (("pair_add", 3), ("mate_done", 6),),
    (("pair_send", 4), ("add_x", 1), ("add_y", 0),),
    (("pair_add", 4), ("add_z", 0), ("pass_done", 6),),
    (("pair_send", 5), ("add_x", 2), ("add_y", 1),),
    (("pair_add", 5), ("add_z", 1), ("add_far", 0),),
    (("add_y", 2),),
    (("add_x", 3),),
    (("add_far", 1), ("give_y", 0),),
    (("add_z", 2),),
    (("add_y", 3), ("give_y", 1),),
    (("far_send", 0), ("add_x", 4),),
    (("far_add", 0), ("add_z", 3), ("add_far", 2), ("finish", 0),),
    (),
    (("far_send", 1), ("add_x", 5), ("finish", 1),),
    (("far_add", 1), ("add_far", 3), ("add_y", 4), ("give_y", 2),),
    (),
    (("far_send", 2), ("add_y", 5), ("give_y", 3),),
    (("far_add", 2), ("add_z", 4),),
    (("add_z", 5), ("finish", 2),),
    (("near_send", 0),),
    (("near_add", 0), ("add_x", 6), ("add_far", 4), ("finish", 3),),
    (),
    (("near_send", 1), ("add_far", 5), ("give_y", 4),),
    (("near_add", 1), ("add_x", 7), ("add_y", 6),),
    (("give_y", 5),),
    (("near_send", 2), ("add_z", 6), ("finish", 4),),
)
PLAN_DRAIN = (
    ("near_add", 2),
    ("add_x", 8),
    ("sums", 0),
    ("add_y", 7),
    ("sums", 1),
    ("add_far", 6),
    ("add_z", 7),
    ("finish", 5),
    ("sums", 2),
    ("give_y", 6),
    ("sums", 3),
    ("add_y", 8),
    ("sums", 4),
    ("add_far", 7),
    ("add_z", 8),
    ("sums", 5),
    ("finish", 6),
    ("give_y", 7),
    ("add_far", 8),
    ("finish", 7),
    ("give_y", 8),
    ("finish", 8),
)

def dot(left, right, left_dim, right_dim):
    return lax.dot_general(
        left, right, (((left_dim,), (right_dim,)), ((), ())), preferred_element_type=F32
    )


def column_sum(values):
    return jnp.sum(values, axis=0, keepdims=True)


def gelu_parts(pre):
    size = jnp.abs(pre) * 0.7071067811865476
    base = 1.0 + 0.3275911 * size
    part = pl.reciprocal(base, approx=True)
    part = part * (2.0 - base * part)
    tail = jnp.exp(-0.5 * pre * pre)
    poly = part * (
        0.254829592
        + part * (-0.284496736 + part * (1.421413741 + part * (-1.453152027 + part * 1.061405429)))
    )
    half = 0.5 * poly * tail
    return jnp.where(pre >= 0, 1.0 - half, half), tail * 0.3989422804014327


def kernel(
    x_in, g_in, seg_in, gain1_in, shift1_in, outb_in, gain2_in, shift2_in, downb_in, upb_in, qvb_in,
    qkv_in, out_in, up_in, down_in,
    mixed_out, input_out, grads_out, sums_out,
    wq, wo, wm, wb, grad, mate_buf, x_buf, y_buf, z_buf,
    x_ref, g_ref, a1_ref, proj_ref, o_ref, x1_ref, hat2_ref, a2_ref, da2_ref,
    hid_ref, low_ref, lse_ref, aug_q, aug_k, sums, sums_recv,
    seg_ref, gain1_ref, shift1_ref, outb_ref, gain2_ref, shift2_ref, downb_ref, upb_ref, qvb_ref, small_sem,
    local_sem, wm_s, wm_r, wx_s, wx_r, wy_s, wy_r, wz_s, wz_r, wf_s, wf_r, wb_s, wb_r,
    pair_s, pair_r, ex_s, ex_r, ey_s, ey_r, ez_s, ez_r, ew_s, ew_r, fz_s, fz_r, fy_s, fy_r, sums_s, sums_r,
    *, rows, seq,
):
    tokens, width = x_ref.shape
    dp, mp = lax.axis_index("dp"), lax.axis_index("mp")
    c, x = mp % 2, mp // 2
    y, z = dp % 2, (dp // 2) % 4
    block = dp - dp % 8
    zb = z % 2
    nx, nc, ny = 1 - x, 1 - c, 1 - y

    def device(zz, yy, xx, cc):
        return (block + zz * 2 + yy, xx * 2 + cc)

    mate = device(z, y, x, nc)
    x_peer = device(z, y, nx, c)
    y_peer = device(z, ny, x, c)
    z_far = device((z + 2) % 4, y, x, c)
    z_pair = device(z + 1 - 2 * zb, y, x, c)
    cross = device(z, y, nx, nc)

    def remote(src, dst, send, recv, where):
        return pltpu.make_async_remote_copy(
            src_ref=src, dst_ref=dst, send_sem=send, recv_sem=recv,
            device_id=where, device_id_type=pl.DeviceIdType.MESH,
        )

    barrier = pltpu.get_barrier_semaphore()
    everyone = [mate, x_peer, cross, y_peer, z_pair, z_far]
    for peer in everyone:
        pl.semaphore_signal(barrier, inc=1, device_id=peer, device_id_type=pl.DeviceIdType.MESH)

    up_stage = grad.at[0, 0, pl.ds(0, width)]
    locals_ = [
        pltpu.make_async_copy(qkv_in.at[:, 0], wq.at[x, 0, :, c], local_sem.at[0]),
        pltpu.make_async_copy(qkv_in.at[:, 1], wq.at[x, 1, :, c], local_sem.at[1]),
        pltpu.make_async_copy(qkv_in.at[:, 2], wq.at[x, 2, :, c], local_sem.at[2]),
        pltpu.make_async_copy(x_in, x_ref, local_sem.at[3]),
        pltpu.make_async_copy(out_in, wo.at[x, :, c], local_sem.at[4]),
        pltpu.make_async_copy(up_in, up_stage, local_sem.at[5]),
        pltpu.make_async_copy(down_in, wm.at[x, c, :, pl.ds(UNIT, UNIT)], local_sem.at[6]),
        pltpu.make_async_copy(g_in, g_ref, local_sem.at[7]),
    ]
    small_copies = [
        pltpu.make_async_copy(src, dst, small_sem.at[i])
        for i, (src, dst) in enumerate((
            (seg_in, seg_ref), (upb_in, upb_ref), (qvb_in, qvb_ref), (gain1_in, gain1_ref), (shift1_in, shift1_ref),
            (outb_in, outb_ref), (gain2_in, gain2_ref), (shift2_in, shift2_ref), (downb_in, downb_ref),
        ))
    ]
    for copy in small_copies + locals_:
        copy.start()
    for copy in small_copies:
        copy.wait()

    from_lane = lax.broadcasted_iota(jnp.int32, (qvb_ref.shape[1], 384), 0)
    to_lane = lax.broadcasted_iota(jnp.int32, (qvb_ref.shape[1], 384), 1)
    placed = jnp.logical_and(
        from_lane == (to_lane // 128) * 64 + to_lane % 64, (to_lane // 64) % 2 == c
    )
    place = jnp.where(placed, 1.0, 0.0).astype(BF16)
    qv_rows = dot(qvb_ref[...], place, 1, 0)
    qv_rows = jnp.concatenate([qv_rows, jnp.zeros((2, width - 384), F32)], axis=1)
    tile_row = lax.broadcasted_iota(jnp.int32, (16, width), 0)
    wb[x, c] = jnp.where(
        tile_row == 0,
        upb_ref[...].astype(F32).reshape(1, width),
        jnp.where(tile_row == 1, qv_rows[0:1], jnp.where(tile_row == 2, qv_rows[1:2], 0.0)),
    ).astype(BF16)
    lane = lax.broadcasted_iota(jnp.int32, (seq, 128), 1)
    for row in range(rows):
        ids = jnp.broadcast_to(seg_ref[row : row + 1, :].astype(F32), (128, seq)).T
        spot = lane % 64
        same = spot == ids.astype(jnp.int32)
        inside = spot < 32
        where = pl.ds(row * seq, seq)
        aug_q[where, :] = jnp.where(same, 1.0, 0.0).astype(BF16)
        aug_k[where, :] = jnp.where(jnp.logical_and(inside, jnp.logical_not(same)), MASKED, 0.0).astype(BF16)
    lse_ref[...] = jnp.zeros_like(lse_ref)
    locals_[5].wait()
    locals_[6].wait()
    tiles = up_stage.shape[1] // UNIT
    for index in range(tiles):
        wm[x, c, index, pl.ds(0, UNIT), :] = up_stage[:, index * UNIT : (index + 1) * UNIT].T
    for number in (0, 1, 2, 4):
        locals_[number].wait()
    pl.semaphore_wait(barrier, len(everyone))

    third = width // 3

    def piece(kind, index, xx, cc, lanes=slice(None)):
        if kind == "q":
            return wq.at[xx, index, :, cc, :, lanes]
        if kind == "o":
            return wo.at[xx, :, cc, :, lanes]
        return wm.at[xx, cc, index, :, lanes]

    def lanes_of(part):
        return pl.ds(pl.multiple_of(part * third, third), third)

    part_x = jnp.where(zb == 1, 2, y)
    part_z = jnp.where(zb == 1, y, 2)

    def kinds(number, run):
        if isinstance(number, int):
            run("q" if number < 3 else "o" if number == 3 else "m", number - 4 if number > 3 else number)
            return
        pl.when(number < 3)(lambda: run("q", number))
        pl.when(number == 3)(lambda: run("o", number))
        pl.when(number > 3)(lambda: run("m", number - 4))

    def to_mate(number, kind, index):
        own = piece(kind, index, x, c)
        return remote(own, own, wm_s.at[number], wm_r.at[number], mate)

    def to_x(number, kind, index):
        own = piece(kind, index, x, c, lanes_of(part_x))
        return remote(own, own, wx_s.at[number], wx_r.at[number], x_peer)

    def on_z(number, kind, index, part):
        held = piece(kind, index, nx, c, lanes_of(part))
        return remote(held, held, wz_s.at[number], wz_r.at[number], z_pair)

    def on_y(number, kind, index, part):
        held = piece(kind, index, nx, c, lanes_of(part))
        return remote(held, held, wy_s.at[number], wy_r.at[number], y_peer)

    def forward(number, kind, index):
        held = piece(kind, index, nx, c)
        return remote(held, held, wf_s.at[number], wf_r.at[number], mate)

    def mate_done(number):
        kinds(number, lambda kind, index: to_mate(number, kind, index).wait_recv())

    def start_x(number):
        kinds(number, lambda kind, index: to_x(number, kind, index).start())

    def pass_x(number):
        def run(kind, index):
            to_x(number, kind, index).wait_recv()
            on_z(number, kind, index, part_x).start()
            pl.when(zb == 0)(lambda: on_y(number, kind, index, part_x).start())

        kinds(number, run)
        if number < 5:
            start_x(number + 2)

    def pass_z(number):
        def run(kind, index):
            on_z(number, kind, index, part_x).wait_recv()
            pl.when(zb == 1)(lambda: on_y(number, kind, index, part_z).start())

        kinds(number, run)

    def pass_y(number):
        def run(kind, index):
            on_y(number, kind, index, part_x).wait_recv()
            forward(number, kind, index).start()

        kinds(number, run)

    def bias_done(number):
        biases[number].wait_recv()

    def pass_done(number):
        kinds(number, lambda kind, index: forward(number, kind, index).wait_recv())

    biases = [
        remote(wb.at[x, c], wb.at[x, c], wb_s.at[i], wb_r.at[i], peer)
        for i, peer in enumerate((mate, x_peer, cross))
    ]
    for number in range(2):
        start_x(number)
        to_mate(number, "q", number).start()
    for copy in biases:
        copy.start()
    to_mate(2, "q", 2).start()
    to_mate(3, "o", 3).start()
    for index in range(tiles):
        to_mate(4 + index, "m", index).start()

    chunk = 128
    locals_[3].wait()
    small_refs = (gain1_ref, shift1_ref, outb_ref, gain2_ref, shift2_ref, downb_ref)

    def small(row):
        return small_refs[row][...].astype(F32).reshape(1, width)

    def norm(values):
        centred = values - jnp.mean(values, axis=-1, keepdims=True)
        inv = lax.rsqrt(jnp.mean(centred * centred, axis=-1, keepdims=True) + EPS)
        return centred * inv, inv

    def at_chunk(step):
        return pl.ds(pl.multiple_of(step * chunk, chunk), chunk)

    def first_norm(step, carry):
        where = at_chunk(step)
        hat, _ = norm(x_ref[where, :].astype(F32))
        a1_ref[where, :] = (small(0) * hat + small(1)).astype(BF16)
        return carry

    even = lane < 64

    def pick(values, others):
        return jnp.where(even, values, others), jnp.where(even, others, values)

    def attend_forward(step):
        xx, t = jnp.where(step < 3, x, nx), step % 3
        weights = wq[xx, t].reshape(3 * 128, width)
        biasq = wb[xx, 0, 1:2, :].astype(F32) + wb[xx, 1, 1:2, :].astype(F32)
        biasv = wb[xx, 0, 2:3, :].astype(F32) + wb[xx, 1, 2:3, :].astype(F32)
        pq = jnp.where(t == 0, biasq[:, :128], jnp.where(t == 1, biasq[:, 128:256], biasq[:, 256:384]))
        pv = jnp.where(t == 0, biasv[:, :128], jnp.where(t == 1, biasv[:, 128:256], biasv[:, 256:384]))
        for row in range(rows):
            where = pl.ds(row * seq, seq)
            value = dot(a1_ref[where, :], weights, 1, 1)
            proj_ref[xx, t, where, 0:128] = ((value[:, :128] + pq).astype(BF16) * 0.125).astype(BF16)
            proj_ref[xx, t, where, 128:256] = value[:, 128:256].astype(BF16)
            proj_ref[xx, t, where, 256:384] = (value[:, 256:] + pv).astype(BF16)
        group = xx * 3 + t
        for row in range(rows):
            where = pl.ds(row * seq, seq)
            qs = pick(proj_ref[xx, t, where, 0:128], aug_q[where, :])
            ks = pick(proj_ref[xx, t, where, 128:256], aug_k[where, :])
            vs = pick(proj_ref[xx, t, where, 256:384], jnp.ones((seq, 128), BF16))
            highest, result = [], []
            for q, k, v in zip(qs, ks, vs):
                scores = dot(q, k, 1, 1)
                top = jnp.max(scores, axis=-1, keepdims=True)
                highest.append(top)
                result.append(dot(jnp.exp(scores - top).astype(BF16), v, 1, 0))
            total = pltpu.roll(jnp.where(even, result[1], result[0]), 64, 1)
            mixed = jnp.where(even, result[0], result[1]) / total
            o_ref[where, pl.ds(pl.multiple_of(group * 128, 128), 128)] = mixed.astype(BF16)
            log_total = jnp.where(even, highest[0], highest[1]) + jnp.log(total)
            lse_ref[where, :] = jnp.where(lane % 64 == group, log_total, lse_ref[where, :])

    def second_norm(step, carry):
        where = pl.ds(pl.multiple_of(step * 256, 256), 256)
        value = x_ref[where, :].astype(F32) + dot(o_ref[where, :], wo[...].reshape(width, width), 1, 0) + small(2)
        hat, inv = norm(value)
        hat2_ref[where, :] = hat.astype(BF16)
        spot = lax.broadcasted_iota(jnp.int32, (256, 128), 1)
        lse_ref[where, :] = jnp.where(spot == INV_LANE, inv, lse_ref[where, :])
        a2_ref[where, :] = (small(3) * hat + small(4)).astype(BF16)
        x1_ref[where, :] = value + small(5)
        da2_ref[where, :] = jnp.zeros_like(value)
        return carry

    def pair_place(pair):
        if isinstance(pair, int):
            return (nx if FAR_PAIRS[pair] else x), PAIR_TILES[pair]
        far = sum(jnp.where(pair == p, 1, 0) for p, flag in enumerate(FAR_PAIRS) if flag)
        tile = sum(jnp.where(pair == p, index, 0) for p, index in enumerate(PAIR_TILES))
        return jnp.where(far == 1, nx, x), tile

    def multiple(value, of):
        return value if isinstance(value, int) else pl.multiple_of(value, of)

    def expert_tile(step):
        xx, index = pair_place(step // 2)
        cc = jnp.where(step % 2 == 0, nc, c)
        w_up = wm[xx, cc, index, pl.ds(0, UNIT), :]
        w_down = wm[xx, cc, index, pl.ds(UNIT, UNIT), :]
        lanes = pl.ds(pl.multiple_of(index * UNIT, UNIT), UNIT)
        bias = wb[xx, cc, 0:1, lanes].astype(F32)
        upb_sum = None
        part_rows = tokens // SPLIT
        for part in range(SPLIT):
            where = pl.ds(part * part_rows, part_rows)
            pre = dot(a2_ref[where, :], w_up, 1, 1) + bias
            back = dot(g_ref[where, :], w_down, 1, 1)
            cumul, density = gelu_parts(pre)
            hidden = (pre * cumul).astype(BF16)
            low = (back * (cumul + pre * density)).astype(BF16)
            hid_ref[where, :] = hidden
            low_ref[where, :] = low
            one = column_sum(low.astype(F32))
            upb_sum = one if upb_sum is None else upb_sum + one
            x1_ref[where, :] += dot(hidden, w_down, 1, 0)
            da2_ref[where, :] += dot(low, w_up, 1, 0)
        sums[pl.ds(UPB + xx * 2 + cc, 1), lanes] = upb_sum
        base = pl.multiple_of(index * 2 * UNIT, UNIT)
        grad[xx, cc, pl.ds(base, UNIT), :] = dot(low_ref[...], a2_ref[...], 0, 0).astype(BF16)
        grad[xx, cc, pl.ds(base + UNIT, UNIT), :] = dot(hid_ref[...], g_ref[...], 0, 0).astype(BF16)

    def norm_back(grad_in, hat, inv, gain):
        scaled = grad_in * gain
        return inv * (
            scaled
            - jnp.mean(scaled, axis=-1, keepdims=True)
            - hat * jnp.mean(scaled * hat, axis=-1, keepdims=True)
        )

    def add_sum(row, values):
        sums[row : row + 1, :] += column_sum(values)

    heads_rows = 6 * UNIT

    def between_norm():
        def one(step, carry):
            where = at_chunk(step)
            da2, hat = da2_ref[where, :], hat2_ref[where, :].astype(F32)
            top = g_ref[where, :].astype(F32)
            add_sum(GAIN2, da2 * hat)
            add_sum(SHIFT2, da2)
            add_sum(DOWNB, top)
            middle = top + norm_back(da2, hat, lse_ref[where, INV_LANE : INV_LANE + 1], small(3))
            da2_ref[where, :] = middle
            low = middle.astype(BF16)
            add_sum(OUTB, low.astype(F32))
            a2_ref[where, :] = low
            hat2_ref[where, :] = x1_ref[where, :].astype(BF16)
            return carry

        lax.fori_loop(0, tokens // chunk, one, 0)
        mixed_copy.start()

    def between_out():
        for xx in range(2):
            half = dot(o_ref[:, xx * 384 : (xx + 1) * 384], a2_ref[...], 0, 0).astype(BF16)
            for t in range(3):
                for cc in range(2):
                    start = (t * 2 + cc) * 64
                    grad[xx, cc, pl.ds(heads_rows + t * 64, 64), :] = half[start : start + 64]

    def between_back():
        def back(step, carry):
            where = pl.ds(pl.multiple_of(step * 256, 256), 256)
            a2_ref[where, :] = dot(a2_ref[where, :], wo[...].reshape(width, width), 1, 1).astype(BF16)
            return carry

        lax.fori_loop(0, tokens // 256, back, 0)

    def attend_backward(step):
        xx, t = jnp.where(step < 9, nx, x), (step // 3) % 3
        group = xx * 3 + t
        lanes = pl.ds(pl.multiple_of(group * 128, 128), 128)

        def one_row():
            where = pl.ds(pl.multiple_of((step % 3) * seq, seq), seq)
            query, key, value = (proj_ref[xx, t, where, i * 128 : (i + 1) * 128] for i in range(3))
            out, back = o_ref[where, lanes], a2_ref[where, lanes]
            none = jnp.zeros((seq, 128), BF16)
            product = out.astype(F32) * back.astype(F32)
            log_total = lse_ref[where, :]
            spot = lane % 64
            tops = [
                jnp.sum(jnp.where(lane == group + shift, log_total, 0.0), axis=-1, keepdims=True)
                for shift in (0, 64)
            ]
            deltas = [jnp.sum(item, axis=-1, keepdims=True) for item in pick(product, jnp.zeros_like(product))]
            q_aug, k_aug = pick(query, aug_q[where, :]), pick(key, aug_k[where, :])
            q_own, k_own, b_own = pick(query, none), pick(key, none), pick(back, none)
            v_aug = pick(value, jnp.where(spot < 3, 1.0, 0.0).astype(BF16))
            splits = []
            for delta in deltas:
                first = (-delta).astype(BF16).astype(F32)
                second = (-delta - first).astype(BF16).astype(F32)
                last = -delta - first - second
                splits.append(
                    jnp.where(spot == 0, first, jnp.where(spot == 1, second, jnp.where(spot == 2, last, 0.0)))
                )
            b_aug = (
                jnp.where(even, back, splits[0].astype(BF16)),
                jnp.where(even, splits[1].astype(BF16), back),
            )
            d_query = d_key = d_value = None
            for i in range(2):
                prob = jnp.exp(dot(q_aug[i], k_aug[i], 1, 1) - tops[i])
                low = prob.astype(BF16)
                inner = dot(b_aug[i], v_aug[i], 1, 1)
                d_score = (prob * inner).astype(BF16)
                parts = (dot(d_score, k_own[i], 1, 0), dot(d_score, q_own[i], 0, 0), dot(low, b_own[i], 0, 0))
                if i == 0:
                    d_query, d_key, d_value = parts
                else:
                    d_query, d_key, d_value = d_query + parts[0], d_key + parts[1], d_value + parts[2]
            low_query = (d_query * 0.125).astype(BF16)
            low_value = d_value.astype(BF16)
            proj_ref[xx, t, where, 0:128] = low_query
            proj_ref[xx, t, where, 128:256] = d_key.astype(BF16)
            proj_ref[xx, t, where, 256:384] = low_value
            sums[QUERYB : QUERYB + 1, lanes] += column_sum(low_query.astype(F32))
            sums[VALUEB : VALUEB + 1, lanes] += column_sum(low_value.astype(F32))

        def weights():
            whole = proj_ref[xx, t]
            weight_grad = dot(whole, a1_ref[...], 0, 0).astype(BF16)
            for part in range(3):
                for cc in range(2):
                    start = part * 128 + cc * 64
                    place = pl.multiple_of(heads_rows + 192 + t * 192 + part * 64, 64)
                    grad[xx, cc, pl.ds(place, 64), :] = weight_grad[start : start + 64]
            part = dot(whole, wq[xx, t].reshape(3 * 128, width), 1, 0)

            @pl.when(step == 2)
            def _():
                x1_ref[...] = part

            @pl.when(step > 2)
            def _():
                x1_ref[...] += part

        pl.when(step % 3 < 2)(one_row)
        pl.when(step % 3 == 2)(weights)

    def last_norm():
        def one(step, carry):
            where = at_chunk(step)
            hat, inv = norm(x_ref[where, :].astype(F32))
            da1 = x1_ref[where, :]
            add_sum(GAIN1, da1 * hat)
            add_sum(SHIFT1, da1)
            g_ref[where, :] = (da2_ref[where, :] + norm_back(da1, hat, inv, small(0))).astype(BF16)
            return carry

        lax.fori_loop(0, tokens // chunk, one, 0)
        input_copy.start()

    sums_out_copy = pltpu.make_async_copy(sums, sums_out, small_sem.at[9])
    mixed_copy = pltpu.make_async_copy(hat2_ref, mixed_out, local_sem.at[8])
    input_copy = pltpu.make_async_copy(g_ref, input_out, local_sem.at[9])

    def add_into(xx, start, count, other, other_start):
        def one(step, carry):
            mine = pl.ds(pl.multiple_of(start + step * 32, 32), 32)
            theirs = pl.ds(pl.multiple_of(other_start + step * 32, 32), 32)
            grad[xx, c, mine, :] = (grad[xx, c, mine, :].astype(F32) + other[theirs, :].astype(F32)).astype(BF16)
            return carry

        lax.fori_loop(0, count // 32, one, 0)

    def pair_copy(xx, granule, start, count):
        return remote(
            grad.at[xx, nc, pl.ds(start, count)],
            mate_buf.at[granule % 2, pl.ds(0, count)],
            pair_s.at[granule], pair_r.at[granule], mate,
        )

    def x_copy(unit):
        where = pl.ds(multiple(unit * UNIT, UNIT), UNIT)
        return remote(grad.at[nx, c, where], x_buf.at[where], ex_s.at[unit], ex_r.at[unit], x_peer)

    def granule_add(xx, granule, start, count):
        pair_copy(xx, granule, start, count).wait_recv()
        add_into(xx, start, count, mate_buf.at[granule % 2], 0)

    def tile_start(index):
        return multiple(index * 2 * UNIT, 2 * UNIT)

    def pair_send(pair):
        xx, index = pair_place(pair)
        pair_copy(xx, pair, tile_start(index), 2 * UNIT).start()

    def pair_add(pair):
        xx, index = pair_place(pair)
        granule_add(xx, pair, tile_start(index), 2 * UNIT)

        if FAR_PAIRS[pair]:
            x_copy(2 * index).start()
            x_copy(2 * index + 1).start()

    def heads_start(number):
        return multiple(heads_rows + number * UNIT, UNIT)

    def far_send(number):
        pair_copy(nx, 6 + number, heads_start(number), UNIT).start()

    def far_add(number):
        granule_add(nx, 6 + number, heads_start(number), UNIT)
        x_copy(6 + number).start()

    def near_send(number):
        pair_copy(x, 9 + number, heads_start(number), UNIT).start()

    def near_add(number):
        granule_add(x, 9 + number, heads_start(number), UNIT)

    half = UNIT // 2
    share = half // 2

    def y_copy(unit):
        return remote(
            grad.at[x, c, pl.ds(pl.multiple_of(unit * UNIT + ny * half, half), half)],
            y_buf.at[pl.ds(multiple(unit * half, half), half)],
            ey_s.at[unit], ey_r.at[unit], y_peer,
        )

    def share_rows(unit, part):
        return pl.ds(pl.multiple_of(unit * UNIT + y * half + part * share, share), share)

    def slot_rows(unit):
        return pl.ds(multiple(unit * share, share), share)

    def pair_z_copy(unit):
        return remote(
            grad.at[x, c, share_rows(unit, 1 - zb)], z_buf.at[0, slot_rows(unit)], ez_s.at[unit], ez_r.at[unit], z_pair
        )

    def far_z_copy(unit):
        return remote(
            grad.at[x, c, share_rows(unit, zb)], z_buf.at[1, slot_rows(unit)], ew_s.at[unit], ew_r.at[unit], z_far
        )

    def back_z_copy(unit):
        where = share_rows(unit, zb)
        return remote(x_buf.at[where], x_buf.at[where], fz_s.at[unit], fz_r.at[unit], z_pair)

    def back_y_copy(unit):
        where = pl.ds(pl.multiple_of(unit * UNIT + y * half, half), half)
        return remote(x_buf.at[where], x_buf.at[where], fy_s.at[unit], fy_r.at[unit], y_peer)

    def add_x(unit):
        x_copy(unit).wait_recv()
        start = multiple(unit * UNIT, UNIT)
        add_into(x, start, UNIT, x_buf, start)
        y_copy(unit).start()

    def add_y(unit):
        y_copy(unit).wait_recv()
        add_into(x, pl.multiple_of(unit * UNIT + y * half, half), half, y_buf, multiple(unit * half, half))
        pair_z_copy(unit).start()

    def add_z(unit):
        pair_z_copy(unit).wait_recv()
        start = pl.multiple_of(unit * UNIT + y * half + zb * share, share)
        add_into(x, start, share, z_buf.at[0], multiple(unit * share, share))
        far_z_copy(unit).start()

    def add_far(unit):
        far_z_copy(unit).wait_recv()
        where = share_rows(unit, zb)
        total = grad[x, c, where, :].astype(F32) + z_buf[1, slot_rows(unit), :].astype(F32)
        x_buf[where, :] = total.astype(BF16)
        back_z_copy(unit).start()

    def give_y(unit):
        back_z_copy(unit).wait_recv()
        back_y_copy(unit).start()

    def out_copy(unit):
        where = pl.ds(multiple(unit * UNIT, UNIT), UNIT)
        return pltpu.make_async_copy(x_buf.at[where], grads_out.at[where], local_sem.at[10 + unit])

    def finish(unit):
        back_y_copy(unit).wait_recv()
        out_copy(unit).start()

    def sums_copy(slot, source, peer):
        return remote(sums_recv.at[6 + source], sums_recv.at[slot], sums_s.at[slot], sums_r.at[slot], peer)

    small_peers = [(i, i, peer) for i, peer in enumerate((mate, x_peer, y_peer, z_pair, z_far))]

    def sums_step(number):
        if number > 0:
            sums_copy(*small_peers[number - 1]).wait_recv()
            sums_recv[6 + number] = sums_recv[5 + number] + sums_recv[number - 1]
        else:
            sums_recv[6] = sums[...]
        if number < 5:
            sums_copy(*small_peers[number]).start()
        else:
            total = sums_recv[11]
            sums[...] = total
            own_up = sums[pl.ds(UPB + mp, 1), :]
            pairs = jnp.where(x == 0, total[:, :384], total[:, 384:])
            spread = jnp.where(placed, 1.0, 0.0)
            own_qv = lax.dot_general(
                pairs, spread, (((1,), (1,)), ((), ())), precision=lax.Precision.HIGHEST, preferred_element_type=F32
            )
            own_qv = jnp.concatenate([own_qv, jnp.zeros((16, width - own_qv.shape[1]), F32)], axis=1)
            total = jnp.where(tile_row == OWN_UP, own_up, total)
            total = jnp.where(tile_row == OWN_QV, own_qv[QUERYB : QUERYB + 1], total)
            sums[...] = jnp.where(tile_row == OWN_QV + 1, own_qv[VALUEB : VALUEB + 1], total)
            sums_out_copy.start()

    events = {
        "pair_add": pair_add, "far_add": far_add, "near_add": near_add,
        "pair_send": pair_send, "far_send": far_send, "near_send": near_send,
        "bias_done": bias_done, "pass_x": pass_x, "pass_z": pass_z, "pass_y": pass_y, "pass_done": pass_done, "mate_done": mate_done,
        "add_x": add_x, "add_y": add_y, "add_z": add_z, "add_far": add_far, "give_y": give_y, "finish": finish,
        "sums": sums_step,
    }

    def run_due(due):
        for name, number in due:
            events[name](number)

    def due_now(step, plan):
        for at, due in enumerate(plan):
            if due:
                pl.when(step == at)(lambda due=due: run_due(due))

    lax.fori_loop(0, tokens // chunk, first_norm, 0)

    def forward_step(step, carry):
        due_now(step, PLAN_FORWARD)
        attend_forward(step)

        return carry

    lax.fori_loop(0, 6, forward_step, 0)
    run_due(PLAN_SECOND)
    lax.fori_loop(0, tokens // 256, second_norm, 0)
    sums[...] = jnp.zeros_like(sums)
    locals_[7].wait()

    def main_step(step, carry):
        due_now(step, PLAN_MAIN)
        pl.when(step < BETWEEN)(lambda: expert_tile(step))
        pl.when(step == BETWEEN)(between_norm)
        pl.when(step == BETWEEN + 1)(between_out)
        pl.when(step == BETWEEN + 2)(between_back)
        pl.when(jnp.logical_and(step >= FIRST_HEADS, step < LAST_NORM))(
            lambda: attend_backward(step - FIRST_HEADS)
        )
        pl.when(step == LAST_NORM)(last_norm)
        return carry

    lax.fori_loop(0, LAST_NORM + 1, main_step, 0)
    run_due(PLAN_DRAIN)

    mixed_copy.wait()
    input_copy.wait()
    sums_out_copy.wait()
    for copy in biases:
        copy.wait_send()

    def piece_sends(number):
        def run(kind, index):
            to_mate(number, kind, index).wait_send()
            to_x(number, kind, index).wait_send()
            on_z(number, kind, index, part_x).wait_send()
            on_y(number, kind, index, part_x).wait_send()
            forward(number, kind, index).wait_send()

        kinds(number, run)

    def last_waits(unit, carry):
        x_copy(unit).wait_send()
        y_copy(unit).wait_send()
        pair_z_copy(unit).wait_send()
        far_z_copy(unit).wait_send()
        back_z_copy(unit).wait_send()
        back_y_copy(unit).wait_send()
        out_copy(unit).wait()
        pl.when(unit < 7)(lambda: piece_sends(unit))
        @pl.when(unit < 6)
        def _():
            xx, index = pair_place(unit)
            pair_copy(xx, unit, tile_start(index), 2 * UNIT).wait_send()

        @pl.when(unit < 3)
        def _():
            pair_copy(nx, 6 + unit, heads_start(unit), UNIT).wait_send()
            pair_copy(x, 9 + unit, heads_start(unit), UNIT).wait_send()

        return carry

    lax.fori_loop(0, 9, last_waits, 0)
    for slot, source, peer in small_peers:
        sums_copy(slot, source, peer).wait_send()


def tail_kernel(
    mixed_in, input_in, grads_in, sums_in,
    mixed_out, input_out, qkv_out, wout_out, up_out, down_out,
    qv_out, gain1_out, shift1_out, outb_out, gain2_out, shift2_out, downb_out, upb_out,
    mixed, inputs, grads, qkv, wout, up, down, sums_ref, qv_ref, in_sem, out_sem, small_sem, *vectors,
):
    tiles = down.shape[0]
    heads = qkv.shape[1]
    copies = [
        pltpu.make_async_copy(mixed_in, mixed, in_sem.at[0]),
        pltpu.make_async_copy(input_in, inputs, in_sem.at[1]),
    ]
    loads = []
    for index in range(tiles + 1):
        rows = pl.ds(index * 2 * UNIT, 2 * UNIT if index < tiles else 3 * UNIT)
        loads.append(pltpu.make_async_copy(grads_in.at[rows], grads.at[rows], in_sem.at[2 + index]))
    sums_copy = pltpu.make_async_copy(sums_in, sums_ref, small_sem.at[8])
    for copy in copies + loads + [sums_copy]:
        copy.start()
    stores = [
        pltpu.make_async_copy(mixed, mixed_out, out_sem.at[2 * tiles + 2]),
        pltpu.make_async_copy(inputs, input_out, out_sem.at[2 * tiles + 3]),
    ]
    for copy, store in zip(copies, stores):
        copy.wait()
        store.start()
    for index in range(tiles):
        loads[index].wait()
        start = index * 2 * UNIT
        down[index] = grads[start + UNIT : start + 2 * UNIT, :].astype(F32)
        stores.append(pltpu.make_async_copy(down.at[index], down_out.at[index], out_sem.at[2 * index]))
        stores[-1].start()
        lanes = pl.ds(index * UNIT, UNIT)
        up[:, lanes] = grads[start : start + UNIT, :].astype(F32).T
        stores.append(pltpu.make_async_copy(up.at[:, lanes], up_out.at[:, lanes], out_sem.at[2 * index + 1]))
        stores[-1].start()
    loads[tiles].wait()
    start = 2 * tiles * UNIT
    wout[...] = grads[start : start + heads * HEAD, :].astype(F32)
    stores.append(pltpu.make_async_copy(wout, wout_out, out_sem.at[2 * tiles]))
    stores[-1].start()
    start += heads * HEAD
    for head in range(heads):
        for part in range(3):
            row = start + (head * 3 + part) * HEAD
            qkv[part, head] = grads[row : row + HEAD, :].astype(F32)
    stores.append(pltpu.make_async_copy(qkv, qkv_out, out_sem.at[2 * tiles + 1]))
    stores[-1].start()
    sums_copy.wait()
    for index, (row, out) in enumerate((
        (GAIN1, gain1_out), (SHIFT1, shift1_out), (OUTB, outb_out), (GAIN2, gain2_out), (SHIFT2, shift2_out),
        (DOWNB, downb_out), (OWN_UP, upb_out),
    )):
        vectors[index][...] = sums_ref[row, :]
        stores.append(pltpu.make_async_copy(vectors[index], out, small_sem.at[index]))
        stores[-1].start()
    qv_ref[...] = sums_ref[OWN_QV : OWN_QV + 2, : qv_ref.shape[1]]
    stores.append(pltpu.make_async_copy(qv_ref, qv_out, small_sem.at[7]))
    stores[-1].start()
    for copy in stores:
        copy.wait()


def on_device(
    tokens, segment_ids, cotangent, norm1_gain, norm1_shift, w_qkv, qv_bias, w_out, out_bias,
    norm2_gain, norm2_shift, w_up, up_bias, w_down, down_bias,
):
    rows, seq, width = tokens.shape
    count = rows * seq
    shard = w_up.shape[1]
    heads = w_out.shape[0] // HEAD
    tiles = shard // UNIT
    units = 2 * tiles + 3
    qkv_rows = jnp.transpose(w_qkv, (1, 2, 0)).reshape(3, heads, HEAD, width)

    any_space = pl.BlockSpec(memory_space=pl.ANY)
    dma = pltpu.SemaphoreType.DMA
    vm = pltpu.VMEM
    mixed, input_grad, grads, sums = pl.pallas_call(
        functools.partial(kernel, rows=rows, seq=seq),
        out_shape=(
            jax.ShapeDtypeStruct((count, width), BF16),
            jax.ShapeDtypeStruct((count, width), BF16),
            jax.ShapeDtypeStruct((units * UNIT, width), BF16),
            jax.ShapeDtypeStruct((16, width), F32),
        ),
        in_specs=[any_space] * 15,
        out_specs=(any_space,) * 4,
        scratch_shapes=[
            vm((2, heads, 3, 2, HEAD, width), BF16),
            vm((2, heads, 2, HEAD, width), BF16),
            vm((2, 2, tiles, 2 * UNIT, width), BF16),
            vm((2, 2, 16, width), BF16),
            vm((2, 2, units * UNIT, width), BF16),
            vm((2, 2 * UNIT, width), BF16),
            vm((units * UNIT, width), BF16),
            vm((units * UNIT // 2, width), BF16),
            vm((2, units * UNIT // 4, width), BF16),
            vm((count, width), BF16),
            vm((count, width), BF16),
            vm((count, width), BF16),
            vm((2, heads, count, 3 * 128), BF16),
            vm((count, width), BF16),
            vm((count, width), F32),
            vm((count, width), BF16),
            vm((count, width), BF16),
            vm((count, width), F32),
            vm((count, UNIT), BF16),
            vm((count, UNIT), BF16),
            vm((count, 128), F32),
            vm((count, 128), BF16),
            vm((count, 128), BF16),
            vm((16, width), F32),
            vm((12, 16, width), F32),
            vm((rows, seq), jnp.int32),
            *[vm((width,), BF16)] * 7,
            vm((2, heads * HEAD), BF16),
            dma((10,)),
            dma((10 + units,)),
            dma((7,)), dma((7,)), dma((7,)), dma((7,)), dma((7,)), dma((7,)),
            dma((7,)), dma((7,)), dma((7,)), dma((7,)), dma((3,)), dma((3,)),
            dma((12,)), dma((12,)),
            dma((units,)), dma((units,)), dma((units,)), dma((units,)),
            dma((units,)), dma((units,)), dma((units,)), dma((units,)), dma((units,)), dma((units,)),
            dma((units,)), dma((units,)), dma((6,)), dma((6,)),
        ],
        compiler_params=pltpu.CompilerParams(
            collective_id=0, has_side_effects=True, vmem_limit_bytes=64 * 2**20 - 2**16
        ),
    )(
        tokens.reshape(count, width), cotangent.reshape(count, width), segment_ids,
        norm1_gain, norm1_shift, out_bias, norm2_gain, norm2_shift, down_bias, up_bias, qv_bias,
        qkv_rows, w_out.reshape(heads, HEAD, width), w_up, w_down.reshape(tiles, UNIT, width),
    )

    groups = lax.axis_size("dp") // 8
    if groups > 1:
        grads, sums = lax.psum((grads.astype(F32) * 0.125, sums * 0.125), "dp")
    whole = [jax.ShapeDtypeStruct((width,), F32)] * 7
    results = pl.pallas_call(
        tail_kernel,
        out_shape=(
            mixed, input_grad,
            jax.ShapeDtypeStruct((3, heads, HEAD, width), F32), jax.ShapeDtypeStruct((heads * HEAD, width), F32),
            jax.ShapeDtypeStruct((width, shard), F32), jax.ShapeDtypeStruct((tiles, UNIT, width), F32),
            jax.ShapeDtypeStruct((2, heads * HEAD), F32), *whole,
        ),
        in_specs=[any_space] * 4,
        out_specs=(any_space,) * 14,
        scratch_shapes=[
            vm((count, width), BF16), vm((count, width), BF16), vm(grads.shape, grads.dtype),
            vm((3, heads, HEAD, width), F32), vm((heads * HEAD, width), F32),
            vm((width, shard), F32), vm((tiles, UNIT, width), F32),
            vm((16, width), F32), vm((2, heads * HEAD), F32),
            dma((2 + tiles + 1,)), dma((2 * tiles + 4,)), dma((9,)),
            *[vm((width,), F32)] * 7,
        ],
        compiler_params=pltpu.CompilerParams(vmem_limit_bytes=63 * 2**20),
    )(mixed, input_grad, grads, sums)
    mixed, input_grad, grad_qkv, grad_out, grad_up, grad_down, grad_qv, *vectors = results
    gain1, shift1, outb, gain2, shift2, downb, upb = vectors
    return (
        mixed.reshape(rows, seq, width),
        input_grad.reshape(rows, seq, width),
        gain1,
        shift1,
        jnp.transpose(grad_qkv.reshape(3, heads * HEAD, width), (2, 0, 1)),
        grad_qv,
        grad_out,
        outb,
        gain2,
        shift2,
        grad_up,
        upb,
        grad_down.reshape(shard, width),
        downb,
    )


def solution(mesh):
    tall = P(("dp", "mp"), None, None)
    return jax.shard_map(
        on_device,
        mesh=mesh,
        in_specs=(
            tall, P(("dp", "mp"), None), tall, P(), P(), P(None, None, "mp"), P(None, "mp"), P("mp", None),
            P(), P(), P(), P(None, "mp"), P("mp"), P("mp", None), P(),
        ),
        out_specs=(
            tall, tall, P(), P(), P(None, None, "mp"), P(None, "mp"), P("mp", None), P(), P(), P(),
            P(None, "mp"), P("mp"), P("mp", None), P(),
        ),
        check_vma=False,
    )
```

time: 225 us -> 185 us (0.82)
  local copies, waits for them, and re-layouts: 24.9 us -> 0 us
  Pallas kernels: 196 us -> 184 us
    pallas_call x1, Pallas kernels: 196 us -> 178 us  [on_device(): pl.pallas_call(functools.partial(kernel, rows=rows, seq=seq), out_shape=(...]
    slice x6 -> x0, local copies, waits for them, and re-layouts: 7.68 us -> none  [the longest x1 1.84 us: on_device(): grad_down = expert[:, 1].reshape(shard, width)]
    unnamed x7 -> x0, local copies, waits for them, and re-layouts: 7.17 us -> none
    pallas_call x0 -> x1, Pallas kernels: none -> 5.98 us  [on_device(): pl.pallas_call(tail_kernel, out_shape=(mixed, input_grad, jax.ShapeDtypeS...]
    another operation x7 -> x0, local copies, waits for them, and re-layouts: 4.15 us -> none  [on_device(): jnp.stack([norm1_gain, norm1_shift, out_bias, norm2_gain, norm2_shift, do...]
    reshape x5 -> x0, local copies, waits for them, and re-layouts: 3.73 us -> none  [the longest x1 2.13 us: on_device(): jnp.transpose(w_qkv, (1, 2, 0)).reshape(3, heads, HEAD, width)]
where the time goes in v3:
time: 185 us
  Pallas kernels  184 us (99%)
    pallas_call x1, Pallas kernels, on_device(): pl.pallas_call(functools.partial(kernel, rows=rows, seq=seq), out_shape=(...  178 us
    pallas_call x1, Pallas kernels, on_device(): pl.pallas_call(tail_kernel, out_shape=(mixed, input_grad, jax.ShapeDtypeS...  5.98 us

profile of v3, /device:TPU:0, one launch (start us, length us, event | category | flops | bytes accessed | tf_op | source)
XLA Modules:
  0.0 184.9 jit_solution(1739371126311268248)
XLA Ops:
  0.7 178.1 %shard_map.254 = (bf16[1024,768]{1,0:T(8,128)(2,1)}, bf16[1024,768]{1,0:T(8,128)(2,1)}, bf16[2304,768]{1,0:T(8,128)(2,1)}, f32[16,768]{1,0:T(8,128)}) custom-call(bf16[1024,768]{1,0:T(8,128)(2,1)} %bitcast.13, bf16[1024,768]{1,0:T(8,128)(2,1)} %bitcast.14, s32[2,512]{1,0:T(2,128)} %seg_in.1, bf16[768]{0:T(1024)(128)(2,1)} %gain1_in.1, ...), custom_call_target="tpu_custom_call" | custom-call | tf_op jit(solution)/shard_map/pallas_call | solution.py:871
  178.7 6.0 %shard_map.255 = (bf16[1024,768]{1,0:T(8,128)(2,1)}, bf16[1024,768]{1,0:T(8,128)(2,1)}, f32[3,3,64,768]{3,2,1,0:T(8,128)}, f32[192,768]{1,0:T(8,128)}, f32[768,7...) custom-call(bf16[1024,768]{1,0:T(8,128)(2,1)} %get-tuple-element.32., ...), custom_call_target="tpu_custom_call" | custom-call | tf_op jit(solution)/shard_map/pallas_call | solution.py:932

commit v4 on v3

v4 whole, which is shorter than its diff:
```python
import functools

import jax
import jax.numpy as jnp
from jax import lax
from jax.experimental import pallas as pl
from jax.experimental.pallas import tpu as pltpu
from jax.sharding import PartitionSpec as P

HEAD = 64
EPS = 1e-06
MASKED = -1e30
UNIT = 256
SPLIT = 4
INV_LANE = 32
OWN_UP, OWN_QV = 12, 13
F32, BF16 = jnp.float32, jnp.bfloat16

GAIN1, SHIFT1, OUTB, GAIN2, SHIFT2, DOWNB, QUERYB, VALUEB, UPB = range(9)

UNITS = (
    (0, 256),
    (256, 256),
    (512, 256),
    (768, 256),
    (1024, 256),
    (1280, 256),
    (1536, 192),
    (1728, 192),
    (1920, 192),
    (2112, 128),
    (2240, 64),
)
GRANULES = (
    (0, 0, 512, (0, 1)),
    (1, 0, 512, (0, 1)),
    (1, 512, 512, (2, 3)),
    (0, 512, 512, (2, 3)),
    (0, 1024, 512, (4, 5)),
    (1, 1024, 512, (4, 5)),
    (1, 1536, 192, (6,)),
    (0, 1536, 192, (6,)),
    (1, 1728, 192, (7,)),
    (1, 1920, 192, (8,)),
    (1, 2112, 192, (9, 10)),
    (0, 1728, 192, (7,)),
    (0, 1920, 192, (8,)),
    (0, 2112, 192, (9, 10)),
)
EARLY = (0, 2)
PIECES, AHEAD = 10, 2
FAR_PAIRS = (0, 1, 1, 0, 0, 1)
PAIR_TILES = (0, 0, 1, 1, 2, 2)
BETWEEN, FIRST_HEADS, LAST_NORM = 12, 15, 33
(
    BIAS_DONE, MATE_DONE, PASS_X, PASS_Y, PASS_DONE, CORE_ADD, CORE_SEND, EARLY_X, EARLY_Y, EARLY_Z,
    ADD_X, ADD_Y, ADD_Z, ADD_FAR, GIVE_Y, FINISH, SUMS, SETTLE,
) = range(18)
PLAN_FORWARD = (
    ((MATE_DONE, 0), (BIAS_DONE, 0),),
    ((PASS_X, 0),),
    ((PASS_X, 1),),
    ((MATE_DONE, 1),),
    (),
    ((PASS_X, 2),),
    ((MATE_DONE, 2),),
    ((PASS_X, 3), (PASS_Y, 0),),
    (),
    ((PASS_DONE, 0), (BIAS_DONE, 1), (BIAS_DONE, 2),),
    ((PASS_X, 4), (PASS_Y, 1),),
    ((PASS_X, 5),),
    ((PASS_DONE, 1),),
    ((PASS_Y, 2),),
    ((PASS_X, 6),),
    ((PASS_DONE, 2),),
    ((PASS_X, 7), (PASS_Y, 3),),
    (),
)
PLAN_SECOND = (
    ((PASS_X, 8), (MATE_DONE, 3), (PASS_DONE, 3),),
    (),
    ((PASS_X, 9), (PASS_Y, 4),),
    (),
)
PLAN_MAIN = (
    ((MATE_DONE, 4), (MATE_DONE, 5),),
    ((PASS_Y, 5), (CORE_SEND, 0),),
    ((PASS_Y, 6), (PASS_DONE, 4), (PASS_DONE, 5),),
    ((CORE_ADD, 0), (CORE_SEND, 1),),
    ((PASS_Y, 7), (CORE_ADD, 1), (PASS_DONE, 6), (PASS_DONE, 7),),
    ((PASS_Y, 8), (CORE_SEND, 2),),
    ((PASS_Y, 9), (MATE_DONE, 6), (MATE_DONE, 7),),
    ((CORE_ADD, 2), (CORE_SEND, 3), (EARLY_Y, 0), (ADD_X, 1),),
    ((CORE_ADD, 3), (EARLY_X, 0), (MATE_DONE, 8), (MATE_DONE, 9),),
    ((CORE_SEND, 4), (EARLY_X, 2), (ADD_Y, 1),),
    ((CORE_ADD, 4), (EARLY_Y, 2), (ADD_X, 3), (PASS_DONE, 8), (PASS_DONE, 9),),
    ((CORE_SEND, 5), (ADD_Z, 1),),
    ((CORE_ADD, 5), (EARLY_Z, 0), (ADD_Y, 3),),
    ((EARLY_Z, 2), (ADD_FAR, 1),),
    ((CORE_SEND, 6), (ADD_Z, 0), (ADD_Z, 3),),
    ((CORE_ADD, 6), (CORE_SEND, 7), (ADD_Z, 2), (GIVE_Y, 1),),
    ((CORE_ADD, 7), (ADD_X, 4),),
    ((ADD_FAR, 0),),
    ((CORE_SEND, 8),),
    ((CORE_ADD, 8), (FINISH, 1),),
    ((ADD_FAR, 3),),
    ((CORE_SEND, 9), (ADD_X, 5), (ADD_Y, 4),),
    ((CORE_ADD, 9), (ADD_FAR, 2), (GIVE_Y, 0), (GIVE_Y, 3),),
    ((ADD_Z, 4),),
    ((CORE_SEND, 10), (ADD_X, 6), (ADD_Y, 5),),
    ((CORE_ADD, 10), (GIVE_Y, 2),),
    ((FINISH, 0),),
    ((CORE_SEND, 11), (ADD_FAR, 4),),
    ((CORE_ADD, 11), (ADD_X, 7), (ADD_Z, 5), (FINISH, 3),),
    ((ADD_Y, 6),),
    ((CORE_SEND, 12), (FINISH, 2),),
    ((CORE_ADD, 12), (ADD_X, 8), (ADD_Y, 7), (GIVE_Y, 4),),
    ((ADD_FAR, 5),),
    ((CORE_SEND, 13), (ADD_Z, 6),),
    ((CORE_ADD, 13), (ADD_X, 9), (ADD_X, 10), (ADD_Y, 8), (ADD_Z, 7),),
    ((GIVE_Y, 5),),
    ((ADD_FAR, 6), (FINISH, 4),),
)
PLAN_DRAIN = (
    (ADD_Z, 8),
    (SUMS, 0),
    (ADD_Y, 9),
    (SETTLE, 0),
    (SETTLE, 1),
    (SETTLE, 2),
    (SETTLE, 3),
    (ADD_FAR, 7),
    (ADD_Y, 10),
    (SETTLE, 4),
    (SETTLE, 5),
    (SETTLE, 6),
    (SETTLE, 7),
    (GIVE_Y, 6),
    (SUMS, 1),
    (SETTLE, 8),
    (SETTLE, 9),
    (SETTLE, 10),
    (SETTLE, 12),
    (SETTLE, 13),
    (SETTLE, 14),
    (SETTLE, 15),
    (SETTLE, 16),
    (SETTLE, 17),
    (SETTLE, 18),
    (ADD_Z, 9),
    (SUMS, 2),
    (ADD_FAR, 8),
    (FINISH, 5),
    (GIVE_Y, 7),
    (SETTLE, 19),
    (ADD_Z, 10),
    (SUMS, 3),
    (FINISH, 6),
    (ADD_FAR, 9),
    (GIVE_Y, 8),
    (SETTLE, 20),
    (SUMS, 4),
    (ADD_FAR, 10),
    (FINISH, 7),
    (GIVE_Y, 9),
    (SUMS, 5),
    (GIVE_Y, 10),
    (SETTLE, 21),
    (SETTLE, 11),
    (SETTLE, 22),
    (FINISH, 8),
    (FINISH, 9),
    (FINISH, 10),
)

def dot(left, right, left_dim, right_dim):
    return lax.dot_general(
        left, right, (((left_dim,), (right_dim,)), ((), ())), preferred_element_type=F32
    )


def column_sum(values):
    return jnp.sum(values, axis=0, keepdims=True)


def gelu_parts(pre):
    cumul = 0.5 + 0.5 * lax.erf(pre * 0.7071067811865476)
    return cumul, jnp.exp(-0.5 * pre * pre) * 0.3989422804014327


def kernel(
    x_in, g_in, seg_in, gain1_in, shift1_in, outb_in, gain2_in, shift2_in, downb_in, upb_in, qvb_in,
    qkv_in, out_in, up_in, down_in,
    mixed_out, input_out, grads_out, sums_out,
    wq, wo, wm, wb, grad, mate_buf, early_buf, x_buf, y_buf, z_buf,
    x_ref, g_ref, a1_ref, proj_ref, o_ref, x1_ref, hat2_ref, a2_ref, da2_ref,
    hid_ref, low_ref, lse_ref, aug_q, aug_k, sums, sums_recv,
    seg_ref, gain1_ref, shift1_ref, outb_ref, gain2_ref, shift2_ref, downb_ref, upb_ref, qvb_ref, small_sem,
    local_sem, wm_s, wm_r, wx_s, wx_r, wy_s, wy_r, wz_s, wz_r, wd_s, wd_r, wf_s, wf_r, wb_s, wb_r,
    core_s, core_r, early_s, early_r, ex_s, ex_r, ey_s, ey_r, ez_s, ez_r, ew_s, ew_r, fz_s, fz_r, fy_s, fy_r, sums_s, sums_r,
    *, rows, seq,
):
    tokens, width = x_ref.shape
    dp, mp = lax.axis_index("dp"), lax.axis_index("mp")
    c, x = mp % 2, mp // 2
    y, z = dp % 2, (dp // 2) % 4
    block = dp - dp % 8
    zb = z % 2
    nx, nc, ny = 1 - x, 1 - c, 1 - y

    def device(zz, yy, xx, cc):
        return (block + zz * 2 + yy, xx * 2 + cc)

    mate = device(z, y, x, nc)
    x_peer = device(z, y, nx, c)
    y_peer = device(z, ny, x, c)
    z_far = device((z + 2) % 4, y, x, c)
    z_pair = device(z + 1 - 2 * zb, y, x, c)
    cross = device(z, y, nx, nc)
    corner = device(z + 1 - 2 * zb, ny, x, c)

    def remote(src, dst, send, recv, where):
        return pltpu.make_async_remote_copy(
            src_ref=src, dst_ref=dst, send_sem=send, recv_sem=recv,
            device_id=where, device_id_type=pl.DeviceIdType.MESH,
        )

    barrier = pltpu.get_barrier_semaphore()
    everyone = [mate, x_peer, cross, y_peer, z_pair, z_far, corner]
    for peer in everyone:
        pl.semaphore_signal(barrier, inc=1, device_id=peer, device_id_type=pl.DeviceIdType.MESH)

    up_stage = grad.at[0, 0, pl.ds(0, width)]
    locals_ = [
        pltpu.make_async_copy(qkv_in.at[:, 0], wq.at[x, 0, :, c], local_sem.at[0]),
        pltpu.make_async_copy(qkv_in.at[:, 1], wq.at[x, 1, :, c], local_sem.at[1]),
        pltpu.make_async_copy(qkv_in.at[:, 2], wq.at[x, 2, :, c], local_sem.at[2]),
        pltpu.make_async_copy(x_in, x_ref, local_sem.at[3]),
        pltpu.make_async_copy(out_in, wo.at[x, :, c], local_sem.at[4]),
        pltpu.make_async_copy(up_in, up_stage, local_sem.at[5]),
        pltpu.make_async_copy(down_in, wm.at[x, c, :, pl.ds(UNIT, UNIT)], local_sem.at[6]),
        pltpu.make_async_copy(g_in, g_ref, local_sem.at[7]),
    ]
    small_copies = [
        pltpu.make_async_copy(src, dst, small_sem.at[i])
        for i, (src, dst) in enumerate((
            (seg_in, seg_ref), (upb_in, upb_ref), (qvb_in, qvb_ref), (gain1_in, gain1_ref), (shift1_in, shift1_ref),
            (outb_in, outb_ref), (gain2_in, gain2_ref), (shift2_in, shift2_ref), (downb_in, downb_ref),
        ))
    ]
    for copy in small_copies + locals_:
        copy.start()
    for copy in small_copies:
        copy.wait()

    from_lane = lax.broadcasted_iota(jnp.int32, (qvb_ref.shape[1], 384), 0)
    to_lane = lax.broadcasted_iota(jnp.int32, (qvb_ref.shape[1], 384), 1)
    placed = jnp.logical_and(
        from_lane == (to_lane // 128) * 64 + to_lane % 64, (to_lane // 64) % 2 == c
    )
    place = jnp.where(placed, 1.0, 0.0).astype(BF16)
    qv_rows = dot(qvb_ref[...], place, 1, 0)
    qv_rows = jnp.concatenate([qv_rows, jnp.zeros((2, width - 384), F32)], axis=1)
    tile_row = lax.broadcasted_iota(jnp.int32, (16, width), 0)
    wb[x, c] = jnp.where(
        tile_row == 0,
        upb_ref[...].astype(F32).reshape(1, width),
        jnp.where(tile_row == 1, qv_rows[0:1], jnp.where(tile_row == 2, qv_rows[1:2], 0.0)),
    ).astype(BF16)
    lane = lax.broadcasted_iota(jnp.int32, (seq, 128), 1)
    for row in range(rows):
        ids = jnp.broadcast_to(seg_ref[row : row + 1, :].astype(F32), (128, seq)).T
        spot = lane % 64
        same = spot == ids.astype(jnp.int32)
        inside = spot < 32
        where = pl.ds(row * seq, seq)
        aug_q[where, :] = jnp.where(same, 1.0, 0.0).astype(BF16)
        aug_k[where, :] = jnp.where(jnp.logical_and(inside, jnp.logical_not(same)), MASKED, 0.0).astype(BF16)
    lse_ref[...] = jnp.zeros_like(lse_ref)
    for number in (0, 1, 2, 4):
        locals_[number].wait()
    pl.semaphore_wait(barrier, len(everyone))

    def piece(kind, index, xx, cc, part=None):
        if kind == "q":
            return wq.at[xx, index, :, cc, some(HEAD, part)]
        if kind == "o":
            return wo.at[xx, :, cc, some(HEAD, part)]
        return wm.at[xx, cc, index // 2, some(UNIT, part, (index % 2) * UNIT)]

    def some(count, part, start=0):
        if part is None:
            return pl.ds(start, count)
        return pl.ds(pl.multiple_of(start + part * (count // 4), 16), count // 4)

    quarter = y * 2 + zb

    def kinds(number, run):
        run("q" if number < 3 else "o" if number == 3 else "m", number - 4 if number > 3 else number)

    def to_mate(number, kind, index):
        own = piece(kind, index, x, c)
        return remote(own, own, wm_s.at[number], wm_r.at[number], mate)

    def to_x(number, kind, index):
        own = piece(kind, index, x, c, quarter)
        return remote(own, own, wx_s.at[number], wx_r.at[number], x_peer)

    def to_square(number, kind, index):
        held = piece(kind, index, nx, c, quarter)
        return [
            remote(held, held, send.at[number], recv.at[number], peer)
            for send, recv, peer in ((wy_s, wy_r, y_peer), (wz_s, wz_r, z_pair), (wd_s, wd_r, corner))
        ]

    def forward(number, kind, index):
        held = piece(kind, index, nx, c)
        return remote(held, held, wf_s.at[number], wf_r.at[number], mate)

    def mate_done(number):
        kinds(number, lambda kind, index: to_mate(number, kind, index).wait_recv())

    def start_x(number):
        kinds(number, lambda kind, index: to_x(number, kind, index).start())

    def pass_x(number):
        def run(kind, index):
            to_x(number, kind, index).wait_recv()
            for copy in to_square(number, kind, index):
                copy.start()

        kinds(number, run)
        if number + AHEAD < PIECES:
            start_x(number + AHEAD)

    def pass_y(number):
        def run(kind, index):
            for copy in to_square(number, kind, index):
                copy.wait_recv()
            forward(number, kind, index).start()

        kinds(number, run)

    def bias_done(number):
        biases[number].wait_recv()

    def pass_done(number):
        kinds(number, lambda kind, index: forward(number, kind, index).wait_recv())

    biases = [
        remote(wb.at[x, c], wb.at[x, c], wb_s.at[i], wb_r.at[i], peer)
        for i, peer in enumerate((mate, x_peer, cross))
    ]
    for copy in biases:
        copy.start()
    for number in range(AHEAD):
        start_x(number)
        if number < 3:
            kinds(number, lambda kind, index: to_mate(number, kind, index).start())
    for number in range(min(AHEAD, 3), 4):
        kinds(number, lambda kind, index: to_mate(number, kind, index).start())
    locals_[5].wait()
    locals_[6].wait()
    tiles = up_stage.shape[1] // UNIT
    for index in range(tiles):
        wm[x, c, index, pl.ds(0, UNIT), :] = up_stage[:, index * UNIT : (index + 1) * UNIT].T
    for number in range(4, PIECES):
        kinds(number, lambda kind, index: to_mate(number, kind, index).start())

    chunk = 128
    locals_[3].wait()
    small_refs = (gain1_ref, shift1_ref, outb_ref, gain2_ref, shift2_ref, downb_ref)

    def small(row):
        return small_refs[row][...].astype(F32).reshape(1, width)

    def norm(values):
        centred = values - jnp.mean(values, axis=-1, keepdims=True)
        inv = lax.rsqrt(jnp.mean(centred * centred, axis=-1, keepdims=True) + EPS)
        return centred * inv, inv

    def at_chunk(step):
        return pl.ds(pl.multiple_of(step * chunk, chunk), chunk)

    def first_norm(step, carry):
        where = at_chunk(step)
        hat, _ = norm(x_ref[where, :].astype(F32))
        a1_ref[where, :] = (small(0) * hat + small(1)).astype(BF16)
        return carry

    even = lane < 64

    def pick(values, others):
        return jnp.where(even, values, others), jnp.where(even, others, values)

    def part_lanes(group, part, count=1):
        return pl.ds(pl.multiple_of(group * 384 + part * 128, 128), count * 128)

    def project(step):
        xx, t = jnp.where(step < 9, x, nx), (step // 3) % 3
        group = xx * 3 + t
        weights = wq[xx, t].reshape(3 * 128, width)
        biasq = wb[xx, 0, 1:2, :].astype(F32) + wb[xx, 1, 1:2, :].astype(F32)
        biasv = wb[xx, 0, 2:3, :].astype(F32) + wb[xx, 1, 2:3, :].astype(F32)
        pq = jnp.where(t == 0, biasq[:, :128], jnp.where(t == 1, biasq[:, 128:256], biasq[:, 256:384]))
        pv = jnp.where(t == 0, biasv[:, :128], jnp.where(t == 1, biasv[:, 128:256], biasv[:, 256:384]))
        for row in range(rows):
            where = pl.ds(row * seq, seq)
            value = dot(a1_ref[where, :], weights, 1, 1)
            proj_ref[where, part_lanes(group, 0)] = ((value[:, :128] + pq).astype(BF16) * 0.125).astype(BF16)
            proj_ref[where, part_lanes(group, 1)] = value[:, 128:256].astype(BF16)
            proj_ref[where, part_lanes(group, 2)] = (value[:, 256:] + pv).astype(BF16)

    def attend_forward(step):
        xx, t = jnp.where(step < 9, x, nx), (step // 3) % 3
        group = xx * 3 + t
        row = step % 3 - 1
        where = pl.ds(pl.multiple_of(row * seq, seq), seq)
        qs = pick(proj_ref[where, part_lanes(group, 0)], aug_q[where, :])
        ks = pick(proj_ref[where, part_lanes(group, 1)], aug_k[where, :])
        vs = pick(proj_ref[where, part_lanes(group, 2)], jnp.ones((seq, 128), BF16))
        scores = [dot(q, k, 1, 1) for q, k in zip(qs, ks)]
        highest = [jnp.max(item, axis=-1, keepdims=True) for item in scores]
        result = [
            dot(jnp.exp(item - top).astype(BF16), v, 1, 0) for item, top, v in zip(scores, highest, vs)
        ]
        total = pltpu.roll(jnp.where(even, result[1], result[0]), 64, 1)
        mixed = jnp.where(even, result[0], result[1]) / total
        o_ref[where, pl.ds(pl.multiple_of(group * 128, 128), 128)] = mixed.astype(BF16)
        log_total = jnp.where(even, highest[0], highest[1]) + jnp.log(total)
        lse_ref[where, :] = jnp.where(lane % 64 == group, log_total, lse_ref[where, :])

    def second_norm(step, carry):
        due_now(step, PLAN_SECOND)
        where = pl.ds(pl.multiple_of(step * 256, 256), 256)
        value = x_ref[where, :].astype(F32) + dot(o_ref[where, :], wo[...].reshape(width, width), 1, 0) + small(2)
        hat, inv = norm(value)
        hat2_ref[where, :] = hat.astype(BF16)
        spot = lax.broadcasted_iota(jnp.int32, (256, 128), 1)
        lse_ref[where, :] = jnp.where(spot == INV_LANE, inv, lse_ref[where, :])
        a2_ref[where, :] = (small(3) * hat + small(4)).astype(BF16)
        x1_ref[where, :] = value + small(5)
        da2_ref[where, :] = jnp.zeros_like(value)
        return carry

    def pair_place(pair):
        far = sum(jnp.where(pair == p, 1, 0) for p, flag in enumerate(FAR_PAIRS) if flag)
        tile = sum(jnp.where(pair == p, index, 0) for p, index in enumerate(PAIR_TILES))
        return jnp.where(far == 1, nx, x), tile

    def expert_tile(step):
        xx, index = pair_place(step // 2)
        cc = jnp.where(step % 2 == 0, nc, c)
        w_up = wm[xx, cc, index, pl.ds(0, UNIT), :]
        w_down = wm[xx, cc, index, pl.ds(UNIT, UNIT), :]
        lanes = pl.ds(pl.multiple_of(index * UNIT, UNIT), UNIT)
        bias = wb[xx, cc, 0:1, lanes].astype(F32)
        upb_sum = None
        part_rows = tokens // SPLIT
        for part in range(SPLIT):
            where = pl.ds(part * part_rows, part_rows)
            pre = dot(a2_ref[where, :], w_up, 1, 1) + bias
            back = dot(g_ref[where, :], w_down, 1, 1)
            cumul, density = gelu_parts(pre)
            hidden = (pre * cumul).astype(BF16)
            low = (back * (cumul + pre * density)).astype(BF16)
            hid_ref[where, :] = hidden
            low_ref[where, :] = low
            one = column_sum(low.astype(F32))
            upb_sum = one if upb_sum is None else upb_sum + one
        sums[pl.ds(UPB + xx * 2 + cc, 1), lanes] = upb_sum
        base = pl.multiple_of(index * 2 * UNIT, UNIT)
        grad[xx, cc, pl.ds(base, UNIT), :] = dot(low_ref[...], a2_ref[...], 0, 0).astype(BF16)
        grad[xx, cc, pl.ds(base + UNIT, UNIT), :] = dot(hid_ref[...], g_ref[...], 0, 0).astype(BF16)
        x1_ref[...] += dot(hid_ref[...], w_down, 1, 0)
        da2_ref[...] += dot(low_ref[...], w_up, 1, 0)

    def norm_back(grad_in, hat, inv, gain):
        scaled = grad_in * gain
        return inv * (
            scaled
            - jnp.mean(scaled, axis=-1, keepdims=True)
            - hat * jnp.mean(scaled * hat, axis=-1, keepdims=True)
        )

    def add_sum(row, values):
        sums[row : row + 1, :] += column_sum(values)

    heads_rows = 6 * UNIT

    def between_norm():
        def one(step, carry):
            where = at_chunk(step)
            da2, hat = da2_ref[where, :], hat2_ref[where, :].astype(F32)
            top = g_ref[where, :].astype(F32)
            add_sum(GAIN2, da2 * hat)
            add_sum(SHIFT2, da2)
            add_sum(DOWNB, top)
            middle = top + norm_back(da2, hat, lse_ref[where, INV_LANE : INV_LANE + 1], small(3))
            da2_ref[where, :] = middle
            low = middle.astype(BF16)
            add_sum(OUTB, low.astype(F32))
            a2_ref[where, :] = low
            hat2_ref[where, :] = x1_ref[where, :].astype(BF16)
            return carry

        lax.fori_loop(0, tokens // chunk, one, 0)
        mixed_copy.start()

    def between_out():
        for xx in range(2):
            half = dot(o_ref[:, xx * 384 : (xx + 1) * 384], a2_ref[...], 0, 0).astype(BF16)
            for t in range(3):
                for cc in range(2):
                    start = (t * 2 + cc) * 64
                    grad[xx, cc, pl.ds(heads_rows + t * 64, 64), :] = half[start : start + 64]

    def between_back():
        def back(step, carry):
            where = pl.ds(pl.multiple_of(step * 256, 256), 256)
            a2_ref[where, :] = dot(a2_ref[where, :], wo[...].reshape(width, width), 1, 1).astype(BF16)
            return carry

        lax.fori_loop(0, tokens // 256, back, 0)

    def attend_backward(step):
        xx, t = jnp.where(step < 9, nx, x), (step // 3) % 3
        group = xx * 3 + t
        lanes = pl.ds(pl.multiple_of(group * 128, 128), 128)

        def one_row():
            where = pl.ds(pl.multiple_of((step % 3) * seq, seq), seq)
            query, key, value = (proj_ref[where, part_lanes(group, i)] for i in range(3))
            out, back = o_ref[where, lanes], a2_ref[where, lanes]
            none = jnp.zeros((seq, 128), BF16)
            product = out.astype(F32) * back.astype(F32)
            log_total = lse_ref[where, :]
            tops = [
                jnp.sum(jnp.where(lane == group + shift, log_total, 0.0), axis=-1, keepdims=True)
                for shift in (0, 64)
            ]
            deltas = [jnp.sum(item, axis=-1, keepdims=True) for item in pick(product, jnp.zeros_like(product))]
            q_aug, k_aug = pick(query, aug_q[where, :]), pick(key, aug_k[where, :])
            q_own, k_own, b_own = pick(query, none), pick(key, none), pick(back, none)
            v_own = pick(value, none)
            d_query = d_key = d_value = None
            for i in range(2):
                prob = jnp.exp(dot(q_aug[i], k_aug[i], 1, 1) - tops[i])
                low = prob.astype(BF16)
                inner = dot(b_own[i], v_own[i], 1, 1) - deltas[i]
                d_score = (prob * inner).astype(BF16)
                parts = (dot(d_score, k_own[i], 1, 0), dot(d_score, q_own[i], 0, 0), dot(low, b_own[i], 0, 0))
                if i == 0:
                    d_query, d_key, d_value = parts
                else:
                    d_query, d_key, d_value = d_query + parts[0], d_key + parts[1], d_value + parts[2]
            low_query = (d_query * 0.125).astype(BF16)
            low_value = d_value.astype(BF16)
            proj_ref[where, part_lanes(group, 0)] = low_query
            proj_ref[where, part_lanes(group, 1)] = d_key.astype(BF16)
            proj_ref[where, part_lanes(group, 2)] = low_value
            sums[QUERYB : QUERYB + 1, lanes] += column_sum(low_query.astype(F32))
            sums[VALUEB : VALUEB + 1, lanes] += column_sum(low_value.astype(F32))

        def weights():
            weight_grad = dot(proj_ref[:, part_lanes(group, 0, 3)], a1_ref[...], 0, 0).astype(BF16)
            for part in range(3):
                for cc in range(2):
                    start = part * 128 + cc * 64
                    place = pl.multiple_of(heads_rows + 192 + t * 192 + part * 64, 64)
                    grad[xx, cc, pl.ds(place, 64), :] = weight_grad[start : start + 64]
        pl.when(step % 3 < 2)(one_row)
        pl.when(step % 3 == 2)(weights)

    def last_norm(step):
        where = pl.ds(pl.multiple_of(step * 256, 256), 256)
        hat, inv = norm(x_ref[where, :].astype(F32))
        da1 = dot(proj_ref[where, :], wq[...].reshape(3 * width, width), 1, 0)
        add_sum(GAIN1, da1 * hat)
        add_sum(SHIFT1, da1)
        g_ref[where, :] = (da2_ref[where, :] + norm_back(da1, hat, inv, small(0))).astype(BF16)
        pl.when(step == tokens // 256 - 1)(lambda: input_copy.start())

    sums_out_copy = pltpu.make_async_copy(sums, sums_out, small_sem.at[9])
    mixed_copy = pltpu.make_async_copy(hat2_ref, mixed_out, local_sem.at[8])
    input_copy = pltpu.make_async_copy(g_ref, input_out, local_sem.at[9])

    def add_into(xx, start, count, other, other_start):
        size = next(size for size in (64, 48, 32, 16) if count % size == 0)

        def one(step, carry):
            mine = pl.ds(pl.multiple_of(start + step * size, 16), size)
            theirs = pl.ds(pl.multiple_of(other_start + step * size, 16), size)
            grad[xx, c, mine, :] = grad[xx, c, mine, :] + other[theirs, :]
            return carry

        if count == size:
            one(0, 0)
        else:
            lax.fori_loop(0, count // size, one, 0)

    def core_copy(granule):
        far, start, count, _ = GRANULES[granule]
        return remote(
            grad.at[nx if far else x, nc, pl.ds(start, count)],
            mate_buf.at[granule % 2, pl.ds(0, count)],
            core_s.at[granule], core_r.at[granule], mate,
        )

    def core_send(granule):
        core_copy(granule).start()

    def core_add(granule):
        far, start, count, units = GRANULES[granule]
        core_copy(granule).wait_recv()
        add_into(nx if far else x, start, count, mate_buf.at[granule % 2], 0)
        for unit in units:
            if unit in EARLY:
                (early_copy if far else outer_copy)(unit).start()
            elif far:
                x_copy(unit).start()

    def outer(unit):
        return (zb, z_pair) if unit in EARLY else (y, y_peer)

    def inner(unit):
        return (y, y_peer) if unit in EARLY else (zb, z_pair)

    def x_copy(unit):
        where = half_rows(unit, outer(unit)[0]) if unit in EARLY else pl.ds(*UNITS[unit])
        return remote(grad.at[nx, c, where], x_buf.at[where], ex_s.at[unit], ex_r.at[unit], x_peer)

    def half_rows(unit, part):
        start, count = UNITS[unit]
        return pl.ds(pl.multiple_of(start + part * (count // 2), 32), count // 2)

    def share_rows(unit, part):
        start, count = UNITS[unit]
        return pl.ds(pl.multiple_of(start + outer(unit)[0] * (count // 2) + part * (count // 4), 16), count // 4)

    def half_slot(unit):
        return pl.ds(UNITS[unit][0] // 2, UNITS[unit][1] // 2)

    def share_slot(unit):
        return pl.ds(UNITS[unit][0] // 4, UNITS[unit][1] // 4)

    def outer_copy(unit):
        part, peer = outer(unit)
        return remote(
            grad.at[x, c, half_rows(unit, 1 - part)], y_buf.at[half_slot(unit)], ey_s.at[unit], ey_r.at[unit], peer
        )

    def early_copy(unit):
        index = EARLY.index(unit)
        where = pl.ds(index * UNIT // 2, UNIT // 2)
        part, peer = outer(unit)
        return remote(
            grad.at[nx, c, half_rows(unit, 1 - part)], early_buf.at[where], early_s.at[index], early_r.at[index], peer
        )

    def inner_copy(unit):
        part, peer = inner(unit)
        return remote(
            grad.at[x, c, share_rows(unit, 1 - part)], z_buf.at[0, share_slot(unit)], ez_s.at[unit], ez_r.at[unit], peer
        )

    def across_copy(unit):
        return remote(
            grad.at[x, c, share_rows(unit, inner(unit)[0])], z_buf.at[1, share_slot(unit)],
            ew_s.at[unit], ew_r.at[unit], z_far,
        )

    def back_inner_copy(unit):
        part, peer = inner(unit)
        where = share_rows(unit, part)
        return remote(x_buf.at[where], x_buf.at[where], fz_s.at[unit], fz_r.at[unit], peer)

    def back_outer_copy(unit):
        part, peer = outer(unit)
        where = half_rows(unit, part)
        return remote(x_buf.at[where], x_buf.at[where], fy_s.at[unit], fy_r.at[unit], peer)

    def early_x(unit):
        early_copy(unit).wait_recv()
        start = EARLY.index(unit) * UNIT // 2
        add_into(nx, half_rows(unit, outer(unit)[0]).start, UNIT // 2, early_buf, start)
        x_copy(unit).start()

    def early_y(unit):
        outer_copy(unit).wait_recv()
        add_into(x, half_rows(unit, outer(unit)[0]).start, UNIT // 2, y_buf, half_slot(unit).start)

    def early_z(unit):
        x_copy(unit).wait_recv()
        start = half_rows(unit, outer(unit)[0]).start
        add_into(x, start, UNIT // 2, x_buf, start)
        inner_copy(unit).start()

    def add_x(unit):
        x_copy(unit).wait_recv()
        start, count = UNITS[unit]
        add_into(x, start, count, x_buf, start)
        outer_copy(unit).start()

    def add_y(unit):
        outer_copy(unit).wait_recv()
        add_into(x, half_rows(unit, outer(unit)[0]).start, UNITS[unit][1] // 2, y_buf, half_slot(unit).start)
        inner_copy(unit).start()

    def add_z(unit):
        inner_copy(unit).wait_recv()
        start = share_rows(unit, inner(unit)[0]).start
        add_into(x, start, UNITS[unit][1] // 4, z_buf.at[0], share_slot(unit).start)
        across_copy(unit).start()

    def add_far(unit):
        across_copy(unit).wait_recv()
        where = share_rows(unit, inner(unit)[0])
        x_buf[where, :] = grad[x, c, where, :] + z_buf[1, share_slot(unit), :]
        back_inner_copy(unit).start()

    def give_y(unit):
        back_inner_copy(unit).wait_recv()
        back_outer_copy(unit).start()

    def out_copy(unit):
        where = pl.ds(*UNITS[unit])
        return pltpu.make_async_copy(x_buf.at[where], grads_out.at[where], local_sem.at[10 + unit])

    def finish(unit):
        back_outer_copy(unit).wait_recv()
        out_copy(unit).start()

    def sums_copy(slot, source, peer):
        return remote(sums_recv.at[6 + source], sums_recv.at[slot], sums_s.at[slot], sums_r.at[slot], peer)

    small_peers = [(i, i, peer) for i, peer in enumerate((mate, x_peer, y_peer, z_pair, z_far))]

    def sums_step(number):
        if number > 0:
            sums_copy(*small_peers[number - 1]).wait_recv()
            sums_recv[6 + number] = sums_recv[5 + number] + sums_recv[number - 1]
        else:
            sums_recv[6] = sums[...]
        if number < 5:
            sums_copy(*small_peers[number]).start()
        else:
            total = sums_recv[11]
            sums[...] = total
            own_up = sums[pl.ds(UPB + mp, 1), :]
            pairs = jnp.where(x == 0, total[:, :384], total[:, 384:])
            spread = jnp.where(placed, 1.0, 0.0)
            own_qv = lax.dot_general(
                pairs, spread, (((1,), (1,)), ((), ())), precision=lax.Precision.HIGHEST, preferred_element_type=F32
            )
            own_qv = jnp.concatenate([own_qv, jnp.zeros((16, width - own_qv.shape[1]), F32)], axis=1)
            total = jnp.where(tile_row == OWN_UP, own_up, total)
            total = jnp.where(tile_row == OWN_QV, own_qv[QUERYB : QUERYB + 1], total)
            sums[...] = jnp.where(tile_row == OWN_QV + 1, own_qv[VALUEB : VALUEB + 1], total)
            sums_out_copy.start()

    def piece_sends(number, kind, index):
        to_mate(number, kind, index).wait_send()
        to_x(number, kind, index).wait_send()
        for copy in to_square(number, kind, index):
            copy.wait_send()
        forward(number, kind, index).wait_send()

    def settle(number):
        if number < PIECES:
            kinds(number, functools.partial(piece_sends, number))
        elif number == PIECES:
            for granule in range(len(GRANULES)):
                core_copy(granule).wait_send()
        elif number == PIECES + 1:
            mixed_copy.wait()
            input_copy.wait()
            sums_out_copy.wait()
            for copy in biases:
                copy.wait_send()
            for slot, source, peer in small_peers:
                sums_copy(slot, source, peer).wait_send()
        else:
            unit = number - PIECES - 2
            for copy in (x_copy, outer_copy, inner_copy, across_copy, back_inner_copy):
                copy(unit).wait_send()
            if unit in EARLY:
                early_copy(unit).wait_send()

    events = {
        BIAS_DONE: bias_done,
        MATE_DONE: mate_done,
        PASS_X: pass_x,
        PASS_Y: pass_y,
        PASS_DONE: pass_done,
        CORE_ADD: core_add,
        CORE_SEND: core_send,
        EARLY_X: early_x,
        EARLY_Y: early_y,
        EARLY_Z: early_z,
        ADD_X: add_x,
        ADD_Y: add_y,
        ADD_Z: add_z,
        ADD_FAR: add_far,
        GIVE_Y: give_y,
        FINISH: finish,
        SUMS: sums_step,
        SETTLE: settle,
    }

    def run_due(due):
        for name, number in due:
            events[name](number)

    def due_now(step, plan):
        def among(low, high):
            if high - low == 1:
                run_due(plan[low])
                return
            middle = (low + high) // 2
            for first, last, here in ((low, middle, step < middle), (middle, high, step >= middle)):
                if any(plan[first:last]):
                    pl.when(here)(functools.partial(among, first, last))

        among(0, len(plan))

    lax.fori_loop(0, tokens // chunk, first_norm, 0)

    def forward_step(step, carry):
        due_now(step, PLAN_FORWARD)
        pl.when(step % 3 == 0)(lambda: project(step))
        pl.when(step % 3 > 0)(lambda: attend_forward(step))
        return carry

    lax.fori_loop(0, 18, forward_step, 0)
    lax.fori_loop(0, tokens // 256, second_norm, 0)
    sums[...] = jnp.zeros_like(sums)
    locals_[7].wait()

    def main_step(step, carry):
        due_now(step, PLAN_MAIN)
        pl.when(step < BETWEEN)(lambda: expert_tile(step))
        pl.when(step == BETWEEN)(between_norm)
        pl.when(step == BETWEEN + 1)(between_out)
        pl.when(step == BETWEEN + 2)(between_back)
        pl.when(jnp.logical_and(step >= FIRST_HEADS, step < LAST_NORM))(
            lambda: attend_backward(step - FIRST_HEADS)
        )
        pl.when(step >= LAST_NORM)(lambda: last_norm(step - LAST_NORM))
        return carry

    lax.fori_loop(0, LAST_NORM + tokens // 256, main_step, 0)
    run_due(PLAN_DRAIN)


    for unit in range(len(UNITS)):
        back_outer_copy(unit).wait_send()
        out_copy(unit).wait()


def tail_kernel(
    mixed_in, input_in, grads_in, sums_in,
    mixed_out, input_out, qkv_out, wout_out, up_out, down_out,
    qv_out, gain1_out, shift1_out, outb_out, gain2_out, shift2_out, downb_out, upb_out,
    mixed, inputs, grads, qkv, wout, up, down, sums_ref, qv_ref, in_sem, out_sem, small_sem, *vectors,
):
    tiles = down.shape[0]
    heads = qkv.shape[1]
    copies = [
        pltpu.make_async_copy(mixed_in, mixed, in_sem.at[0]),
        pltpu.make_async_copy(input_in, inputs, in_sem.at[1]),
    ]
    loads = []
    for index in range(tiles + 1):
        rows = pl.ds(index * 2 * UNIT, 2 * UNIT if index < tiles else 3 * UNIT)
        loads.append(pltpu.make_async_copy(grads_in.at[rows], grads.at[rows], in_sem.at[2 + index]))
    sums_copy = pltpu.make_async_copy(sums_in, sums_ref, small_sem.at[8])
    for copy in copies + loads + [sums_copy]:
        copy.start()
    stores = [
        pltpu.make_async_copy(mixed, mixed_out, out_sem.at[2 * tiles + 2]),
        pltpu.make_async_copy(inputs, input_out, out_sem.at[2 * tiles + 3]),
    ]
    for copy, store in zip(copies, stores):
        copy.wait()
        store.start()
    for index in range(tiles):
        loads[index].wait()
        start = index * 2 * UNIT
        down[index] = grads[start + UNIT : start + 2 * UNIT, :].astype(F32)
        stores.append(pltpu.make_async_copy(down.at[index], down_out.at[index], out_sem.at[2 * index]))
        stores[-1].start()
        lanes = pl.ds(index * UNIT, UNIT)
        up[:, lanes] = grads[start : start + UNIT, :].astype(F32).T
        stores.append(pltpu.make_async_copy(up.at[:, lanes], up_out.at[:, lanes], out_sem.at[2 * index + 1]))
        stores[-1].start()
    loads[tiles].wait()
    start = 2 * tiles * UNIT
    wout[...] = grads[start : start + heads * HEAD, :].astype(F32)
    stores.append(pltpu.make_async_copy(wout, wout_out, out_sem.at[2 * tiles]))
    stores[-1].start()
    start += heads * HEAD
    for head in range(heads):
        for part in range(3):
            row = start + (head * 3 + part) * HEAD
            qkv[part, head] = grads[row : row + HEAD, :].astype(F32)
    stores.append(pltpu.make_async_copy(qkv, qkv_out, out_sem.at[2 * tiles + 1]))
    stores[-1].start()
    sums_copy.wait()
    for index, (row, out) in enumerate((
        (GAIN1, gain1_out), (SHIFT1, shift1_out), (OUTB, outb_out), (GAIN2, gain2_out), (SHIFT2, shift2_out),
        (DOWNB, downb_out), (OWN_UP, upb_out),
    )):
        vectors[index][...] = sums_ref[row, :]
        stores.append(pltpu.make_async_copy(vectors[index], out, small_sem.at[index]))
        stores[-1].start()
    qv_ref[...] = sums_ref[OWN_QV : OWN_QV + 2, : qv_ref.shape[1]]
    stores.append(pltpu.make_async_copy(qv_ref, qv_out, small_sem.at[7]))
    stores[-1].start()
    for copy in stores:
        copy.wait()


def on_device(
    tokens, segment_ids, cotangent, norm1_gain, norm1_shift, w_qkv, qv_bias, w_out, out_bias,
    norm2_gain, norm2_shift, w_up, up_bias, w_down, down_bias,
):
    rows, seq, width = tokens.shape
    count = rows * seq
    shard = w_up.shape[1]
    heads = w_out.shape[0] // HEAD
    tiles = shard // UNIT
    units = 2 * tiles + 3
    qkv_rows = jnp.transpose(w_qkv, (1, 2, 0)).reshape(3, heads, HEAD, width)

    any_space = pl.BlockSpec(memory_space=pl.ANY)
    dma = pltpu.SemaphoreType.DMA
    vm = pltpu.VMEM
    mixed, input_grad, grads, sums = pl.pallas_call(
        functools.partial(kernel, rows=rows, seq=seq),
        out_shape=(
            jax.ShapeDtypeStruct((count, width), BF16),
            jax.ShapeDtypeStruct((count, width), BF16),
            jax.ShapeDtypeStruct((units * UNIT, width), BF16),
            jax.ShapeDtypeStruct((16, width), F32),
        ),
        in_specs=[any_space] * 15,
        out_specs=(any_space,) * 4,
        scratch_shapes=[
            vm((2, heads, 3, 2, HEAD, width), BF16),
            vm((2, heads, 2, HEAD, width), BF16),
            vm((2, 2, tiles, 2 * UNIT, width), BF16),
            vm((2, 2, 16, width), BF16),
            vm((2, 2, units * UNIT, width), BF16),
            vm((2, 2 * UNIT, width), BF16),
            vm((len(EARLY) * UNIT // 2, width), BF16),
            vm((units * UNIT, width), BF16),
            vm((units * UNIT // 2, width), BF16),
            vm((2, units * UNIT // 4, width), BF16),
            vm((count, width), BF16),
            vm((count, width), BF16),
            vm((count, width), BF16),
            vm((count, 2 * heads * 3 * 128), BF16),
            vm((count, width), BF16),
            vm((count, width), F32),
            vm((count, width), BF16),
            vm((count, width), BF16),
            vm((count, width), F32),
            vm((count, UNIT), BF16),
            vm((count, UNIT), BF16),
            vm((count, 128), F32),
            vm((count, 128), BF16),
            vm((count, 128), BF16),
            vm((16, width), F32),
            vm((12, 16, width), F32),
            vm((rows, seq), jnp.int32),
            *[vm((width,), BF16)] * 7,
            vm((2, heads * HEAD), BF16),
            dma((10,)),
            dma((10 + len(UNITS),)),
            *[dma((PIECES,))] * 12, dma((3,)), dma((3,)),
            dma((len(GRANULES),)), dma((len(GRANULES),)), dma((len(EARLY),)), dma((len(EARLY),)),
            *[dma((len(UNITS),))] * 12,
            dma((6,)), dma((6,)),
        ],
        compiler_params=pltpu.CompilerParams(
            collective_id=0, has_side_effects=True, vmem_limit_bytes=64 * 2**20 - 2**16
        ),
    )(
        tokens.reshape(count, width), cotangent.reshape(count, width), segment_ids,
        norm1_gain, norm1_shift, out_bias, norm2_gain, norm2_shift, down_bias, up_bias, qv_bias,
        qkv_rows, w_out.reshape(heads, HEAD, width), w_up, w_down.reshape(tiles, UNIT, width),
    )

    groups = lax.axis_size("dp") // 8
    if groups > 1:
        grads, sums = lax.psum((grads.astype(F32) * 0.125, sums * 0.125), "dp")
    whole = [jax.ShapeDtypeStruct((width,), F32)] * 7
    results = pl.pallas_call(
        tail_kernel,
        out_shape=(
            mixed, input_grad,
            jax.ShapeDtypeStruct((3, heads, HEAD, width), F32), jax.ShapeDtypeStruct((heads * HEAD, width), F32),
            jax.ShapeDtypeStruct((width, shard), F32), jax.ShapeDtypeStruct((tiles, UNIT, width), F32),
            jax.ShapeDtypeStruct((2, heads * HEAD), F32), *whole,
        ),
        in_specs=[any_space] * 4,
        out_specs=(any_space,) * 14,
        scratch_shapes=[
            vm((count, width), BF16), vm((count, width), BF16), vm(grads.shape, grads.dtype),
            vm((3, heads, HEAD, width), F32), vm((heads * HEAD, width), F32),
            vm((width, shard), F32), vm((tiles, UNIT, width), F32),
            vm((16, width), F32), vm((2, heads * HEAD), F32),
            dma((2 + tiles + 1,)), dma((2 * tiles + 4,)), dma((9,)),
            *[vm((width,), F32)] * 7,
        ],
        compiler_params=pltpu.CompilerParams(vmem_limit_bytes=63 * 2**20),
    )(mixed, input_grad, grads, sums)
    mixed, input_grad, grad_qkv, grad_out, grad_up, grad_down, grad_qv, *vectors = results
    gain1, shift1, outb, gain2, shift2, downb, upb = vectors
    return (
        mixed.reshape(rows, seq, width),
        input_grad.reshape(rows, seq, width),
        gain1,
        shift1,
        jnp.transpose(grad_qkv.reshape(3, heads * HEAD, width), (2, 0, 1)),
        grad_qv,
        grad_out,
        outb,
        gain2,
        shift2,
        grad_up,
        upb,
        grad_down.reshape(shard, width),
        downb,
    )


def solution(mesh):
    tall = P(("dp", "mp"), None, None)
    return jax.shard_map(
        on_device,
        mesh=mesh,
        in_specs=(
            tall, P(("dp", "mp"), None), tall, P(), P(), P(None, None, "mp"), P(None, "mp"), P("mp", None),
            P(), P(), P(), P(None, "mp"), P("mp"), P("mp", None), P(),
        ),
        out_specs=(
            tall, tall, P(), P(), P(None, None, "mp"), P(None, "mp"), P("mp", None), P(), P(), P(),
            P(None, "mp"), P("mp"), P("mp", None), P(),
        ),
        check_vma=False,
    )
```

time: 185 us -> 157 us (0.85)
  Pallas kernels: 184 us -> 156 us
    pallas_call x1, Pallas kernels: 178 us -> 150 us  [on_device(): pl.pallas_call(functools.partial(kernel, rows=rows, seq=seq), out_shape=(...]
where the time goes in v4:
time: 157 us
  Pallas kernels  156 us (99%)
    pallas_call x1, Pallas kernels, on_device(): pl.pallas_call(functools.partial(kernel, rows=rows, seq=seq), out_shape=(...  150 us
    pallas_call x1, Pallas kernels, on_device(): pl.pallas_call(tail_kernel, out_shape=(mixed, input_grad, jax.ShapeDtypeS...  5.98 us

profile of v4, /device:TPU:0, one launch (start us, length us, event | category | flops | bytes accessed | tf_op | source)
XLA Modules:
  0.0 156.8 jit_solution(3234200894372559547)
XLA Ops:
  0.7 150.2 %shard_map.254 = (bf16[1024,768]{1,0:T(8,128)(2,1)}, bf16[1024,768]{1,0:T(8,128)(2,1)}, bf16[2304,768]{1,0:T(8,128)(2,1)}, f32[16,768]{1,0:T(8,128)}) custom-call(bf16[1024,768]{1,0:T(8,128)(2,1)} %bitcast.13, bf16[1024,768]{1,0:T(8,128)(2,1)} %bitcast.14, s32[2,512]{1,0:T(2,128)} %seg_in.1, bf16[768]{0:T(1024)(128)(2,1)} %gain1_in.1, ...), custom_call_target="tpu_custom_call" | custom-call | tf_op jit(solution)/shard_map/pallas_call | solution.py:939
  150.9 6.0 %shard_map.255 = (bf16[1024,768]{1,0:T(8,128)(2,1)}, bf16[1024,768]{1,0:T(8,128)(2,1)}, f32[3,3,64,768]{3,2,1,0:T(8,128)}, f32[192,768]{1,0:T(8,128)}, f32[768,7...) custom-call(bf16[1024,768]{1,0:T(8,128)(2,1)} %get-tuple-element.32., ...), custom_call_target="tpu_custom_call" | custom-call | tf_op jit(solution)/shard_map/pallas_call | solution.py:999

commit v5 on v4

--- a/solution.py
+++ b/solution.py
@@ -18,159 +18,154 @@
 
 GAIN1, SHIFT1, OUTB, GAIN2, SHIFT2, DOWNB, QUERYB, VALUEB, UPB = range(9)
 
+KINDS = 16
+(
+    TO_MATE, TO_X, TO_Y, TO_Z, TO_CORNER, FORWARD, BIAS, CORE, EARLY_OUT, X_OUT, OUTER, INNER, ACROSS, BACK_INNER,
+    BACK_OUTER, SUMS_OUT,
+) = range(KINDS)
+
 UNITS = (
-    (0, 256),
-    (256, 256),
-    (512, 256),
-    (768, 256),
-    (1024, 256),
-    (1280, 256),
+    (0, 128),
+    (128, 128),
+    (256, 128),
+    (384, 128),
+    (512, 128),
+    (640, 128),
+    (768, 128),
+    (896, 128),
+    (1024, 128),
+    (1152, 128),
+    (1280, 128),
+    (1408, 128),
     (1536, 192),
     (1728, 192),
-    (1920, 192),
-    (2112, 128),
+    (1920, 128),
+    (2048, 64),
+    (2112, 64),
+    (2176, 64),
     (2240, 64),
 )
 GRANULES = (
-    (0, 0, 512, (0, 1)),
-    (1, 0, 512, (0, 1)),
-    (1, 512, 512, (2, 3)),
-    (0, 512, 512, (2, 3)),
-    (0, 1024, 512, (4, 5)),
-    (1, 1024, 512, (4, 5)),
-    (1, 1536, 192, (6,)),
-    (0, 1536, 192, (6,)),
-    (1, 1728, 192, (7,)),
-    (1, 1920, 192, (8,)),
-    (1, 2112, 192, (9, 10)),
-    (0, 1728, 192, (7,)),
-    (0, 1920, 192, (8,)),
-    (0, 2112, 192, (9, 10)),
+    (0, 0, 512, (0, 1, 2, 3)),
+    (1, 0, 512, (0, 1, 2, 3)),
+    (0, 512, 512, (4, 5, 6, 7)),
+    (1, 512, 512, (4, 5, 6, 7)),
+    (0, 1024, 512, (8, 9, 10, 11)),
+    (1, 1024, 512, (8, 9, 10, 11)),
+    (1, 1536, 192, (12,)),
+    (0, 1536, 192, (12,)),
+    (1, 1728, 192, (13,)),
+    (1, 1920, 192, (14, 15)),
+    (1, 2112, 192, (16, 17, 18)),
+    (0, 1728, 192, (13,)),
+    (0, 1920, 192, (14, 15)),
+    (0, 2112, 192, (16, 17, 18)),
 )
-EARLY = (0, 2)
-PIECES, AHEAD = 10, 2
-FAR_PAIRS = (0, 1, 1, 0, 0, 1)
+EARLY = (0, 1, 4, 5)
+PIECES, AHEAD = 10, 3
+FAR_PAIRS = (0, 1, 0, 1, 0, 1)
 PAIR_TILES = (0, 0, 1, 1, 2, 2)
 BETWEEN, FIRST_HEADS, LAST_NORM = 12, 15, 33
 (
     BIAS_DONE, MATE_DONE, PASS_X, PASS_Y, PASS_DONE, CORE_ADD, CORE_SEND, EARLY_X, EARLY_Y, EARLY_Z,
-    ADD_X, ADD_Y, ADD_Z, ADD_FAR, GIVE_Y, FINISH, SUMS, SETTLE,
-) = range(18)
+    ADD_X, ADD_Y, ADD_Z, ADD_FAR, GIVE_Y, FINISH, SUMS,
+) = range(17)
 PLAN_FORWARD = (
     ((MATE_DONE, 0), (BIAS_DONE, 0),),
     ((PASS_X, 0),),
-    ((PASS_X, 1),),
-    ((MATE_DONE, 1),),
     (),
+    ((PASS_X, 1), (MATE_DONE, 1),),
     ((PASS_X, 2),),
-    ((MATE_DONE, 2),),
-    ((PASS_X, 3), (PASS_Y, 0),),
     (),
+    ((PASS_X, 3), (MATE_DONE, 2),),
+    ((PASS_Y, 0),),
+    ((PASS_X, 4),),
     ((PASS_DONE, 0), (BIAS_DONE, 1), (BIAS_DONE, 2),),
-    ((PASS_X, 4), (PASS_Y, 1),),
-    ((PASS_X, 5),),
-    ((PASS_DONE, 1),),
+    ((PASS_X, 5), (PASS_Y, 1),),
+    (),
+    ((PASS_X, 6), (PASS_DONE, 1),),
     ((PASS_Y, 2),),
-    ((PASS_X, 6),),
+    ((PASS_X, 7),),
     ((PASS_DONE, 2),),
-    ((PASS_X, 7), (PASS_Y, 3),),
+    ((PASS_X, 8), (PASS_Y, 3),),
     (),
 )
 PLAN_SECOND = (
-    ((PASS_X, 8), (MATE_DONE, 3), (PASS_DONE, 3),),
+    ((PASS_X, 9), (MATE_DONE, 3), (PASS_DONE, 3),),
     (),
-    ((PASS_X, 9), (PASS_Y, 4),),
     (),
+    ((PASS_Y, 4),),
 )
 PLAN_MAIN = (
     ((MATE_DONE, 4), (MATE_DONE, 5),),
     ((PASS_Y, 5), (CORE_SEND, 0),),
-    ((PASS_Y, 6), (PASS_DONE, 4), (PASS_DONE, 5),),
-    ((CORE_ADD, 0), (CORE_SEND, 1),),
-    ((PASS_Y, 7), (CORE_ADD, 1), (PASS_DONE, 6), (PASS_DONE, 7),),
-    ((PASS_Y, 8), (CORE_SEND, 2),),
-    ((PASS_Y, 9), (MATE_DONE, 6), (MATE_DONE, 7),),
-    ((CORE_ADD, 2), (CORE_SEND, 3), (EARLY_Y, 0), (ADD_X, 1),),
-    ((CORE_ADD, 3), (EARLY_X, 0), (MATE_DONE, 8), (MATE_DONE, 9),),
-    ((CORE_SEND, 4), (EARLY_X, 2), (ADD_Y, 1),),
-    ((CORE_ADD, 4), (EARLY_Y, 2), (ADD_X, 3), (PASS_DONE, 8), (PASS_DONE, 9),),
-    ((CORE_SEND, 5), (ADD_Z, 1),),
-    ((CORE_ADD, 5), (EARLY_Z, 0), (ADD_Y, 3),),
-    ((EARLY_Z, 2), (ADD_FAR, 1),),
-    ((CORE_SEND, 6), (ADD_Z, 0), (ADD_Z, 3),),
-    ((CORE_ADD, 6), (CORE_SEND, 7), (ADD_Z, 2), (GIVE_Y, 1),),
-    ((CORE_ADD, 7), (ADD_X, 4),),
-    ((ADD_FAR, 0),),
-    ((CORE_SEND, 8),),
-    ((CORE_ADD, 8), (FINISH, 1),),
-    ((ADD_FAR, 3),),
-    ((CORE_SEND, 9), (ADD_X, 5), (ADD_Y, 4),),
-    ((CORE_ADD, 9), (ADD_FAR, 2), (GIVE_Y, 0), (GIVE_Y, 3),),
-    ((ADD_Z, 4),),
-    ((CORE_SEND, 10), (ADD_X, 6), (ADD_Y, 5),),
-    ((CORE_ADD, 10), (GIVE_Y, 2),),
-    ((FINISH, 0),),
-    ((CORE_SEND, 11), (ADD_FAR, 4),),
-    ((CORE_ADD, 11), (ADD_X, 7), (ADD_Z, 5), (FINISH, 3),),
-    ((ADD_Y, 6),),
-    ((CORE_SEND, 12), (FINISH, 2),),
-    ((CORE_ADD, 12), (ADD_X, 8), (ADD_Y, 7), (GIVE_Y, 4),),
-    ((ADD_FAR, 5),),
-    ((CORE_SEND, 13), (ADD_Z, 6),),
-    ((CORE_ADD, 13), (ADD_X, 9), (ADD_X, 10), (ADD_Y, 8), (ADD_Z, 7),),
-    ((GIVE_Y, 5),),
-    ((ADD_FAR, 6), (FINISH, 4),),
+    ((PASS_DONE, 4), (PASS_DONE, 5),),
+    ((PASS_Y, 6), (CORE_ADD, 0), (CORE_SEND, 1),),
+    ((PASS_Y, 7), (MATE_DONE, 6), (MATE_DONE, 7),),
+    ((PASS_Y, 8), (CORE_ADD, 1), (CORE_SEND, 2),),
+    ((PASS_DONE, 6), (PASS_DONE, 7),),
+    ((EARLY_Y, 0), (PASS_Y, 9), (CORE_ADD, 2), (CORE_SEND, 3), (ADD_X, 2),),
+    ((EARLY_Y, 1), (EARLY_X, 0), (MATE_DONE, 8), (MATE_DONE, 9),),
+    ((ADD_Y, 2), (CORE_ADD, 3), (EARLY_Y, 4), (CORE_SEND, 4), (ADD_X, 3), (EARLY_X, 1),),
+    ((EARLY_Z, 0), (EARLY_Y, 5), (ADD_Z, 2), (CORE_ADD, 4), (PASS_DONE, 8), (PASS_DONE, 9),),
+    ((ADD_Y, 3), (ADD_Z, 0), (CORE_SEND, 5), (ADD_X, 6), (EARLY_X, 4), (EARLY_X, 5),),
+    ((ADD_FAR, 2), (ADD_Z, 3), (CORE_ADD, 5), (ADD_X, 7),),
+    ((ADD_Y, 6), (ADD_FAR, 0), (EARLY_Z, 1), (GIVE_Y, 2), (EARLY_Z, 4),),
+    ((ADD_Y, 7), (ADD_FAR, 3), (EARLY_Z, 5), (CORE_SEND, 6),),
+    ((ADD_Z, 1), (ADD_Z, 6), (CORE_ADD, 6), (CORE_SEND, 7), (GIVE_Y, 0),),
+    ((FINISH, 2), (ADD_Z, 7), (ADD_Z, 4), (CORE_ADD, 7), (ADD_X, 8), (GIVE_Y, 3),),
+    ((ADD_FAR, 1), (ADD_Z, 5),),
+    ((CORE_SEND, 8), (ADD_X, 9), (FINISH, 0),),
+    ((ADD_Y, 8), (ADD_FAR, 6), (CORE_ADD, 8),),
+    ((FINISH, 3), (ADD_FAR, 7), (ADD_X, 10), (ADD_FAR, 4), (GIVE_Y, 1),),
+    ((ADD_Z, 8), (CORE_SEND, 9), (ADD_Y, 9), (GIVE_Y, 6),),
+    ((ADD_FAR, 5), (CORE_ADD, 9), (ADD_X, 11), (ADD_Y, 10), (GIVE_Y, 7),),
+    ((FINISH, 1), (ADD_FAR, 8), (GIVE_Y, 4),),
+    ((FINISH, 6), (ADD_Z, 9), (CORE_SEND, 10),),
+    ((ADD_Z, 10), (CORE_ADD, 10), (ADD_X, 12), (GIVE_Y, 5), (GIVE_Y, 8), (ADD_Y, 11),),
+    ((FINISH, 4), (FINISH, 7), (ADD_FAR, 9),),
+    ((CORE_SEND, 11),),
+    ((ADD_Y, 12), (ADD_FAR, 10), (FINISH, 5), (CORE_ADD, 11), (ADD_X, 13),),
+    ((FINISH, 8), (ADD_Z, 11), (GIVE_Y, 9),),
+    ((CORE_SEND, 12), (ADD_Z, 12),),
+    ((ADD_Y, 13), (CORE_ADD, 12), (ADD_X, 14), (ADD_X, 15), (GIVE_Y, 10),),
+    ((FINISH, 9), (ADD_FAR, 11),),
+    ((CORE_SEND, 13), (ADD_Z, 13),),
+    ((ADD_Y, 14), (ADD_FAR, 12), (ADD_Y, 15), (CORE_ADD, 13), (ADD_X, 16), (ADD_X, 17), (ADD_X, 18), (GIVE_Y, 11),),
+    ((FINISH, 10),),
+    ((ADD_Y, 16), (ADD_Z, 14), (ADD_FAR, 13), (GIVE_Y, 12), (ADD_Y, 17),),
 )
 PLAN_DRAIN = (
-    (ADD_Z, 8),
+    (ADD_Y, 18),
+    (ADD_Z, 15),
     (SUMS, 0),
-    (ADD_Y, 9),
-    (SETTLE, 0),
-    (SETTLE, 1),
-    (SETTLE, 2),
-    (SETTLE, 3),
-    (ADD_FAR, 7),
-    (ADD_Y, 10),
-    (SETTLE, 4),
-    (SETTLE, 5),
-    (SETTLE, 6),
-    (SETTLE, 7),
-    (GIVE_Y, 6),
+    (ADD_Z, 16),
+    (FINISH, 11),
     (SUMS, 1),
-    (SETTLE, 8),
-    (SETTLE, 9),
-    (SETTLE, 10),
-    (SETTLE, 12),
-    (SETTLE, 13),
-    (SETTLE, 14),
-    (SETTLE, 15),
-    (SETTLE, 16),
-    (SETTLE, 17),
-    (SETTLE, 18),
-    (ADD_Z, 9),
+    (ADD_FAR, 14),
+    (GIVE_Y, 13),
+    (ADD_Z, 17),
+    (ADD_Z, 18),
+    (ADD_FAR, 15),
+    (FINISH, 12),
+    (ADD_FAR, 16),
     (SUMS, 2),
-    (ADD_FAR, 8),
-    (FINISH, 5),
-    (GIVE_Y, 7),
-    (SETTLE, 19),
-    (ADD_Z, 10),
+    (GIVE_Y, 14),
+    (ADD_FAR, 17),
+    (GIVE_Y, 15),
     (SUMS, 3),
-    (FINISH, 6),
-    (ADD_FAR, 9),
-    (GIVE_Y, 8),
-    (SETTLE, 20),
+    (GIVE_Y, 16),
+    (FINISH, 13),
+    (ADD_FAR, 18),
+    (GIVE_Y, 17),
     (SUMS, 4),
-    (ADD_FAR, 10),
-    (FINISH, 7),
-    (GIVE_Y, 9),
+    (FINISH, 14),
+    (GIVE_Y, 18),
+    (FINISH, 15),
+    (FINISH, 16),
     (SUMS, 5),
-    (GIVE_Y, 10),
-    (SETTLE, 21),
-    (SETTLE, 11),
-    (SETTLE, 22),
-    (FINISH, 8),
-    (FINISH, 9),
-    (FINISH, 10),
+    (FINISH, 17),
+    (FINISH, 18),
 )
 
 def dot(left, right, left_dim, right_dim):
@@ -196,8 +191,8 @@
     x_ref, g_ref, a1_ref, proj_ref, o_ref, x1_ref, hat2_ref, a2_ref, da2_ref,
     hid_ref, low_ref, lse_ref, aug_q, aug_k, sums, sums_recv,
     seg_ref, gain1_ref, shift1_ref, outb_ref, gain2_ref, shift2_ref, downb_ref, upb_ref, qvb_ref, small_sem,
-    local_sem, wm_s, wm_r, wx_s, wx_r, wy_s, wy_r, wz_s, wz_r, wd_s, wd_r, wf_s, wf_r, wb_s, wb_r,
-    core_s, core_r, early_s, early_r, ex_s, ex_r, ey_s, ey_r, ez_s, ez_r, ew_s, ew_r, fz_s, fz_r, fy_s, fy_r, sums_s, sums_r,
+    local_sem, sent, wm_r, wx_r, wy_r, wz_r, wd_r, wf_r, wb_r,
+    core_r, early_r, ex_r, ey_r, ez_r, ew_r, fz_r, fy_r, sums_r,
     *, rows, seq,
 ):
     tokens, width = x_ref.shape
@@ -300,22 +295,22 @@
 
     def to_mate(number, kind, index):
         own = piece(kind, index, x, c)
-        return remote(own, own, wm_s.at[number], wm_r.at[number], mate)
+        return remote(own, own, sent.at[TO_MATE], wm_r.at[number], mate)
 
     def to_x(number, kind, index):
         own = piece(kind, index, x, c, quarter)
-        return remote(own, own, wx_s.at[number], wx_r.at[number], x_peer)
+        return remote(own, own, sent.at[TO_X], wx_r.at[number], x_peer)
 
     def to_square(number, kind, index):
         held = piece(kind, index, nx, c, quarter)
         return [
-            remote(held, held, send.at[number], recv.at[number], peer)
-            for send, recv, peer in ((wy_s, wy_r, y_peer), (wz_s, wz_r, z_pair), (wd_s, wd_r, corner))
+            remote(held, held, sent.at[send], recv.at[number], peer)
+            for send, recv, peer in ((TO_Y, wy_r, y_peer), (TO_Z, wz_r, z_pair), (TO_CORNER, wd_r, corner))
         ]
 
     def forward(number, kind, index):
         held = piece(kind, index, nx, c)
-        return remote(held, held, wf_s.at[number], wf_r.at[number], mate)
+        return remote(held, held, sent.at[FORWARD], wf_r.at[number], mate)
 
     def mate_done(number):
         kinds(number, lambda kind, index: to_mate(number, kind, index).wait_recv())
@@ -348,7 +343,7 @@
         kinds(number, lambda kind, index: forward(number, kind, index).wait_recv())
 
     biases = [
-        remote(wb.at[x, c], wb.at[x, c], wb_s.at[i], wb_r.at[i], peer)
+        remote(wb.at[x, c], wb.at[x, c], sent.at[BIAS], wb_r.at[i], peer)
         for i, peer in enumerate((mate, x_peer, cross))
     ]
     for copy in biases:
@@ -604,7 +599,7 @@
         return remote(
             grad.at[nx if far else x, nc, pl.ds(start, count)],
             mate_buf.at[granule % 2, pl.ds(0, count)],
-            core_s.at[granule], core_r.at[granule], mate,
+            sent.at[CORE], core_r.at[granule], mate,
         )
 
     def core_send(granule):
@@ -628,7 +623,7 @@
 
     def x_copy(unit):
         where = half_rows(unit, outer(unit)[0]) if unit in EARLY else pl.ds(*UNITS[unit])
-        return remote(grad.at[nx, c, where], x_buf.at[where], ex_s.at[unit], ex_r.at[unit], x_peer)
+        return remote(grad.at[nx, c, where], x_buf.at[where], sent.at[X_OUT], ex_r.at[unit], x_peer)
 
     def half_rows(unit, part):
         start, count = UNITS[unit]
@@ -647,53 +642,55 @@
     def outer_copy(unit):
         part, peer = outer(unit)
         return remote(
-            grad.at[x, c, half_rows(unit, 1 - part)], y_buf.at[half_slot(unit)], ey_s.at[unit], ey_r.at[unit], peer
+            grad.at[x, c, half_rows(unit, 1 - part)], y_buf.at[half_slot(unit)], sent.at[OUTER], ey_r.at[unit], peer
         )
+
+    def early_slot(unit):
+        count = UNITS[unit][1] // 2
+        return pl.ds(EARLY.index(unit) * count, count)
 
     def early_copy(unit):
         index = EARLY.index(unit)
-        where = pl.ds(index * UNIT // 2, UNIT // 2)
         part, peer = outer(unit)
         return remote(
-            grad.at[nx, c, half_rows(unit, 1 - part)], early_buf.at[where], early_s.at[index], early_r.at[index], peer
+            grad.at[nx, c, half_rows(unit, 1 - part)], early_buf.at[early_slot(unit)], sent.at[EARLY_OUT], early_r.at[index], peer
         )
 
     def inner_copy(unit):
         part, peer = inner(unit)
         return remote(
-            grad.at[x, c, share_rows(unit, 1 - part)], z_buf.at[0, share_slot(unit)], ez_s.at[unit], ez_r.at[unit], peer
+            grad.at[x, c, share_rows(unit, 1 - part)], z_buf.at[0, share_slot(unit)], sent.at[INNER], ez_r.at[unit], peer
         )
 
     def across_copy(unit):
         return remote(
             grad.at[x, c, share_rows(unit, inner(unit)[0])], z_buf.at[1, share_slot(unit)],
-            ew_s.at[unit], ew_r.at[unit], z_far,
+            sent.at[ACROSS], ew_r.at[unit], z_far,
         )
 
     def back_inner_copy(unit):
         part, peer = inner(unit)
         where = share_rows(unit, part)
-        return remote(x_buf.at[where], x_buf.at[where], fz_s.at[unit], fz_r.at[unit], peer)
+        return remote(x_buf.at[where], x_buf.at[where], sent.at[BACK_INNER], fz_r.at[unit], peer)
 
     def back_outer_copy(unit):
         part, peer = outer(unit)
         where = half_rows(unit, part)
-        return remote(x_buf.at[where], x_buf.at[where], fy_s.at[unit], fy_r.at[unit], peer)
+        return remote(x_buf.at[where], x_buf.at[where], sent.at[BACK_OUTER], fy_r.at[unit], peer)
 
     def early_x(unit):
         early_copy(unit).wait_recv()
-        start = EARLY.index(unit) * UNIT // 2
-        add_into(nx, half_rows(unit, outer(unit)[0]).start, UNIT // 2, early_buf, start)
+        add_into(nx, half_rows(unit, outer(unit)[0]).start, UNITS[unit][1] // 2, early_buf, early_slot(unit).start)
         x_copy(unit).start()
 
     def early_y(unit):
         outer_copy(unit).wait_recv()
-        add_into(x, half_rows(unit, outer(unit)[0]).start, UNIT // 2, y_buf, half_slot(unit).start)
+        add_into(x, half_rows(unit, outer(unit)[0]).start, UNITS[unit][1] // 2, y_buf, half_slot(unit).start)
 
     def early_z(unit):
         x_copy(unit).wait_recv()
         start = half_rows(unit, outer(unit)[0]).start
-        add_into(x, start, UNIT // 2, x_buf, start)
+        add_into(x, start, UNITS[unit][1] // 2, x_buf, start)
         inner_copy(unit).start()
 
     def add_x(unit):
@@ -725,14 +722,14 @@
 
     def out_copy(unit):
         where = pl.ds(*UNITS[unit])
-        return pltpu.make_async_copy(x_buf.at[where], grads_out.at[where], local_sem.at[10 + unit])
+        return pltpu.make_async_copy(x_buf.at[where], grads_out.at[where], local_sem.at[10])
 
     def finish(unit):
         back_outer_copy(unit).wait_recv()
         out_copy(unit).start()
 
     def sums_copy(slot, source, peer):
-        return remote(sums_recv.at[6 + source], sums_recv.at[slot], sums_s.at[slot], sums_r.at[slot], peer)
+        return remote(sums_recv.at[6 + source], sums_recv.at[slot], sent.at[SUMS_OUT], sums_r.at[slot], peer)
 
     small_peers = [(i, i, peer) for i, peer in enumerate((mate, x_peer, y_peer, z_pair, z_far))]
 
@@ -759,34 +756,6 @@
             sums[...] = jnp.where(tile_row == OWN_QV + 1, own_qv[VALUEB : VALUEB + 1], total)
             sums_out_copy.start()
 
-    def piece_sends(number, kind, index):
-        to_mate(number, kind, index).wait_send()
-        to_x(number, kind, index).wait_send()
-        for copy in to_square(number, kind, index):
-            copy.wait_send()
-        forward(number, kind, index).wait_send()
-
-    def settle(number):
-        if number < PIECES:
-            kinds(number, functools.partial(piece_sends, number))
-        elif number == PIECES:
-            for granule in range(len(GRANULES)):
-                core_copy(granule).wait_send()
-        elif number == PIECES + 1:
-            mixed_copy.wait()
-            input_copy.wait()
-            sums_out_copy.wait()
-            for copy in biases:
-                copy.wait_send()
-            for slot, source, peer in small_peers:
-                sums_copy(slot, source, peer).wait_send()
-        else:
-            unit = number - PIECES - 2
-            for copy in (x_copy, outer_copy, inner_copy, across_copy, back_inner_copy):
-                copy(unit).wait_send()
-            if unit in EARLY:
-                early_copy(unit).wait_send()
-
     events = {
         BIAS_DONE: bias_done,
         MATE_DONE: mate_done,
@@ -805,7 +774,6 @@
         GIVE_Y: give_y,
         FINISH: finish,
         SUMS: sums_step,
-        SETTLE: settle,
     }
 
     def run_due(due):
@@ -852,10 +820,26 @@
     lax.fori_loop(0, LAST_NORM + tokens // 256, main_step, 0)
     run_due(PLAN_DRAIN)
 
-
-    for unit in range(len(UNITS)):
-        back_outer_copy(unit).wait_send()
-        out_copy(unit).wait()
+    shard_rows = grad.shape[2]
+    own = grad.at[0, 0]
+    rows_sent = {
+        TO_MATE: shard_rows, TO_X: shard_rows // 4, TO_Y: shard_rows // 4, TO_Z: shard_rows // 4,
+        TO_CORNER: shard_rows // 4, FORWARD: shard_rows, BIAS: 3 * 16,
+        EARLY_OUT: sum(UNITS[unit][1] for unit in EARLY) // 2,
+        X_OUT: sum(count // 2 if unit in EARLY else count for unit, (_, count) in enumerate(UNITS)),
+        OUTER: shard_rows // 2, INNER: shard_rows // 4, ACROSS: shard_rows // 4, BACK_INNER: shard_rows // 4,
+        BACK_OUTER: shard_rows // 2,
+    }
+    for kind, count in rows_sent.items():
+        all_rows = own.at[pl.ds(0, count)]
+        remote(all_rows, all_rows, sent.at[kind], wb_r.at[0], mate).wait_send()
+    remote(grad.at[0], grad.at[0], sent.at[CORE], wb_r.at[0], mate).wait_send()
+    all_sums = sums_recv.at[pl.ds(0, 5)]
+    remote(all_sums, all_sums, sent.at[SUMS_OUT], wb_r.at[0], mate).wait_send()
+    mixed_copy.wait()
+    input_copy.wait()
+    sums_out_copy.wait()
+    pltpu.make_async_copy(x_buf, grads_out, local_sem.at[10]).wait()
 
 
 def tail_kernel(
@@ -953,7 +937,7 @@
             vm((2, 2, 16, width), BF16),
             vm((2, 2, units * UNIT, width), BF16),
             vm((2, 2 * UNIT, width), BF16),
-            vm((len(EARLY) * UNIT // 2, width), BF16),
+            vm((sum(UNITS[unit][1] for unit in EARLY) // 2, width), BF16),
             vm((units * UNIT, width), BF16),
             vm((units * UNIT // 2, width), BF16),
             vm((2, units * UNIT // 4, width), BF16),
@@ -977,11 +961,9 @@
             *[vm((width,), BF16)] * 7,
             vm((2, heads * HEAD), BF16),
             dma((10,)),
-            dma((10 + len(UNITS),)),
-            *[dma((PIECES,))] * 12, dma((3,)), dma((3,)),
-            dma((len(GRANULES),)), dma((len(GRANULES),)), dma((len(EARLY),)), dma((len(EARLY),)),
-            *[dma((len(UNITS),))] * 12,
-            dma((6,)), dma((6,)),
+            dma((11,)), dma((KINDS,)),
+            *[dma((PIECES,))] * 6, dma((3,)),
+            dma((len(GRANULES),)), dma((len(EARLY),)), *[dma((len(UNITS),))] * 6, dma((5,)),
         ],
         compiler_params=pltpu.CompilerParams(
             collective_id=0, has_side_effects=True, vmem_limit_bytes=64 * 2**20 - 2**16

time: 157 us -> 152 us (0.968)
  Pallas kernels: 156 us -> 151 us
    pallas_call x1, Pallas kernels: 150 us -> 145 us  [on_device(): pl.pallas_call(functools.partial(kernel, rows=rows, seq=seq), out_shape=(...]
where the time goes in v5:
time: 152 us
  Pallas kernels  151 us (99%)
    pallas_call x1, Pallas kernels, on_device(): pl.pallas_call(functools.partial(kernel, rows=rows, seq=seq), out_shape=(...  145 us
    pallas_call x1, Pallas kernels, on_device(): pl.pallas_call(tail_kernel, out_shape=(mixed, input_grad, jax.ShapeDtypeS...  5.98 us

profile of v5, /device:TPU:0, one launch (start us, length us, event | category | flops | bytes accessed | tf_op | source)
XLA Modules:
  0.0 151.8 jit_solution(11551762248641466993)
XLA Ops:
  0.7 145.0 %shard_map.254 = (bf16[1024,768]{1,0:T(8,128)(2,1)}, bf16[1024,768]{1,0:T(8,128)(2,1)}, bf16[2304,768]{1,0:T(8,128)(2,1)}, f32[16,768]{1,0:T(8,128)}) custom-call(bf16[1024,768]{1,0:T(8,128)(2,1)} %bitcast.13, bf16[1024,768]{1,0:T(8,128)(2,1)} %bitcast.14, s32[2,512]{1,0:T(2,128)} %seg_in.1, bf16[768]{0:T(1024)(128)(2,1)} %gain1_in.1, ...), custom_call_target="tpu_custom_call" | custom-call | tf_op jit(solution)/shard_map/pallas_call | solution.py:923
  145.7 6.0 %shard_map.255 = (bf16[1024,768]{1,0:T(8,128)(2,1)}, bf16[1024,768]{1,0:T(8,128)(2,1)}, f32[3,3,64,768]{3,2,1,0:T(8,128)}, f32[192,768]{1,0:T(8,128)}, f32[768,7...) custom-call(bf16[1024,768]{1,0:T(8,128)(2,1)} %get-tuple-element.32., ...), custom_call_target="tpu_custom_call" | custom-call | tf_op jit(solution)/shard_map/pallas_call | solution.py:981

commit v6 on v5

--- a/solution.py
+++ b/solution.py
@@ -38,7 +38,8 @@
     (1280, 128),
     (1408, 128),
     (1536, 192),
-    (1728, 192),
+    (1728, 128),
+    (1856, 64),
     (1920, 128),
     (2048, 64),
     (2112, 64),
@@ -54,18 +55,18 @@
     (1, 1024, 512, (8, 9, 10, 11)),
     (1, 1536, 192, (12,)),
     (0, 1536, 192, (12,)),
-    (1, 1728, 192, (13,)),
-    (1, 1920, 192, (14, 15)),
-    (1, 2112, 192, (16, 17, 18)),
-    (0, 1728, 192, (13,)),
-    (0, 1920, 192, (14, 15)),
-    (0, 2112, 192, (16, 17, 18)),
+    (1, 1728, 192, (13, 14)),
+    (1, 1920, 192, (15, 16)),
+    (1, 2112, 192, (17, 18, 19)),
+    (0, 1728, 192, (13, 14)),
+    (0, 1920, 192, (15, 16)),
+    (0, 2112, 192, (17, 18, 19)),
 )
-EARLY = (0, 1, 4, 5)
+EARLY = (3, 5, 6, 7)
 PIECES, AHEAD = 10, 3
 FAR_PAIRS = (0, 1, 0, 1, 0, 1)
 PAIR_TILES = (0, 0, 1, 1, 2, 2)
-BETWEEN, FIRST_HEADS, LAST_NORM = 12, 15, 33
+BETWEEN, FIRST_HEADS, LAST_NORM, MIX = 12, 15, 33, 37
 (
     BIAS_DONE, MATE_DONE, PASS_X, PASS_Y, PASS_DONE, CORE_ADD, CORE_SEND, EARLY_X, EARLY_Y, EARLY_Z,
     ADD_X, ADD_Y, ADD_Z, ADD_FAR, GIVE_Y, FINISH, SUMS,
@@ -87,14 +88,14 @@
     ((PASS_Y, 2),),
     ((PASS_X, 7),),
     ((PASS_DONE, 2),),
-    ((PASS_X, 8), (PASS_Y, 3),),
-    (),
+    ((PASS_X, 8),),
+    ((PASS_Y, 3),),
 )
 PLAN_SECOND = (
     ((PASS_X, 9), (MATE_DONE, 3), (PASS_DONE, 3),),
     (),
+    ((PASS_Y, 4),),
     (),
-    ((PASS_Y, 4),),
 )
 PLAN_MAIN = (
     ((MATE_DONE, 4), (MATE_DONE, 5),),
@@ -102,70 +103,60 @@
     ((PASS_DONE, 4), (PASS_DONE, 5),),
     ((PASS_Y, 6), (CORE_ADD, 0), (CORE_SEND, 1),),
     ((PASS_Y, 7), (MATE_DONE, 6), (MATE_DONE, 7),),
-    ((PASS_Y, 8), (CORE_ADD, 1), (CORE_SEND, 2),),
-    ((PASS_DONE, 6), (PASS_DONE, 7),),
-    ((EARLY_Y, 0), (PASS_Y, 9), (CORE_ADD, 2), (CORE_SEND, 3), (ADD_X, 2),),
-    ((EARLY_Y, 1), (EARLY_X, 0), (MATE_DONE, 8), (MATE_DONE, 9),),
-    ((ADD_Y, 2), (CORE_ADD, 3), (EARLY_Y, 4), (CORE_SEND, 4), (ADD_X, 3), (EARLY_X, 1),),
-    ((EARLY_Z, 0), (EARLY_Y, 5), (ADD_Z, 2), (CORE_ADD, 4), (PASS_DONE, 8), (PASS_DONE, 9),),
-    ((ADD_Y, 3), (ADD_Z, 0), (CORE_SEND, 5), (ADD_X, 6), (EARLY_X, 4), (EARLY_X, 5),),
-    ((ADD_FAR, 2), (ADD_Z, 3), (CORE_ADD, 5), (ADD_X, 7),),
-    ((ADD_Y, 6), (ADD_FAR, 0), (EARLY_Z, 1), (GIVE_Y, 2), (EARLY_Z, 4),),
-    ((ADD_Y, 7), (ADD_FAR, 3), (EARLY_Z, 5), (CORE_SEND, 6),),
-    ((ADD_Z, 1), (ADD_Z, 6), (CORE_ADD, 6), (CORE_SEND, 7), (GIVE_Y, 0),),
-    ((FINISH, 2), (ADD_Z, 7), (ADD_Z, 4), (CORE_ADD, 7), (ADD_X, 8), (GIVE_Y, 3),),
-    ((ADD_FAR, 1), (ADD_Z, 5),),
-    ((CORE_SEND, 8), (ADD_X, 9), (FINISH, 0),),
-    ((ADD_Y, 8), (ADD_FAR, 6), (CORE_ADD, 8),),
-    ((FINISH, 3), (ADD_FAR, 7), (ADD_X, 10), (ADD_FAR, 4), (GIVE_Y, 1),),
-    ((ADD_Z, 8), (CORE_SEND, 9), (ADD_Y, 9), (GIVE_Y, 6),),
-    ((ADD_FAR, 5), (CORE_ADD, 9), (ADD_X, 11), (ADD_Y, 10), (GIVE_Y, 7),),
-    ((FINISH, 1), (ADD_FAR, 8), (GIVE_Y, 4),),
-    ((FINISH, 6), (ADD_Z, 9), (CORE_SEND, 10),),
-    ((ADD_Z, 10), (CORE_ADD, 10), (ADD_X, 12), (GIVE_Y, 5), (GIVE_Y, 8), (ADD_Y, 11),),
-    ((FINISH, 4), (FINISH, 7), (ADD_FAR, 9),),
-    ((CORE_SEND, 11),),
-    ((ADD_Y, 12), (ADD_FAR, 10), (FINISH, 5), (CORE_ADD, 11), (ADD_X, 13),),
-    ((FINISH, 8), (ADD_Z, 11), (GIVE_Y, 9),),
-    ((CORE_SEND, 12), (ADD_Z, 12),),
-    ((ADD_Y, 13), (CORE_ADD, 12), (ADD_X, 14), (ADD_X, 15), (GIVE_Y, 10),),
-    ((FINISH, 9), (ADD_FAR, 11),),
+    ((CORE_ADD, 1), (CORE_SEND, 2),),
+    ((PASS_Y, 8), (PASS_DONE, 6), (PASS_DONE, 7),),
+    ((PASS_Y, 9), (CORE_ADD, 2), (CORE_SEND, 3), (EARLY_Y, 3), (ADD_X, 0),),
+    ((EARLY_X, 3), (MATE_DONE, 8), (MATE_DONE, 9),),
+    ((ADD_X, 1), (CORE_ADD, 3), (CORE_SEND, 4), (ADD_Y, 0), (EARLY_Y, 5), (EARLY_Y, 6),),
+    ((ADD_X, 2), (EARLY_Y, 7), (PASS_DONE, 8), (PASS_DONE, 9),),
+    ((EARLY_Z, 3), (CORE_ADD, 4), (CORE_SEND, 5), (ADD_Y, 1), (EARLY_X, 5), (EARLY_X, 6),),
+    ((ADD_X, 4), (ADD_Y, 2), (EARLY_X, 7), (CORE_ADD, 5), (ADD_Z, 0), (ADD_Z, 3),),
+    ((EARLY_Z, 5), (EARLY_Z, 6), (ADD_Z, 1), (ADD_Z, 2), (ADD_Y, 4),),
+    ((EARLY_Z, 7), (CORE_SEND, 6), (ADD_FAR, 0),),
+    ((CORE_ADD, 6), (CORE_SEND, 7), (ADD_FAR, 3), (ADD_Z, 5), (ADD_Z, 6),),
+    ((ADD_X, 8), (GIVE_Y, 0), (CORE_ADD, 7), (ADD_FAR, 1), (ADD_Z, 4), (ADD_Z, 7),),
+    ((GIVE_Y, 3), (ADD_FAR, 2), (ADD_X, 9),),
+    ((CORE_SEND, 8), (GIVE_Y, 1), (ADD_FAR, 5),),
+    ((CORE_ADD, 8), (ADD_Y, 8), (FINISH, 0), (ADD_FAR, 6),),
+    ((ADD_X, 10), (ADD_Y, 9), (GIVE_Y, 2), (FINISH, 3), (ADD_FAR, 4),),
+    ((CORE_SEND, 9), (ADD_FAR, 7), (ADD_Z, 8),),
+    ((ADD_X, 11), (GIVE_Y, 5), (CORE_ADD, 9), (GIVE_Y, 6), (FINISH, 1), (ADD_Z, 9),),
+    ((GIVE_Y, 4), (ADD_Y, 10),),
+    ((CORE_SEND, 10), (ADD_FAR, 8),),
+    ((ADD_X, 12), (GIVE_Y, 7), (CORE_ADD, 10), (FINISH, 2), (FINISH, 5), (FINISH, 6), (ADD_FAR, 9),),
+    ((ADD_Y, 11), (ADD_Z, 10),),
+    ((CORE_SEND, 11), (GIVE_Y, 8), (FINISH, 4),),
+    ((CORE_ADD, 11), (ADD_X, 13), (ADD_X, 14), (FINISH, 7),),
+    ((GIVE_Y, 9), (ADD_Y, 12), (ADD_FAR, 10), (ADD_Z, 11),),
+    ((CORE_SEND, 12), (FINISH, 8),),
+    ((CORE_ADD, 12), (ADD_X, 15), (ADD_X, 16), (ADD_Y, 13), (ADD_Y, 14), (ADD_Z, 12),),
+    ((GIVE_Y, 10), (FINISH, 9), (ADD_FAR, 11),),
     ((CORE_SEND, 13), (ADD_Z, 13),),
-    ((ADD_Y, 14), (ADD_FAR, 12), (ADD_Y, 15), (CORE_ADD, 13), (ADD_X, 16), (ADD_X, 17), (ADD_X, 18), (GIVE_Y, 11),),
-    ((FINISH, 10),),
-    ((ADD_Y, 16), (ADD_Z, 14), (ADD_FAR, 13), (GIVE_Y, 12), (ADD_Y, 17),),
+    ((ADD_Y, 15), (ADD_Y, 16), (CORE_ADD, 13), (ADD_X, 17), (ADD_X, 18), (ADD_X, 19), (ADD_Z, 14),),
+    ((GIVE_Y, 11), (FINISH, 10), (ADD_FAR, 12),),
+    ((ADD_Y, 17), (ADD_FAR, 13), (ADD_Z, 15), (ADD_Z, 16),),
+    ((SUMS, 0), (GIVE_Y, 12), (ADD_Y, 18), (ADD_Y, 19), (ADD_FAR, 14), (ADD_Z, 17),),
+    ((SUMS, 1), (GIVE_Y, 13), (FINISH, 11), (ADD_FAR, 15),),
+    ((GIVE_Y, 14), (ADD_FAR, 16), (ADD_Z, 18), (ADD_Z, 19), (SUMS, 2), (FINISH, 12), (ADD_FAR, 17),),
+    ((GIVE_Y, 15),),
 )
 PLAN_DRAIN = (
-    (ADD_Y, 18),
-    (ADD_Z, 15),
-    (SUMS, 0),
-    (ADD_Z, 16),
-    (FINISH, 11),
-    (SUMS, 1),
-    (ADD_FAR, 14),
-    (GIVE_Y, 13),
-    (ADD_Z, 17),
-    (ADD_Z, 18),
-    (ADD_FAR, 15),
-    (FINISH, 12),
-    (ADD_FAR, 16),
-    (SUMS, 2),
-    (GIVE_Y, 14),
-    (ADD_FAR, 17),
-    (GIVE_Y, 15),
     (SUMS, 3),
     (GIVE_Y, 16),
     (FINISH, 13),
+    (FINISH, 14),
     (ADD_FAR, 18),
     (GIVE_Y, 17),
+    (ADD_FAR, 19),
     (SUMS, 4),
-    (FINISH, 14),
+    (FINISH, 15),
     (GIVE_Y, 18),
-    (FINISH, 15),
     (FINISH, 16),
+    (GIVE_Y, 19),
+    (FINISH, 17),
     (SUMS, 5),
-    (FINISH, 17),
     (FINISH, 18),
+    (FINISH, 19),
 )
 
 def dot(left, right, left_dim, right_dim):
@@ -186,12 +177,12 @@
 def kernel(
     x_in, g_in, seg_in, gain1_in, shift1_in, outb_in, gain2_in, shift2_in, downb_in, upb_in, qvb_in,
     qkv_in, out_in, up_in, down_in,
-    mixed_out, input_out, grads_out, sums_out,
+    mixed_out, input_out, grads_out, sums_out, hid_out,
     wq, wo, wm, wb, grad, mate_buf, early_buf, x_buf, y_buf, z_buf,
     x_ref, g_ref, a1_ref, proj_ref, o_ref, x1_ref, hat2_ref, a2_ref, da2_ref,
     hid_ref, low_ref, lse_ref, aug_q, aug_k, sums, sums_recv,
     seg_ref, gain1_ref, shift1_ref, outb_ref, gain2_ref, shift2_ref, downb_ref, upb_ref, qvb_ref, small_sem,
-    local_sem, sent, wm_r, wx_r, wy_r, wz_r, wd_r, wf_r, wb_r,
+    local_sem, spill_sem, fetch_sem, sent, wm_r, wx_r, wy_r, wz_r, wd_r, wf_r, wb_r,
     core_r, early_r, ex_r, ey_r, ez_r, ew_r, fz_r, fy_r, sums_r,
     *, rows, seq,
 ):
@@ -443,7 +434,19 @@
         tile = sum(jnp.where(pair == p, index, 0) for p, index in enumerate(PAIR_TILES))
         return jnp.where(far == 1, nx, x), tile
 
+    def spill(step):
+        return pltpu.make_async_copy(hid_ref.at[step % 2], hid_out.at[step], spill_sem.at[step % 2])
+
+    def fetch(tile):
+        if tile < 9:
+            place = proj_ref.at[:, pl.ds(tile * UNIT, UNIT)]
+        else:
+            place = a1_ref.at[:, pl.ds((tile - 9) * UNIT, UNIT)]
+        return pltpu.make_async_copy(hid_out.at[tile], place, fetch_sem.at[tile])
+
     def expert_tile(step):
+        slot = step % 2
+        pl.when(step >= 2)(lambda: spill(step - 2).wait())
         xx, index = pair_place(step // 2)
         cc = jnp.where(step % 2 == 0, nc, c)
         w_up = wm[xx, cc, index, pl.ds(0, UNIT), :]
@@ -459,15 +462,15 @@
             cumul, density = gelu_parts(pre)
             hidden = (pre * cumul).astype(BF16)
             low = (back * (cumul + pre * density)).astype(BF16)
-            hid_ref[where, :] = hidden
+            hid_ref[slot, where, :] = hidden
             low_ref[where, :] = low
             one = column_sum(low.astype(F32))
             upb_sum = one if upb_sum is None else upb_sum + one
         sums[pl.ds(UPB + xx * 2 + cc, 1), lanes] = upb_sum
         base = pl.multiple_of(index * 2 * UNIT, UNIT)
         grad[xx, cc, pl.ds(base, UNIT), :] = dot(low_ref[...], a2_ref[...], 0, 0).astype(BF16)
-        grad[xx, cc, pl.ds(base + UNIT, UNIT), :] = dot(hid_ref[...], g_ref[...], 0, 0).astype(BF16)
-        x1_ref[...] += dot(hid_ref[...], w_down, 1, 0)
+        grad[xx, cc, pl.ds(base + UNIT, UNIT), :] = dot(hid_ref[slot], g_ref[...], 0, 0).astype(BF16)
+        spill(step).start()
         da2_ref[...] += dot(low_ref[...], w_up, 1, 0)
 
     def norm_back(grad_in, hat, inv, gain):
@@ -496,11 +499,11 @@
             low = middle.astype(BF16)
             add_sum(OUTB, low.astype(F32))
             a2_ref[where, :] = low
-            hat2_ref[where, :] = x1_ref[where, :].astype(BF16)
             return carry
 
         lax.fori_loop(0, tokens // chunk, one, 0)
-        mixed_copy.start()
+        for tile in (10, 11):
+            spill(tile).wait()
 
     def between_out():
         for xx in range(2):
@@ -576,6 +579,24 @@
         g_ref[where, :] = (da2_ref[where, :] + norm_back(da1, hat, inv, small(0))).astype(BF16)
         pl.when(step == tokens // 256 - 1)(lambda: input_copy.start())
 
+    def mix(step):
+        @pl.when(step == 0)
+        def _():
+            for tile in range(12):
+                fetch(tile).start()
+            for tile in range(12):
+                fetch(tile).wait()
+
+        where = pl.ds(pl.multiple_of(step * 256, 256), 256)
+        total = x1_ref[where, :]
+        for tile in range(12):
+            hidden = proj_ref[where, pl.ds(tile * UNIT, UNIT)] if tile < 9 else a1_ref[where, pl.ds((tile - 9) * UNIT, UNIT)]
+            xx = nx if FAR_PAIRS[tile // 2] else x
+            cc = c if tile % 2 else nc
+            total += dot(hidden, wm[xx, cc, PAIR_TILES[tile // 2], pl.ds(UNIT, UNIT), :], 1, 0)
+        hat2_ref[where, :] = total.astype(BF16)
+        pl.when(step == tokens // 256 - 1)(lambda: mixed_copy.start())
+
     sums_out_copy = pltpu.make_async_copy(sums, sums_out, small_sem.at[9])
     mixed_copy = pltpu.make_async_copy(hat2_ref, mixed_out, local_sem.at[8])
     input_copy = pltpu.make_async_copy(g_ref, input_out, local_sem.at[9])
@@ -814,10 +835,11 @@
         pl.when(jnp.logical_and(step >= FIRST_HEADS, step < LAST_NORM))(
             lambda: attend_backward(step - FIRST_HEADS)
         )
-        pl.when(step >= LAST_NORM)(lambda: last_norm(step - LAST_NORM))
+        pl.when(jnp.logical_and(step >= LAST_NORM, step < MIX))(lambda: last_norm(step - LAST_NORM))
+        pl.when(step >= MIX)(lambda: mix(step - MIX))
         return carry
 
-    lax.fori_loop(0, LAST_NORM + tokens // 256, main_step, 0)
+    lax.fori_loop(0, MIX + tokens // 256, main_step, 0)
     run_due(PLAN_DRAIN)
 
     shard_rows = grad.shape[2]
@@ -920,16 +942,17 @@
     any_space = pl.BlockSpec(memory_space=pl.ANY)
     dma = pltpu.SemaphoreType.DMA
     vm = pltpu.VMEM
-    mixed, input_grad, grads, sums = pl.pallas_call(
+    mixed, input_grad, grads, sums, _ = pl.pallas_call(
         functools.partial(kernel, rows=rows, seq=seq),
         out_shape=(
             jax.ShapeDtypeStruct((count, width), BF16),
             jax.ShapeDtypeStruct((count, width), BF16),
             jax.ShapeDtypeStruct((units * UNIT, width), BF16),
             jax.ShapeDtypeStruct((16, width), F32),
+            jax.ShapeDtypeStruct((4 * tiles, count, UNIT), BF16),
         ),
         in_specs=[any_space] * 15,
-        out_specs=(any_space,) * 4,
+        out_specs=(any_space,) * 5,
         scratch_shapes=[
             vm((2, heads, 3, 2, HEAD, width), BF16),
             vm((2, heads, 2, HEAD, width), BF16),
@@ -950,7 +973,7 @@
             vm((count, width), BF16),
             vm((count, width), BF16),
             vm((count, width), F32),
-            vm((count, UNIT), BF16),
+            vm((2, count, UNIT), BF16),
             vm((count, UNIT), BF16),
             vm((count, 128), F32),
             vm((count, 128), BF16),
@@ -961,7 +984,7 @@
             *[vm((width,), BF16)] * 7,
             vm((2, heads * HEAD), BF16),
             dma((10,)),
-            dma((11,)), dma((KINDS,)),
+            dma((11,)), dma((2,)), dma((12,)), dma((KINDS,)),
             *[dma((PIECES,))] * 6, dma((3,)),
             dma((len(GRANULES),)), dma((len(EARLY),)), *[dma((len(UNITS),))] * 6, dma((5,)),
         ],

time: 152 us -> 152 us (level)
  no operation moved by 1% of the time
where the time goes in v6:
time: 152 us; the launch traced here: 151 us
  Pallas kernels  151 us (99%)
    pallas_call x1, Pallas kernels, on_device(): pl.pallas_call(functools.partial(kernel, rows=rows, seq=seq), out_shape=(...  145 us
    pallas_call x1, Pallas kernels, on_device(): pl.pallas_call(tail_kernel, out_shape=(mixed, input_grad, jax.ShapeDtypeS...  5.98 us

profile of v6, /device:TPU:0, one launch (start us, length us, event | category | flops | bytes accessed | tf_op | source)
XLA Modules:
  0.0 151.5 jit_solution(11666977114835628824)
XLA Ops:
  0.7 144.7 %shard_map.254 = (bf16[1024,768]{1,0:T(8,128)(2,1)}, bf16[1024,768]{1,0:T(8,128)(2,1)}, bf16[2304,768]{1,0:T(8,128)(2,1)}, f32[16,768]{1,0:T(8,128)}, bf16[12,1024,256]{2,1,0:T(8,128)(2,1)}) custom-call(bf16[1024,768]{1,0:T(8,128)(2,1)} %bitcast.13, bf16[1024,768]{1,0:T(8,128)(2,1)} %bitcast.14, s32[2,512]{1,0:T(2,128)} %seg_in.1, bf16[768]{0:T(1024)(128)(2,1)} %gain1_in.1, ...), custom_call_target="tpu_custom_call" | custom-call | tf_op jit(solution)/shard_map/pallas_call | solution.py:945
  145.3 6.0 %shard_map.255 = (bf16[1024,768]{1,0:T(8,128)(2,1)}, bf16[1024,768]{1,0:T(8,128)(2,1)}, f32[3,3,64,768]{3,2,1,0:T(8,128)}, f32[192,768]{1,0:T(8,128)}, f32[768,7...) custom-call(bf16[1024,768]{1,0:T(8,128)(2,1)} %get-tuple-element.32., ...), custom_call_target="tpu_custom_call" | custom-call | tf_op jit(solution)/shard_map/pallas_call | solution.py:1004
